TPU v7x, 32 devices: a whole 2x2x4 slice. The times are simulated.
32 devices in a mesh: ctx: 16 (over z, y, x), tp: 2 (over core).
Axes of the slice: x: 2, y: 2, z: 4, core: 2. Of those that a mesh axis runs over, the one named last changes fastest.
Arguments:
- stretch_order: int32 [16], replicated, may hold values from 0 to 15, as said below
- attn_queries: bfloat16 [2048, 4096], P('ctx', 'tp'), may hold values from -4.6 to 4.6
- attn_keys: bfloat16 [2048, 1024], P('ctx', 'tp'), may hold values from -4.6 to 4.6
- attn_values: bfloat16 [2048, 1024], P('ctx', 'tp'), may hold values from -6 to 6
- attn_grad: bfloat16 [2048, 4096], P('ctx', 'tp'), may hold values from -6 to 6
- mamba_input: bfloat16 [2048, 4096], P('ctx', 'tp'), may hold values from -21 to 21
- gate_input: bfloat16 [2048, 4096], P('ctx', 'tp'), may hold values from -6 to 6
- state_write: bfloat16 [2048, 1024], P('ctx', 'tp'), may hold values from -6 to 6
- state_read: bfloat16 [2048, 1024], P('ctx', 'tp'), may hold values from -0.5 to 0.5
- step_raw: float32 [2048, 64], P('ctx', 'tp'), may hold values from -8 to 2
- decay_log: float32 [64], P('tp')
- skip_gain: float32 [64], P('tp'), may hold values from 0.5 to 1.5
- norm_gain: float32 [4096], P('tp'), may hold values from 0.25 to 1.75
- mamba_grad: bfloat16 [2048, 4096], P('ctx', 'tp'), may hold values from -6 to 6
Outputs:
- attn_output: bfloat16 [2048, 4096], P('ctx', 'tp')
- query_grad: bfloat16 [2048, 4096], P('ctx', 'tp')
- mamba_output: bfloat16 [2048, 4096], P('ctx', 'tp')
- input_grad: bfloat16 [2048, 4096], P('ctx', 'tp')
- write_grad: bfloat16 [2048, 1024], P('ctx', 'tp')
- read_grad: bfloat16 [2048, 1024], P('ctx', 'tp')
Inputs may be any that keep to these rules, and one draw needn't show every extreme that they name: `stretch_order`: entry i is (i + s) mod 16 for one s of each draw.
All inputs are finite; a program needn't handle non-finite values.
Results may differ from a plain program's by a relative error of at most 0.015.
Values may be sent and summed in bfloat16 or wider, within the bound.
No kernel may reach another device: no remote copies, remote signals or barrier semaphores. Data moves between devices by JAX's collectives and lax.ppermute only.
A program may use at most 128 MiB of HBM per device.

v0:
```python
from functools import partial

import jax
import jax.numpy as jnp
from jax import lax
from jax.sharding import PartitionSpec as P

MAMBA_HEAD_HALF = 64
MDIM = 64
NSTATE = 128
AHD = 128


NEG_FILL = -1e30
NORM_EPS = 1e-05


def as_sent(x):

    def short(part):
        return part.astype(jnp.bfloat16) if part.dtype == jnp.float32 else part

    return jax.tree.map(short, x)


def shifted(value, axis, steps):
    count = lax.axis_size(axis)
    pairs = [(source, (source + steps) % count) for source in range(count)]
    return lax.ppermute(value, axis, pairs)


def stretch_parts(input_rows, write_rows, read_rows, rate_rows, decay_rate, skip_rate):
    length = input_rows.shape[0]
    cumlog = jnp.cumsum(rate_rows * decay_rate[None], axis=0)
    scores = jnp.einsum("tgn,sgn->gts", read_rows, write_rows, preferred_element_type=jnp.float32)
    position = jnp.arange(length)
    causal = position[:, None] >= position[None, :]
    levels = jnp.transpose(cumlog, (1, 2, 0))
    spread = levels[:, :, :, None] - levels[:, :, None, :]
    decays = jnp.where(causal, jnp.exp(jnp.where(causal, spread, 0.0)), 0.0)
    mixing = (decays * scores[:, None] * jnp.transpose(rate_rows, (1, 2, 0))[:, :, None, :]).astype(
        jnp.bfloat16
    )
    local_out = jnp.einsum(
        "gkts,sgkp->tgkp", mixing, input_rows, preferred_element_type=jnp.float32
    )
    input_float = input_rows.astype(jnp.float32)
    local_out = local_out + skip_rate[None, :, :, None] * input_float
    tail_weight = jnp.exp(cumlog[-1][None] - cumlog) * rate_rows
    weighted = (input_float * tail_weight[..., None]).astype(jnp.bfloat16)
    local_state = jnp.einsum(
        "sgkp,sgn->gkpn", weighted, write_rows, preferred_element_type=jnp.float32
    )
    return (local_out, cumlog, jnp.exp(cumlog[-1]), local_state)


def carried_term(read_rows, cumlog, state_in):
    inner = jnp.einsum(
        "tgn,gkpn->tgkp", read_rows.astype(jnp.float32), state_in, precision=lax.Precision.HIGHEST
    )
    return jnp.exp(cumlog)[..., None] * inner


def stretch_full(input_rows, write_rows, read_rows, rate_rows, decay_rate, skip_rate, state_in):
    local_out, cumlog, through, local_state = stretch_parts(
        input_rows, write_rows, read_rows, rate_rows, decay_rate, skip_rate
    )
    output = local_out + carried_term(read_rows, cumlog, state_in)
    return (output, through[..., None, None] * state_in + local_state)


def state_touch(read_rows, cumlog, mixed_rows):
    return jnp.einsum(
        "tgn,tgkp->gkpn",
        read_rows.astype(jnp.float32),
        jnp.exp(cumlog)[..., None] * mixed_rows,
        precision=lax.Precision.HIGHEST,
    )


def compose_pair(early, late):
    return (early[0] * late[0], late[0][..., None, None] * early[1] + late[1])


def choose_pair(flag, first_pair, second_pair):
    return (
        jnp.where(flag, first_pair[0], second_pair[0]),
        jnp.where(flag, first_pair[1], second_pair[1]),
    )


def state_chain(leading, trailing, my_pair, ctx_count):
    rounds = (ctx_count - 1).bit_length()
    identity = (jnp.ones_like(leading[0]), jnp.zeros_like(leading[1]))
    running = leading
    for round_index in range(rounds):
        span_width = 1 << round_index
        received = shifted((as_sent(running[0]), as_sent(running[1])), "ctx", span_width)
        running = choose_pair(my_pair < span_width, running, compose_pair(received, running))
    before = shifted((as_sent(running[0]), as_sent(running[1])), "ctx", 1)
    into_leading = choose_pair(my_pair == 0, identity, before)
    distance = ctx_count - 1 - my_pair
    falling_run = choose_pair(distance == 0, compose_pair(running, trailing), trailing)
    for round_index in range(rounds):
        span_width = 1 << round_index
        received = shifted((as_sent(falling_run[0]), as_sent(falling_run[1])), "ctx", -span_width)
        falling_run = choose_pair(
            distance < span_width, falling_run, compose_pair(received, falling_run)
        )
    after = shifted((as_sent(falling_run[0]), as_sent(falling_run[1])), "ctx", -1)
    into_trailing = choose_pair(distance == 0, running, after)
    return (into_leading[1], into_trailing[1])


def key_positions(first_row, row_count, stretch_order, tok_rows, ctx_count):
    half_rows = tok_rows // 2
    row_index = first_row + jnp.arange(row_count, dtype=jnp.int32)
    owner_index = row_index // tok_rows
    offset = row_index % tok_rows
    matches = owner_index[:, None] == jnp.arange(ctx_count, dtype=jnp.int32)[None, :]
    owner_pair = jnp.sum(jnp.where(matches, stretch_order[None, :], 0), axis=1)
    block_index = jnp.where(offset < half_rows, owner_pair, 2 * ctx_count - 1 - owner_pair)
    return block_index * half_rows + offset % half_rows


def forward_update(carried, queries_half, query_pos, key_piece, value_piece, key_pos, score_scale):
    row_peak, row_total, weighted_sum = carried
    scores = (
        jnp.einsum("rgkd,sgd->gkrs", queries_half, key_piece, preferred_element_type=jnp.float32)
        * score_scale
    )
    visible = key_pos[None, :] <= query_pos[:, None]
    new_peak = jnp.maximum(row_peak, jnp.max(jnp.where(visible, scores, NEG_FILL), axis=-1))
    probabilities = jnp.where(visible, jnp.exp(scores - new_peak[..., None]), 0.0)
    row_total = jnp.sum(probabilities, axis=-1)
    update = jnp.einsum(
        "gkrs,sgd->gkrd",
        probabilities.astype(jnp.bfloat16),
        value_piece,
        preferred_element_type=jnp.float32,
    )
    return (new_peak, row_total, update)


def backward_update(
    carried,
    queries_half,
    grads_half,
    log_total,
    delta_rows,
    query_pos,
    key_piece,
    value_piece,
    key_pos,
    score_scale,
):
    scores = (
        jnp.einsum("rgkd,sgd->gkrs", queries_half, key_piece, preferred_element_type=jnp.float32)
        * score_scale
    )
    visible = key_pos[None, :] <= query_pos[:, None]
    probabilities = jnp.where(visible, jnp.exp(scores - log_total[..., None]), 0.0)
    prob_grad = jnp.einsum(
        "rgkd,sgd->gkrs", grads_half, value_piece, preferred_element_type=jnp.float32
    )
    score_grad = (probabilities * (prob_grad - delta_rows[..., None])).astype(jnp.bfloat16)
    return jnp.einsum("gkrs,sgd->rgkd", score_grad, key_piece, preferred_element_type=jnp.float32)


def keep_carried(carried):
    return carried


def body(
    stretch_order,
    attn_queries,
    attn_keys,
    attn_values,
    attn_grad,
    mamba_input,
    gate_input,
    state_write,
    state_read,
    step_raw,
    decay_log,
    skip_gain,
    norm_gain,
    mamba_grad,
):
    tok_rows = attn_queries.shape[0]
    half_rows = tok_rows // 2
    ctx_count = lax.axis_size("ctx")
    my_index = lax.axis_index("ctx")
    my_pair = stretch_order[my_index]
    kv_local = attn_keys.shape[1] // AHD
    per_kv = attn_queries.shape[1] // AHD // kv_local
    score_scale = AHD ** (-0.5)
    query_pos = key_positions(
        my_index * tok_rows, tok_rows, stretch_order, tok_rows, ctx_count
    ).reshape(2, half_rows)
    query_blocks = attn_queries.reshape(2, half_rows, kv_local, per_kv, AHD)
    grad_blocks = attn_grad.reshape(2, half_rows, kv_local, per_kv, AHD)
    start_half = (
        jnp.full((kv_local, per_kv, half_rows), NEG_FILL, jnp.float32),
        jnp.zeros((kv_local, per_kv, half_rows), jnp.float32),
        jnp.zeros((kv_local, per_kv, half_rows, AHD), jnp.float32),
    )
    carried = (start_half, start_half)
    pieces = (
        lax.all_gather(attn_keys, "ctx", axis=0, tiled=True),
        lax.all_gather(attn_values, "ctx", axis=0, tiled=True),
    )
    row_count = pieces[0].shape[0]
    key_pos = key_positions(jnp.int32(0), row_count, stretch_order, tok_rows, ctx_count)
    key_piece = pieces[0].reshape(row_count, kv_local, AHD)
    value_piece = pieces[1].reshape(row_count, kv_local, AHD)
    updated = []
    for fold_half_index in range(2):
        step_fn = partial(
            forward_update,
            queries_half=query_blocks[fold_half_index],
            query_pos=query_pos[fold_half_index],
            key_piece=key_piece,
            value_piece=value_piece,
            key_pos=key_pos,
            score_scale=score_scale,
        )
        future = jnp.min(key_pos) > jnp.max(query_pos[fold_half_index])
        updated.append(lax.cond(future, keep_carried, step_fn, carried[fold_half_index]))
    forward_state = tuple(updated)
    output_halves = []
    log_totals = []
    delta_halves = []
    for half_index in range(2):
        row_peak, row_total, weighted_sum = forward_state[half_index]
        output_half = jnp.transpose(weighted_sum / row_total[..., None], (2, 0, 1, 3)).astype(
            jnp.bfloat16
        )
        output_half = lax.optimization_barrier(output_half)
        delta_rows = jnp.sum(
            grad_blocks[half_index].astype(jnp.float32) * output_half.astype(jnp.float32), axis=-1
        )
        delta_halves.append(jnp.transpose(delta_rows, (1, 2, 0)))
        log_totals.append(row_peak + jnp.log(row_total))
        output_halves.append(output_half)
    attn_output = jnp.stack(output_halves).reshape(tok_rows, kv_local * per_kv * AHD)
    grad_start = jnp.zeros((half_rows, kv_local, per_kv, AHD), jnp.float32)
    carried = (grad_start, grad_start)
    pieces = (
        lax.all_gather(attn_keys, "ctx", axis=0, tiled=True),
        lax.all_gather(attn_values, "ctx", axis=0, tiled=True),
    )
    row_count = pieces[0].shape[0]
    key_pos = key_positions(jnp.int32(0), row_count, stretch_order, tok_rows, ctx_count)
    key_piece = pieces[0].reshape(row_count, kv_local, AHD)
    value_piece = pieces[1].reshape(row_count, kv_local, AHD)
    updated = []
    for half_index in range(2):
        step_fn = partial(
            backward_update,
            queries_half=query_blocks[half_index],
            grads_half=grad_blocks[half_index],
            log_total=log_totals[half_index],
            delta_rows=delta_halves[half_index],
            query_pos=query_pos[half_index],
            key_piece=key_piece,
            value_piece=value_piece,
            key_pos=key_pos,
            score_scale=score_scale,
        )
        future = jnp.min(key_pos) > jnp.max(query_pos[half_index])
        updated.append(lax.cond(future, keep_carried, step_fn, carried[half_index]))
    grad_state = tuple(updated)
    query_grad = (
        (jnp.stack(grad_state) * score_scale)
        .astype(jnp.bfloat16)
        .reshape(tok_rows, kv_local * per_kv * AHD)
    )
    heads_dev = mamba_input.shape[1] // MDIM
    groups_dev = state_write.shape[1] // NSTATE
    per_group = heads_dev // groups_dev
    input_blocks = mamba_input.reshape(2, half_rows, groups_dev, per_group, MDIM)
    write_blocks = state_write.reshape(2, half_rows, groups_dev, NSTATE)
    read_blocks = state_read.reshape(2, half_rows, groups_dev, NSTATE)
    rate_blocks = jax.nn.softplus(step_raw).reshape(2, half_rows, groups_dev, per_group)
    decay_rate = -jnp.exp(decay_log).reshape(groups_dev, per_group)
    skip_rate = skip_gain.reshape(groups_dev, per_group)
    first_parts = stretch_parts(
        input_blocks[0], write_blocks[0], read_blocks[0], rate_blocks[0], decay_rate, skip_rate
    )
    second_parts = stretch_parts(
        input_blocks[1], write_blocks[1], read_blocks[1], rate_blocks[1], decay_rate, skip_rate
    )
    into_first, into_second = state_chain(
        (first_parts[2], first_parts[3]), (second_parts[2], second_parts[3]), my_pair, ctx_count
    )
    mixed_first = first_parts[0] + carried_term(read_blocks[0], first_parts[1], into_first)
    mixed_second = second_parts[0] + carried_term(read_blocks[1], second_parts[1], into_second)
    mixed = jnp.stack([mixed_first, mixed_second]).reshape(tok_rows, heads_dev * MDIM)
    silu_gate = jax.nn.silu(gate_input.astype(jnp.float32))
    gated = mixed * silu_gate
    square_sum = lax.psum(jnp.sum(gated * gated, axis=-1), "tp")
    inverse_rms = lax.rsqrt(square_sum / (MAMBA_HEAD_HALF * MDIM) + NORM_EPS)[:, None]
    mamba_output = (gated * inverse_rms * norm_gain[None]).astype(jnp.bfloat16)
    scaled_grad = mamba_grad.astype(jnp.float32) * norm_gain[None]
    cross_sum = lax.psum(jnp.sum(scaled_grad * gated, axis=-1), "tp")
    gated_grad = (
        inverse_rms * scaled_grad
        - gated * inverse_rms**3 * (cross_sum / (MAMBA_HEAD_HALF * MDIM))[:, None]
    )
    mixed_grad = (gated_grad * silu_gate).reshape(2, half_rows, groups_dev, per_group, MDIM)
    touch_first = state_touch(read_blocks[0], first_parts[1], mixed_grad[0])
    touch_second = state_touch(read_blocks[1], second_parts[1], mixed_grad[1])
    after_second, after_first = state_chain(
        (second_parts[2], touch_second), (first_parts[2], touch_first), my_pair, ctx_count
    )
    states_in = (into_first, into_second)
    states_after = (after_first, after_second)
    input_parts = []
    write_parts = []
    read_parts = []
    for block_index in range(2):

        def local_fn(inputs_part, writes_part, reads_part, block_index=block_index):
            return stretch_full(
                inputs_part,
                writes_part,
                reads_part,
                rate_blocks[block_index],
                decay_rate,
                skip_rate,
                states_in[block_index],
            )

        primal, pullback = jax.vjp(
            local_fn, input_blocks[block_index], write_blocks[block_index], read_blocks[block_index]
        )
        input_change, write_change, read_change = pullback(
            (mixed_grad[block_index], states_after[block_index])
        )
        input_parts.append(input_change)
        write_parts.append(write_change)
        read_parts.append(read_change)
    input_grad = jnp.stack(input_parts).reshape(tok_rows, heads_dev * MDIM)
    write_grad = jnp.stack(write_parts).reshape(tok_rows, groups_dev * NSTATE)
    read_grad = jnp.stack(read_parts).reshape(tok_rows, groups_dev * NSTATE)
    return (attn_output, query_grad, mamba_output, input_grad, write_grad, read_grad)


def solution(mesh):
    placed = (
        P(),
        P("ctx", "tp"),
        P("ctx", "tp"),
        P("ctx", "tp"),
        P("ctx", "tp"),
        P("ctx", "tp"),
        P("ctx", "tp"),
        P("ctx", "tp"),
        P("ctx", "tp"),
        P("ctx", "tp"),
        P("tp"),
        P("tp"),
        P("tp"),
        P("ctx", "tp"),
    )
    return jax.shard_map(
        body,
        mesh=mesh,
        in_specs=placed,
        out_specs=(
            P("ctx", "tp"),
            P("ctx", "tp"),
            P("ctx", "tp"),
            P("ctx", "tp"),
            P("ctx", "tp"),
            P("ctx", "tp"),
        ),
        check_vma=False,
    )
```

profile of v0, /device:TPU:6, one launch (start us, length us, event | category | flops | bytes accessed | tf_op | source)
XLA Modules:
  0.0 505.9 jit_solution(729966237933211003)
XLA Ops:
  23.8 8.7 %collective-permute-done.18 = bf16[4,8]{1,0:T(4,128)(2,1)S(1)} collective-permute-done((bf16[4,8]{1,0:T(4,128)(2,1)S(1)}, bf16[4,8]{1,0:T(4,128)(2,1)S(1)}, u32[]{:S(2)}, u32[]{:S(2)}) %collective-permute-start.18) | collective-permute-done | bytes 96 | tf_op jit(solution)/shard_map/ppermute | solution.py:29
  38.9 3.1 collective-permute-done.22
  42.9 4.4 collective-permute-done.24
  48.4 2.5 collective-permute-start.1
  50.9 11.6 %collective-permute-done.1 = bf16[4,8]{1,0:T(4,128)(2,1)S(1)} collective-permute-done((bf16[4,8]{1,0:T(4,128)(2,1)S(1)}, bf16[4,8]{1,0:T(4,128)(2,1)S(1)}, u32[]{:S(2)}, u32[]{:S(2)}) %collective-permute-start.1) | collective-permute-done | bytes 96 | tf_op jit(solution)/shard_map/ppermute | solution.py:29
  64.6 3.3 collective-permute-start.3
  67.9 14.2 %collective-permute-done.3 = bf16[4,8]{1,0:T(4,128)(2,1)S(1)} collective-permute-done((bf16[4,8]{1,0:T(4,128)(2,1)S(1)}, bf16[4,8]{1,0:T(4,128)(2,1)S(1)}, u32[]{:S(2)}, u32[]{:S(2)}) %collective-permute-start.3) | collective-permute-done | bytes 96 | tf_op jit(solution)/shard_map/ppermute | solution.py:29
  82.1 10.0 %collective-permute-done.4 = bf16[4,8,64,128]{3,2,1,0:T(8,128)(2,1)S(1)} collective-permute-done((bf16[4,8,64,128]{3,2,1,0:T(8,128)(2,1)S(1)}, bf16[4,8,64,128]{3,2,1,0:T(8,128)(2,1)S(1)}, u32[]{:S(2)}, u32[]{:S(2)}) %collective-permute-start.4) | collective-permute-done | bytes 524320 | tf_op jit(solution)/shard_map/ppermute | solution.py:29
  93.2 5.3 %collective-permute-start.6 = (bf16[4,8,64,128]{3,2,1,0:T(8,128)(2,1)}, bf16[4,8,64,128]{3,2,1,0:T(8,128)(2,1)S(1)}, u32[]{:S(2)}, u32[]{:S(2)}) collective-permute-start(bf16[4,8,64,128]{3,2,1,0:T(8,128)(2,1)} %fusion.143), channel_id=1, source_target_pairs={{0,16},{2,18},{4,20},{6,22},{8,24},{10,26},{12,28},{14,30},{16,0},... | collective-permute-start | bytes 1572872 | tf_op jit(solution)/shard_map/ppermute | solution.py:29
  103.2 5.1 %collective-permute-done.5 = bf16[4,8]{1,0:T(4,128)(2,1)S(1)} collective-permute-done((bf16[4,8]{1,0:T(4,128)(2,1)S(1)}, bf16[4,8]{1,0:T(4,128)(2,1)S(1)}, u32[]{:S(2)}, u32[]{:S(2)}) %collective-permute-start.5) | collective-permute-done | bytes 96 | tf_op jit(solution)/shard_map/ppermute | solution.py:29
  108.9 8.8 %collective-permute-done.6 = bf16[4,8,64,128]{3,2,1,0:T(8,128)(2,1)S(1)} collective-permute-done((bf16[4,8,64,128]{3,2,1,0:T(8,128)(2,1)}, bf16[4,8,64,128]{3,2,1,0:T(8,128)(2,1)S(1)}, u32[]{:S(2)}, u32[]{:S(2)}) %collective-permute-start.6) | collective-permute-done | bytes 524320 | tf_op jit(solution)/shard_map/ppermute | solution.py:29
  118.5 2.2 fusion.244
  120.7 2.3 fusion.263
  127.1 3.7 collective-permute-done.8
  131.6 5.9 %collective-permute-done.9 = bf16[4,8,64,128]{3,2,1,0:T(8,128)(2,1)S(1)} collective-permute-done((bf16[4,8,64,128]{3,2,1,0:T(8,128)(2,1)}, bf16[4,8,64,128]{3,2,1,0:T(8,128)(2,1)S(1)}, u32[]{:S(2)}, u32[]{:S(2)}) %collective-permute-start.9) | collective-permute-done | bytes 524320 | tf_op jit(solution)/shard_map/ppermute | solution.py:29
  137.7 4.8 collective-permute-start.11
  145.5 6.9 %collective-permute-done.10 = bf16[4,8]{1,0:T(4,128)(2,1)S(1)} collective-permute-done((bf16[4,8]{1,0:T(4,128)(2,1)S(1)}, bf16[4,8]{1,0:T(4,128)(2,1)S(1)}, u32[]{:S(2)}, u32[]{:S(2)}) %collective-permute-start.10) | collective-permute-done | bytes 96 | tf_op jit(solution)/shard_map/ppermute | solution.py:29
  153.2 2.2 fusion.247
  155.4 8.1 %collective-permute-start.13 = (bf16[4,8,64,128]{3,2,1,0:T(8,128)(2,1)}, bf16[4,8,64,128]{3,2,1,0:T(8,128)(2,1)S(1)}, u32[]{:S(2)}, u32[]{:S(2)}) collective-permute-start(bf16[4,8,64,128]{3,2,1,0:T(8,128)(2,1)} %get-tuple-element.273), channel_id=1, source_target_pairs={{0,24},{2,26},{4,28},{6,30},{8,0},{10,2},{12,4},{14,6},{16,8},{18,... | collective-permute-start | bytes 1572872 | tf_op jit(solution)/shard_map/ppermute | solution.py:29
  165.8 6.9 %collective-permute-done.12 = bf16[4,8]{1,0:T(4,128)(2,1)S(1)} collective-permute-done((bf16[4,8]{1,0:T(4,128)(2,1)}, bf16[4,8]{1,0:T(4,128)(2,1)S(1)}, u32[]{:S(2)}, u32[]{:S(2)}) %collective-permute-start.12) | collective-permute-done | bytes 96 | tf_op jit(solution)/shard_map/ppermute | solution.py:29
  183.3 3.0 fusion.81
  186.3 2.8 collective-permute-start.14
  189.9 5.3 %collective-permute-done.14 = bf16[4,8]{1,0:T(4,128)(2,1)S(1)} collective-permute-done((bf16[4,8]{1,0:T(4,128)(2,1)}, bf16[4,8]{1,0:T(4,128)(2,1)S(1)}, u32[]{:S(2)}, u32[]{:S(2)}) %collective-permute-start.14) | collective-permute-done | bytes 96 | tf_op jit(solution)/shard_map/ppermute | solution.py:29
  195.9 21.6 %collective-permute-start.7 = (bf16[4,8,64,128]{3,2,1,0:T(8,128)(2,1)}, bf16[4,8,64,128]{3,2,1,0:T(8,128)(2,1)S(1)}, u32[]{:S(2)}, u32[]{:S(2)}) collective-permute-start(bf16[4,8,64,128]{3,2,1,0:T(8,128)(2,1)} %get-tuple-element.267), channel_id=1, source_target_pairs={{0,2},{2,4},{4,6},{6,8},{8,10},{10,12},{12,14},{14,16},{16,18},{18... | collective-permute-start | bytes 1572872 | tf_op jit(solution)/shard_map/ppermute | solution.py:29
  217.5 9.2 %collective-permute-done.15 = bf16[4,8,64,128]{3,2,1,0:T(8,128)(2,1)S(1)} collective-permute-done((bf16[4,8,64,128]{3,2,1,0:T(8,128)(2,1)}, bf16[4,8,64,128]{3,2,1,0:T(8,128)(2,1)S(1)}, u32[]{:S(2)}, u32[]{:S(2)}) %collective-permute-start.15) | collective-permute-done | bytes 524320 | tf_op jit(solution)/shard_map/ppermute | solution.py:29
  230.8 3.0 collective-permute-done.7
  235.5 4.0 collective-permute-done.16
  245.9 2.5 all-reduce
  248.4 2.6 subtract_multiply_fusion
  253.9 3.8 collective-permute-start.17
  258.8 10.4 %collective-permute-done.17 = bf16[4,8,64,128]{3,2,1,0:T(8,128)(2,1)S(1)} collective-permute-done((bf16[4,8,64,128]{3,2,1,0:T(8,128)(2,1)S(1)}, bf16[4,8,64,128]{3,2,1,0:T(8,128)(2,1)S(1)}, u32[]{:S(2)}, u32[]{:S(2)}) %collective-permute-start.17) | collective-permute-done | bytes 524320 | tf_op jit(solution)/shard_map/ppermute | solution.py:29
  270.3 8.8 %collective-permute-start.19 = (bf16[4,8,64,128]{3,2,1,0:T(8,128)(2,1)}, bf16[4,8,64,128]{3,2,1,0:T(8,128)(2,1)}, u32[]{:S(2)}, u32[]{:S(2)}) collective-permute-start(bf16[4,8,64,128]{3,2,1,0:T(8,128)(2,1)} %fusion.146), channel_id=1, source_target_pairs={{0,4},{2,6},{4,8},{6,10},{8,12},{10,14},{12,16},{14,18},{16,20},{1... | collective-permute-start | bytes 1572872 | tf_op jit(solution)/shard_map/ppermute | solution.py:29
  286.0 4.1 collective-permute-done.19
  290.1 2.4 fusion.242
  294.5 2.6 collective-permute-start.28
  299.0 11.1 %collective-permute-start.30 = (bf16[4,8]{1,0:T(4,128)(2,1)S(1)}, bf16[4,8]{1,0:T(4,128)(2,1)S(1)}, u32[]{:S(2)}, u32[]{:S(2)}) collective-permute-start(bf16[4,8]{1,0:T(4,128)(2,1)S(1)} %get-tuple-element.248), channel_id=1, source_target_pairs={{0,24},{2,26},{4,28},{6,30},{8,0},{10,2},{12,4},{14,6},{16,8},{18,... | collective-permute-start | bytes 200 | tf_op jit(solution)/shard_map/ppermute | solution.py:29
  312.6 12.7 %conditional.5 = (f32[4,4,64]{2,1,0:T(4,128)}, f32[4,4,64]{2,1,0:T(4,128)}, f32[4,4,64]{2,1,0:T(4,128)}, f32[4,4,64,128]{3,1,0,2:T(4,128)S(1)}) conditional(s32[]{:T(128)} %convert_element_type.386, (s32[2048]{0:T(1024)}, s32[1,64]{1,0:T(1,128)}, bf16[2048,4,128]{0,2,1:T(8,128)(2,1)}, bf16[64,4,4,128]{3,2,1,0:T(4,128)(2,1)}, ...), branch_computations={%region_9.12_spmd, %region_12.13_spmd} | conditional | flops 1096940544 | bytes 40149308 | solution.py:229
  313.9 3.4 fusion.14
  317.9 3.5 fusion.18
  322.7 2.3 fusion.19
  330.8 13.3 %conditional.4 = (f32[4,4,64]{2,1,0:T(4,128)}, f32[4,4,64]{2,1,0:T(4,128)}, f32[4,4,64]{2,1,0:T(4,128)}, f32[4,4,64,128]{3,1,0,2:T(4,128)}) conditional(s32[]{:T(128)} %convert_element_type.383, (s32[2048]{0:T(1024)}, s32[1,64]{1,0:T(1,128)}, bf16[2048,4,128]{0,2,1:T(8,128)(2,1)}, bf16[64,4,4,128]{3,2,1,0:T(4,128)(2,1)S(1)}, ...), branch_computations={%region_4.7_spmd, %region_7.8_spmd} | conditional | flops 1096940544 | bytes 40149308 | solution.py:229
  331.6 3.4 fusion
  335.7 3.5 fusion.4
  340.5 2.3 fusion.5
  349.8 2.5 squeeze.83
  352.3 2.7 fusion.239
  356.0 4.1 fusion.265
  364.6 16.5 %conditional.7 = (f32[1,64,4,4,128]{4,1,3,2,0:T(8,128)}) conditional(s32[]{:T(128)} %convert_element_type.386, (s32[2048]{0:T(1024)}, s32[1,64]{1,0:T(1,128)}, bf16[2048,4,128]{0,2,1:T(8,128)(2,1)S(1)}, bf16[64,4,4,128]{3,2,1,0:T(4,128)(2,1)}, f32[4,4,64]{2,1,0:T(4,128)}, /*index=5*/f32[4,4,64]{2,1,0:T(4,128)}, bf16[2048,4,128]{0,2,1:T(8,128)(2,1)}, ...), branch_computations={%region_17.18_spmd, %region_18.19_spmd} | conditional | flops 1623327744 | bytes 24450368 | solution.py:272
  364.6 5.6 %fusion.66 = f32[4,2048,64,4]{1,2,3,0:T(8,128)} fusion(bf16[2048,4,128]{0,2,1:T(8,128)(2,1)S(1)} %get-tuple-element.233, bf16[64,4,4,128]{3,2,1,0:T(4,128)(2,1)} %get-tuple-element.234), kind=kOutput, calls=%fused_computation.70 | convolution fusion | flops 536870912 | bytes 10747904 | tf_op jit(solution)/shard_map/cond/branch_0_fun/rgkd,sgd->gkrs/dot_general | solution.py:158
  372.7 8.4 %fusion.68 = f32[1,64,4,4,128]{4,1,3,2,0:T(8,128)} fusion(bf16[2048,4,128]{0,2,1:T(8,128)(2,1)S(1)} %get-tuple-element.233, f32[4,2048,64,4]{1,2,3,0:T(8,128)} %fusion.66, f32[4,4,64]{2,1,0:T(4,128)S(1)} %copy.298, f32[4,4,64]{2,1,0:T(4,128)S(1)} %add.111, pred[64,2048]{1,0:T(8,128)(4,1)} %broadcast_compare_fusion.3, ...), kind=kOutput, calls=%fused_computation.72 | convolution fusion | flops 1086324736 | bytes 13508608 | tf_op jit(solution)/shard_map/cond/branch_0_fun/gkrs,sgd->rgkd/dot_general | solution.py:167
  383.1 15.1 %conditional.6 = (f32[1,64,4,4,128]{4,1,3,2,0:T(8,128)}) conditional(s32[]{:T(128)} %convert_element_type.383, (s32[2048]{0:T(1024)}, s32[1,64]{1,0:T(1,128)S(1)}, bf16[2048,4,128]{0,2,1:T(8,128)(2,1)S(1)}, bf16[64,4,4,128]{3,2,1,0:T(4,128)(2,1)S(1)}, f32[4,4,64]{2,1,0:T(4,128)}, /*index=5*/f32[4,4,64]{2,1,0:T(4,128)}, ...), branch_computations={%region_14.15_spmd, %region_15.16_spmd} | conditional | flops 1623327744 | bytes 24449316 | solution.py:272
  383.4 4.6 fusion.41
  389.8 8.4 %fusion.43 = f32[1,64,4,4,128]{4,1,3,2,0:T(8,128)} fusion(bf16[2048,4,128]{0,2,1:T(8,128)(2,1)S(1)} %get-tuple-element.224, f32[4,2048,64,4]{1,2,3,0:T(8,128)} %fusion.41, f32[4,4,64]{2,1,0:T(4,128)S(1)} %copy.293, f32[4,4,64]{2,1,0:T(4,128)S(1)} %add.110, pred[64,2048]{1,0:T(8,128)(4,1)S(1)} %broadcast_compare_fusion.2, ...), kind=kOutput, calls=%fused_computation.50 | convolution fusion | flops 1086324736 | bytes 13508608 | tf_op jit(solution)/shard_map/cond/branch_0_fun/gkrs,sgd->rgkd/dot_general | solution.py:167
  410.6 10.3 %collective-permute-done.27 = bf16[4,8,64,128]{3,2,1,0:T(8,128)(2,1)S(1)} collective-permute-done((bf16[4,8,64,128]{3,2,1,0:T(8,128)(2,1)S(1)}, bf16[4,8,64,128]{3,2,1,0:T(8,128)(2,1)S(1)}, u32[]{:S(2)}, u32[]{:S(2)}) %collective-permute-start.27) | collective-permute-done | bytes 524320 | tf_op jit(solution)/shard_map/ppermute | solution.py:29
  421.0 2.6 fusion.236
  423.6 3.2 collective-permute-start.29
  428.8 2.5 fusion.109
  431.3 5.1 %collective-permute-done.29 = bf16[4,8,64,128]{3,2,1,0:T(8,128)(2,1)S(1)} collective-permute-done((bf16[4,8,64,128]{3,2,1,0:T(8,128)(2,1)}, bf16[4,8,64,128]{3,2,1,0:T(8,128)(2,1)S(1)}, u32[]{:S(2)}, u32[]{:S(2)}) %collective-permute-start.29) | collective-permute-done | bytes 524320 | tf_op jit(solution)/shard_map/ppermute | solution.py:29
  437.2 2.3 fusion.149
  439.4 3.7 fusion.123
  446.6 2.4 collective-permute-start.33
  449.0 3.0 fusion.125
  452.0 21.5 %collective-permute-done.31 = bf16[4,8,64,128]{3,2,1,0:T(8,128)(2,1)} collective-permute-done((bf16[4,8,64,128]{3,2,1,0:T(8,128)(2,1)}, bf16[4,8,64,128]{3,2,1,0:T(8,128)(2,1)}, u32[]{:S(2)}, u32[]{:S(2)}) %collective-permute-start.31) | collective-permute-done | bytes 524320 | tf_op jit(solution)/shard_map/ppermute | solution.py:29
  480.2 11.2 %collective-permute-done.32 = bf16[4,8,64,128]{3,2,1,0:T(8,128)(2,1)S(1)} collective-permute-done((bf16[4,8,64,128]{3,2,1,0:T(8,128)(2,1)S(1)}, bf16[4,8,64,128]{3,2,1,0:T(8,128)(2,1)S(1)}, u32[]{:S(2)}, u32[]{:S(2)}) %collective-permute-start.32) | collective-permute-done | bytes 524320 | tf_op jit(solution)/shard_map/ppermute | solution.py:29
  (285 shorter events, 143.5 us)
Async XLA Ops:
  7.2 305.4 %all-gather.3.cloned.1.call-start = ((), (), s32[]{:S(2)}) async-start(), calls=%async_computation | async-start | bytes 2228224 | tf_op jit(solution)/shard_map/all_gather | solution.py:210
  8.9 303.7 %all-gather.5.cloned.1.call-start = ((), (), s32[]{:S(2)}) async-start(), calls=%async_computation.1 | async-start | bytes 2228224 | tf_op jit(solution)/shard_map/all_gather | solution.py:211
  16.3 46.1 %copy-start.7 = (bf16[64,4,8,64]{3,2,1,0:T(8,128)(2,1)}, bf16[64,4,8,64]{3,2,1,0:T(8,128)(2,1)S(1)}, u32[]{:S(2)}) copy-start(bf16[64,4,8,64]{3,2,1,0:T(8,128)(2,1)S(1)} %squeeze.37) | copy-start | bytes 786436
  17.3 30.5 %collective-permute-start = (bf16[4,8,64,128]{3,2,1,0:T(8,128)(2,1)S(1)}, bf16[4,8,64,128]{3,2,1,0:T(8,128)(2,1)S(1)}, u32[]{:S(2)}, u32[]{:S(2)}) collective-permute-start(bf16[4,8,64,128]{3,2,1,0:T(8,128)(2,1)S(1)} %get-tuple-element.328), channel_id=1, source_target_pairs={{0,2},{2,4},{4,6},{6,8},{8,10},{10,12},{12,14},{14,16},{16,18},{18... | collective-permute-start | bytes 1572872 | tf_op jit(solution)/shard_map/ppermute | solution.py:29
  19.1 13.4 %collective-permute-start.18 = (bf16[4,8]{1,0:T(4,128)(2,1)S(1)}, bf16[4,8]{1,0:T(4,128)(2,1)S(1)}, u32[]{:S(2)}, u32[]{:S(2)}) collective-permute-start(bf16[4,8]{1,0:T(4,128)(2,1)S(1)} %fusion.232), channel_id=1, source_target_pairs={{0,2},{2,4},{4,6},{6,8},{8,10},{10,12},{12,14},{14,16},{16,18},{18... | collective-permute-start | bytes 200 | tf_op jit(solution)/shard_map/ppermute | solution.py:29
  33.1 66.8 %copy-start.42 = (f32[4,8]{1,0:T(4,128)}, f32[4,8]{1,0:T(4,128)S(1)}, u32[]{:S(2)}) copy-start(f32[4,8]{1,0:T(4,128)S(1)} %get-tuple-element.263) | copy-start | bytes 388
  33.1 3.6 collective-permute-start.20
  36.7 5.4 %collective-permute-start.22 = (bf16[4,8]{1,0:T(4,128)(2,1)S(1)}, bf16[4,8]{1,0:T(4,128)(2,1)S(1)}, u32[]{:S(2)}, u32[]{:S(2)}) collective-permute-start(bf16[4,8]{1,0:T(4,128)(2,1)S(1)} %get-tuple-element.260), channel_id=1, source_target_pairs={{0,8},{2,10},{4,12},{6,14},{8,16},{10,18},{12,20},{14,22},{16,24},... | collective-permute-start | bytes 200 | tf_op jit(solution)/shard_map/ppermute | solution.py:29
  42.1 5.2 %collective-permute-start.24 = (bf16[4,8]{1,0:T(4,128)(2,1)S(1)}, bf16[4,8]{1,0:T(4,128)(2,1)S(1)}, u32[]{:S(2)}, u32[]{:S(2)}) collective-permute-start(bf16[4,8]{1,0:T(4,128)(2,1)S(1)} %get-tuple-element.256), channel_id=1, source_target_pairs={{0,16},{2,18},{4,20},{6,22},{8,24},{10,26},{12,28},{14,30},{16,0},... | collective-permute-start | bytes 200 | tf_op jit(solution)/shard_map/ppermute | solution.py:29
  47.8 52.1 %copy-start.33 = (f32[4,8]{1,0:T(4,128)}, f32[4,8]{1,0:T(4,128)S(1)}, u32[]{:S(2)}) copy-start(f32[4,8]{1,0:T(4,128)S(1)} %get-tuple-element.302) | copy-start | bytes 388
  48.1 14.3 %collective-permute-start.2 = (bf16[4,8,64,128]{3,2,1,0:T(8,128)(2,1)S(1)}, bf16[4,8,64,128]{3,2,1,0:T(8,128)(2,1)S(1)}, u32[]{:S(2)}, u32[]{:S(2)}) collective-permute-start(bf16[4,8,64,128]{3,2,1,0:T(8,128)(2,1)S(1)} %fusion.142), channel_id=1, source_target_pairs={{0,4},{2,6},{4,8},{6,10},{8,12},{10,14},{12,16},{14,18},{16,20},{1... | collective-permute-start | bytes 1572872 | tf_op jit(solution)/shard_map/ppermute | solution.py:29
  48.4 14.0 %collective-permute-start.1 = (bf16[4,8]{1,0:T(4,128)(2,1)S(1)}, bf16[4,8]{1,0:T(4,128)(2,1)S(1)}, u32[]{:S(2)}, u32[]{:S(2)}) collective-permute-start(bf16[4,8]{1,0:T(4,128)(2,1)S(1)} %get-tuple-element.301), channel_id=1, source_target_pairs={{0,2},{2,4},{4,6},{6,8},{8,10},{10,12},{12,14},{14,16},{16,18},{18... | collective-permute-start | bytes 200 | tf_op jit(solution)/shard_map/ppermute | solution.py:29
  62.8 29.3 %collective-permute-start.4 = (bf16[4,8,64,128]{3,2,1,0:T(8,128)(2,1)S(1)}, bf16[4,8,64,128]{3,2,1,0:T(8,128)(2,1)S(1)}, u32[]{:S(2)}, u32[]{:S(2)}) collective-permute-start(bf16[4,8,64,128]{3,2,1,0:T(8,128)(2,1)S(1)} %get-tuple-element.283), channel_id=1, source_target_pairs={{0,8},{2,10},{4,12},{6,14},{8,16},{10,18},{12,20},{14,22},{16,24},... | collective-permute-start | bytes 1572872 | tf_op jit(solution)/shard_map/ppermute | solution.py:29
  64.6 17.5 %collective-permute-start.3 = (bf16[4,8]{1,0:T(4,128)(2,1)S(1)}, bf16[4,8]{1,0:T(4,128)(2,1)S(1)}, u32[]{:S(2)}, u32[]{:S(2)}) collective-permute-start(bf16[4,8]{1,0:T(4,128)(2,1)S(1)} %get-tuple-element.281), channel_id=1, source_target_pairs={{0,4},{2,6},{4,8},{6,10},{8,12},{10,14},{12,16},{14,18},{16,20},{1... | collective-permute-start | bytes 200 | tf_op jit(solution)/shard_map/ppermute | solution.py:29
  82.1 35.5 %copy-start.37 = (f32[4,8]{1,0:T(4,128)}, f32[4,8]{1,0:T(4,128)S(1)}, u32[]{:S(2)}) copy-start(f32[4,8]{1,0:T(4,128)S(1)} %get-tuple-element.280) | copy-start | bytes 388
  93.2 24.5 %collective-permute-start.6 = (bf16[4,8,64,128]{3,2,1,0:T(8,128)(2,1)}, bf16[4,8,64,128]{3,2,1,0:T(8,128)(2,1)S(1)}, u32[]{:S(2)}, u32[]{:S(2)}) collective-permute-start(bf16[4,8,64,128]{3,2,1,0:T(8,128)(2,1)} %fusion.143), channel_id=1, source_target_pairs={{0,16},{2,18},{4,20},{6,22},{8,24},{10,26},{12,28},{14,30},{16,0},... | collective-permute-start | bytes 1572872 | tf_op jit(solution)/shard_map/ppermute | solution.py:29
  99.9 53.2 %copy-start.13 = (bf16[64,4,8,64]{3,2,1,0:T(8,128)(2,1)}, bf16[64,4,8,64]{3,2,1,0:T(8,128)(2,1)S(1)}, u32[]{:S(2)}) copy-start(bf16[64,4,8,64]{3,2,1,0:T(8,128)(2,1)S(1)} %squeeze.80) | copy-start | bytes 786436
  100.9 79.5 %copy-start.16 = (bf16[64,4,128]{2,1,0:T(4,128)(2,1)}, bf16[64,4,128]{2,1,0:T(4,128)(2,1)S(1)}, u32[]{:S(2)}) copy-start(bf16[64,4,128]{2,1,0:T(4,128)(2,1)S(1)} %squeeze.79) | copy-start | bytes 196612
  102.4 5.8 %collective-permute-start.5 = (bf16[4,8]{1,0:T(4,128)(2,1)S(1)}, bf16[4,8]{1,0:T(4,128)(2,1)S(1)}, u32[]{:S(2)}, u32[]{:S(2)}) collective-permute-start(bf16[4,8]{1,0:T(4,128)(2,1)S(1)} %get-tuple-element.279), channel_id=1, source_target_pairs={{0,8},{2,10},{4,12},{6,14},{8,16},{10,18},{12,20},{14,22},{16,24},... | collective-permute-start | bytes 200 | tf_op jit(solution)/shard_map/ppermute | solution.py:29
  120.7 118.8 %copy-start.4 = (f32[4,8,64,128]{3,2,1,0:T(8,128)}, f32[4,8,64,128]{3,2,1,0:T(8,128)S(1)}, u32[]{:S(2)}) copy-start(f32[4,8,64,128]{3,2,1,0:T(8,128)S(1)} %get-tuple-element.268) | copy-start | bytes 3145732
  123.0 14.4 %collective-permute-start.9 = (bf16[4,8,64,128]{3,2,1,0:T(8,128)(2,1)}, bf16[4,8,64,128]{3,2,1,0:T(8,128)(2,1)S(1)}, u32[]{:S(2)}, u32[]{:S(2)}) collective-permute-start(bf16[4,8,64,128]{3,2,1,0:T(8,128)(2,1)} %get-tuple-element.330), channel_id=1, source_target_pairs={{0,30},{2,0},{4,2},{6,4},{8,6},{10,8},{12,10},{14,12},{16,14},{18,... | collective-permute-start | bytes 1572872 | tf_op jit(solution)/shard_map/ppermute | solution.py:29
  126.3 4.6 collective-permute-start.8
  137.7 15.5 %collective-permute-start.11 = (bf16[4,8,64,128]{3,2,1,0:T(8,128)(2,1)S(1)}, bf16[4,8,64,128]{3,2,1,0:T(8,128)(2,1)S(1)}, u32[]{:S(2)}, u32[]{:S(2)}) collective-permute-start(bf16[4,8,64,128]{3,2,1,0:T(8,128)(2,1)S(1)} %fusion.144), channel_id=1, source_target_pairs={{0,28},{2,30},{4,0},{6,2},{8,4},{10,6},{12,8},{14,10},{16,12},{18,... | collective-permute-start | bytes 1572872 | tf_op jit(solution)/shard_map/ppermute | solution.py:29
  145.4 6.9 %collective-permute-start.10 = (bf16[4,8]{1,0:T(4,128)(2,1)S(1)}, bf16[4,8]{1,0:T(4,128)(2,1)S(1)}, u32[]{:S(2)}, u32[]{:S(2)}) collective-permute-start(bf16[4,8]{1,0:T(4,128)(2,1)S(1)} %get-tuple-element.275), channel_id=1, source_target_pairs={{0,30},{2,0},{4,2},{6,4},{8,6},{10,8},{12,10},{14,12},{16,14},{18,... | collective-permute-start | bytes 200 | tf_op jit(solution)/shard_map/ppermute | solution.py:29
  155.4 18.6 %collective-permute-start.13 = (bf16[4,8,64,128]{3,2,1,0:T(8,128)(2,1)}, bf16[4,8,64,128]{3,2,1,0:T(8,128)(2,1)S(1)}, u32[]{:S(2)}, u32[]{:S(2)}) collective-permute-start(bf16[4,8,64,128]{3,2,1,0:T(8,128)(2,1)} %get-tuple-element.273), channel_id=1, source_target_pairs={{0,24},{2,26},{4,28},{6,30},{8,0},{10,2},{12,4},{14,6},{16,8},{18,... | collective-permute-start | bytes 1572872 | tf_op jit(solution)/shard_map/ppermute | solution.py:29
  165.8 6.9 %collective-permute-start.12 = (bf16[4,8]{1,0:T(4,128)(2,1)}, bf16[4,8]{1,0:T(4,128)(2,1)S(1)}, u32[]{:S(2)}, u32[]{:S(2)}) collective-permute-start(bf16[4,8]{1,0:T(4,128)(2,1)} %get-tuple-element.271), channel_id=1, source_target_pairs={{0,28},{2,30},{4,0},{6,2},{8,4},{10,6},{12,8},{14,10},{16,12},{18,... | collective-permute-start | bytes 200 | tf_op jit(solution)/shard_map/ppermute | solution.py:29
  175.6 51.2 %collective-permute-start.15 = (bf16[4,8,64,128]{3,2,1,0:T(8,128)(2,1)}, bf16[4,8,64,128]{3,2,1,0:T(8,128)(2,1)S(1)}, u32[]{:S(2)}, u32[]{:S(2)}) collective-permute-start(bf16[4,8,64,128]{3,2,1,0:T(8,128)(2,1)} %fusion.145), channel_id=1, source_target_pairs={{0,16},{2,18},{4,20},{6,22},{8,24},{10,26},{12,28},{14,30},{16,0},... | collective-permute-start | bytes 1572872 | tf_op jit(solution)/shard_map/ppermute | solution.py:29
  181.3 71.0 %copy-start.25 = (f32[64,4,8]{0,2,1:T(8,128)}, f32[64,4,8]{0,2,1:T(8,128)S(1)}, u32[]{:S(2)}) copy-start(f32[64,4,8]{0,2,1:T(8,128)S(1)} %copy.321) | copy-start | bytes 24580
  182.3 51.5 %copy-start.48 = (f32[4,8,64]{2,1,0:T(8,128)}, f32[4,8,64]{2,1,0:T(8,128)S(1)}, u32[]{:S(2)}) copy-start(f32[4,8,64]{2,1,0:T(8,128)S(1)} %copy.301) | copy-start | bytes 24580
  183.3 59.0 %copy-start.32 = (f32[64,4,8]{0,2,1:T(8,128)}, f32[64,4,8]{0,2,1:T(8,128)S(1)}, u32[]{:S(2)}) copy-start(f32[64,4,8]{0,2,1:T(8,128)S(1)} %copy.307) | copy-start | bytes 24580
  186.3 9.0 %collective-permute-start.14 = (bf16[4,8]{1,0:T(4,128)(2,1)}, bf16[4,8]{1,0:T(4,128)(2,1)S(1)}, u32[]{:S(2)}, u32[]{:S(2)}) collective-permute-start(bf16[4,8]{1,0:T(4,128)(2,1)} %get-tuple-element.269), channel_id=1, source_target_pairs={{0,24},{2,26},{4,28},{6,30},{8,0},{10,2},{12,4},{14,6},{16,8},{18,... | collective-permute-start | bytes 200 | tf_op jit(solution)/shard_map/ppermute | solution.py:29
  189.9 50.4 %copy-start.15 = (f32[64,4,8,64]{3,0,2,1:T(8,128)S(1)}, f32[64,4,8,64]{3,0,2,1:T(8,128)}, u32[]{:S(2)}) copy-start(f32[64,4,8,64]{3,0,2,1:T(8,128)} %fusion.81) | copy-start | bytes 1572868
  195.9 37.9 %collective-permute-start.7 = (bf16[4,8,64,128]{3,2,1,0:T(8,128)(2,1)}, bf16[4,8,64,128]{3,2,1,0:T(8,128)(2,1)S(1)}, u32[]{:S(2)}, u32[]{:S(2)}) collective-permute-start(bf16[4,8,64,128]{3,2,1,0:T(8,128)(2,1)} %get-tuple-element.267), channel_id=1, source_target_pairs={{0,2},{2,4},{4,6},{6,8},{8,10},{10,12},{12,14},{14,16},{16,18},{18... | collective-permute-start | bytes 1572872 | tf_op jit(solution)/shard_map/ppermute | solution.py:29
  227.8 11.7 %collective-permute-start.16 = (bf16[4,8,64,128]{3,2,1,0:T(8,128)(2,1)S(1)}, bf16[4,8,64,128]{3,2,1,0:T(8,128)(2,1)S(1)}, u32[]{:S(2)}, u32[]{:S(2)}) collective-permute-start(bf16[4,8,64,128]{3,2,1,0:T(8,128)(2,1)S(1)} %fusion.131), channel_id=1, source_target_pairs={{0,30},{2,0},{4,2},{6,4},{8,6},{10,8},{12,10},{14,12},{16,14},{18,... | collective-permute-start | bytes 1572872 | tf_op jit(solution)/shard_map/ppermute | solution.py:29
  243.5 25.7 %copy-start.34 = (f32[4,8]{1,0:T(4,128)S(1)}, f32[4,8]{1,0:T(4,128)}, u32[]{:S(2)}) copy-start(f32[4,8]{1,0:T(4,128)} %get-tuple-element.303) | copy-start | bytes 388
  253.9 15.3 %collective-permute-start.17 = (bf16[4,8,64,128]{3,2,1,0:T(8,128)(2,1)S(1)}, bf16[4,8,64,128]{3,2,1,0:T(8,128)(2,1)S(1)}, u32[]{:S(2)}, u32[]{:S(2)}) collective-permute-start(bf16[4,8,64,128]{3,2,1,0:T(8,128)(2,1)S(1)} %get-tuple-element.332), channel_id=1, source_target_pairs={{0,2},{2,4},{4,6},{6,8},{8,10},{10,12},{12,14},{14,16},{16,18},{18... | collective-permute-start | bytes 1572872 | tf_op jit(solution)/shard_map/ppermute | solution.py:29
  270.3 19.8 %collective-permute-start.19 = (bf16[4,8,64,128]{3,2,1,0:T(8,128)(2,1)}, bf16[4,8,64,128]{3,2,1,0:T(8,128)(2,1)}, u32[]{:S(2)}, u32[]{:S(2)}) collective-permute-start(bf16[4,8,64,128]{3,2,1,0:T(8,128)(2,1)} %fusion.146), channel_id=1, source_target_pairs={{0,4},{2,6},{4,8},{6,10},{8,12},{10,14},{12,16},{14,18},{16,20},{1... | collective-permute-start | bytes 1572872 | tf_op jit(solution)/shard_map/ppermute | solution.py:29
  286.0 7.8 %collective-permute-start.26 = (bf16[4,8]{1,0:T(4,128)(2,1)}, bf16[4,8]{1,0:T(4,128)(2,1)S(1)}, u32[]{:S(2)}, u32[]{:S(2)}) collective-permute-start(bf16[4,8]{1,0:T(4,128)(2,1)} %get-tuple-element.254), channel_id=1, source_target_pairs={{0,30},{2,0},{4,2},{6,4},{8,6},{10,8},{12,10},{14,12},{16,14},{18,... | collective-permute-start | bytes 200 | tf_op jit(solution)/shard_map/ppermute | solution.py:29
  292.5 34.3 %copy-start.5 = (f32[4,8,64,128]{3,2,1,0:T(8,128)}, f32[4,8,64,128]{3,2,1,0:T(8,128)S(1)}, u32[]{:S(2)}) copy-start(f32[4,8,64,128]{3,2,1,0:T(8,128)S(1)} %get-tuple-element.265) | copy-start | bytes 3145732
  292.5 34.3 %collective-permute-start.21 = (bf16[4,8,64,128]{3,2,1,0:T(8,128)(2,1)}, bf16[4,8,64,128]{3,2,1,0:T(8,128)(2,1)S(1)}, u32[]{:S(2)}, u32[]{:S(2)}) collective-permute-start(bf16[4,8,64,128]{3,2,1,0:T(8,128)(2,1)} %get-tuple-element.264), channel_id=1, source_target_pairs={{0,8},{2,10},{4,12},{6,14},{8,16},{10,18},{12,20},{14,22},{16,24},... | collective-permute-start | bytes 1572872 | tf_op jit(solution)/shard_map/ppermute | solution.py:29
  294.5 4.5 collective-permute-start.28
  299.0 13.0 %collective-permute-start.30 = (bf16[4,8]{1,0:T(4,128)(2,1)S(1)}, bf16[4,8]{1,0:T(4,128)(2,1)S(1)}, u32[]{:S(2)}, u32[]{:S(2)}) collective-permute-start(bf16[4,8]{1,0:T(4,128)(2,1)S(1)} %get-tuple-element.248), channel_id=1, source_target_pairs={{0,24},{2,26},{4,28},{6,30},{8,0},{10,2},{12,4},{14,6},{16,8},{18,... | collective-permute-start | bytes 200 | tf_op jit(solution)/shard_map/ppermute | solution.py:29
  328.5 23.8 %collective-permute-start.23 = (bf16[4,8,64,128]{3,2,1,0:T(8,128)(2,1)}, bf16[4,8,64,128]{3,2,1,0:T(8,128)(2,1)}, u32[]{:S(2)}, u32[]{:S(2)}) collective-permute-start(bf16[4,8,64,128]{3,2,1,0:T(8,128)(2,1)} %fusion.147), channel_id=1, source_target_pairs={{0,16},{2,18},{4,20},{6,22},{8,24},{10,26},{12,28},{14,30},{16,0},... | collective-permute-start | bytes 1572872 | tf_op jit(solution)/shard_map/ppermute | solution.py:29
  344.0 20.6 %copy-start = (bf16[2048,512]{0,1:T(8,128)(2,1)S(1)}, bf16[2048,512]{0,1:T(8,128)(2,1)}, u32[]{:S(2)}) copy-start(bf16[2048,512]{0,1:T(8,128)(2,1)} %all-gather.3.cloned.1.call-done) | copy-start | bytes 6291460
  360.1 45.1 %collective-permute-start.25 = (bf16[4,8,64,128]{3,2,1,0:T(8,128)(2,1)}, bf16[4,8,64,128]{3,2,1,0:T(8,128)(2,1)}, u32[]{:S(2)}, u32[]{:S(2)}) collective-permute-start(bf16[4,8,64,128]{3,2,1,0:T(8,128)(2,1)} %get-tuple-element.334), channel_id=1, source_target_pairs={{0,30},{2,0},{4,2},{6,4},{8,6},{10,8},{12,10},{14,12},{16,14},{18,... | collective-permute-start | bytes 1572872 | tf_op jit(solution)/shard_map/ppermute | solution.py:29
  364.6 18.6 %copy-start.51 = (s32[1,64]{1,0:T(1,128)S(1)}, s32[1,64]{1,0:T(1,128)}, u32[]{:S(2)}) copy-start(s32[1,64]{1,0:T(1,128)} %get-tuple-element.324) | copy-start | bytes 772
  383.1 20.0 %copy-start.50 = (f32[4,8,64]{2,1,0:T(8,128)S(1)}, f32[4,8,64]{2,1,0:T(8,128)}, u32[]{:S(2)}) copy-start(f32[4,8,64]{2,1,0:T(8,128)} %copy.315) | copy-start | bytes 24580
  383.1 22.1 %copy-start.35 = (f32[4,8]{1,0:T(4,128)S(1)}, f32[4,8]{1,0:T(4,128)}, u32[]{:S(2)}) copy-start(f32[4,8]{1,0:T(4,128)} %get-tuple-element.255) | copy-start | bytes 388
  398.2 22.8 %copy-start.6 = (f32[4,8,64,128]{3,2,1,0:T(8,128)S(1)}, f32[4,8,64,128]{3,2,1,0:T(8,128)}, u32[]{:S(2)}) copy-start(f32[4,8,64,128]{3,2,1,0:T(8,128)} %get-tuple-element.335) | copy-start | bytes 3145732
  398.2 22.8 %copy-start.44 = (f32[4,8]{1,0:T(4,128)S(1)}, f32[4,8]{1,0:T(4,128)}, u32[]{:S(2)}) copy-start(f32[4,8]{1,0:T(4,128)} %copy-done.43) | copy-start | bytes 388
  398.2 28.7 %copy-start.19 = (bf16[8,4,8,128]{3,2,1,0:T(8,128)(2,1)S(1)}, bf16[8,4,8,128]{3,2,1,0:T(8,128)(2,1)}, u32[]{:S(2)}) copy-start(bf16[8,4,8,128]{3,2,1,0:T(8,128)(2,1)} %get-tuple-element.338) | copy-start | bytes 196612
  399.7 28.0 %copy-start.18 = (bf16[8,4,8,128]{3,2,1,0:T(8,128)(2,1)S(1)}, bf16[8,4,8,128]{3,2,1,0:T(8,128)(2,1)}, u32[]{:S(2)}) copy-start(bf16[8,4,8,128]{3,2,1,0:T(8,128)(2,1)} %get-tuple-element.310) | copy-start | bytes 196612
  403.2 34.0 %copy-start.40 = (f32[4,8]{1,0:T(4,128)S(1)}, f32[4,8]{1,0:T(4,128)}, u32[]{:S(2)}) copy-start(f32[4,8]{1,0:T(4,128)} %copy-done.39) | copy-start | bytes 388
  405.2 34.2 %copy-start.26 = (f32[64,4,8]{0,2,1:T(8,128)S(1)}, f32[64,4,8]{0,2,1:T(8,128)}, u32[]{:S(2)}) copy-start(f32[64,4,8]{0,2,1:T(8,128)} %copy-done.25) | copy-start | bytes 24580
  406.8 14.1 %collective-permute-start.27 = (bf16[4,8,64,128]{3,2,1,0:T(8,128)(2,1)S(1)}, bf16[4,8,64,128]{3,2,1,0:T(8,128)(2,1)S(1)}, u32[]{:S(2)}, u32[]{:S(2)}) collective-permute-start(bf16[4,8,64,128]{3,2,1,0:T(8,128)(2,1)S(1)} %fusion.148), channel_id=1, source_target_pairs={{0,28},{2,30},{4,0},{6,2},{8,4},{10,6},{12,8},{14,10},{16,12},{18,... | collective-permute-start | bytes 1572872 | tf_op jit(solution)/shard_map/ppermute | solution.py:29
  408.6 30.9 %copy-start.27 = (bf16[4,64,128]{2,1,0:T(8,128)(2,1)S(1)}, bf16[4,64,128]{2,1,0:T(8,128)(2,1)}, u32[]{:S(2)}) copy-start(bf16[4,64,128]{2,1,0:T(8,128)(2,1)} %convolution_convert_fusion.6) | copy-start | bytes 196612
  423.6 12.7 %collective-permute-start.29 = (bf16[4,8,64,128]{3,2,1,0:T(8,128)(2,1)}, bf16[4,8,64,128]{3,2,1,0:T(8,128)(2,1)S(1)}, u32[]{:S(2)}, u32[]{:S(2)}) collective-permute-start(bf16[4,8,64,128]{3,2,1,0:T(8,128)(2,1)} %get-tuple-element.252), channel_id=1, source_target_pairs={{0,24},{2,26},{4,28},{6,30},{8,0},{10,2},{12,4},{14,6},{16,8},{18,... | collective-permute-start | bytes 1572872 | tf_op jit(solution)/shard_map/ppermute | solution.py:29
  431.3 47.3 %copy-start.17 = (bf16[64,4,128]{2,1,0:T(4,128)(2,1)S(1)}, bf16[64,4,128]{2,1,0:T(4,128)(2,1)}, u32[]{:S(2)}) copy-start(bf16[64,4,128]{2,1,0:T(4,128)(2,1)} %copy-done.16) | copy-start | bytes 196612
  439.4 52.0 %copy-start.2 = (f32[4,8,64,128]{3,2,1,0:T(8,128)S(1)}, f32[4,8,64,128]{3,2,1,0:T(8,128)}, u32[]{:S(2)}) copy-start(f32[4,8,64,128]{3,2,1,0:T(8,128)} %copy-done.1) | copy-start | bytes 3145732
  439.4 34.1 %collective-permute-start.31 = (bf16[4,8,64,128]{3,2,1,0:T(8,128)(2,1)}, bf16[4,8,64,128]{3,2,1,0:T(8,128)(2,1)}, u32[]{:S(2)}, u32[]{:S(2)}) collective-permute-start(bf16[4,8,64,128]{3,2,1,0:T(8,128)(2,1)} %fusion.149), channel_id=1, source_target_pairs={{0,16},{2,18},{4,20},{6,22},{8,24},{10,26},{12,28},{14,30},{16,0},... | collective-permute-start | bytes 1572872 | tf_op jit(solution)/shard_map/ppermute | solution.py:29
  443.2 32.6 %copy-start.29 = (bf16[1,64,4,128]{3,1,2,0:T(8,128)(2,1)S(1)}, bf16[1,64,4,128]{3,1,2,0:T(8,128)(2,1)}, u32[]{:S(2)}) copy-start(bf16[1,64,4,128]{3,1,2,0:T(8,128)(2,1)} %fusion.123) | copy-start | bytes 196612
  444.6 34.0 %copy-start.22 = (bf16[64,4,8,64]{3,0,2,1:T(8,128)(2,1)S(1)}, bf16[64,4,8,64]{3,0,2,1:T(8,128)(2,1)}, u32[]{:S(2)}) copy-start(bf16[64,4,8,64]{3,0,2,1:T(8,128)(2,1)} %fusion.109) | copy-start | bytes 786436
  446.6 30.0 %collective-permute-start.33 = (bf16[4,8,64,128]{3,2,1,0:T(8,128)(2,1)}, bf16[4,8,64,128]{3,2,1,0:T(8,128)(2,1)S(1)}, u32[]{:S(2)}, u32[]{:S(2)}) collective-permute-start(bf16[4,8,64,128]{3,2,1,0:T(8,128)(2,1)} %get-tuple-element.258), channel_id=1, source_target_pairs={{0,2},{2,4},{4,6},{6,8},{8,10},{10,12},{12,14},{14,16},{16,18},{18... | collective-permute-start | bytes 1572872 | tf_op jit(solution)/shard_map/ppermute | solution.py:29
  475.4 16.0 %collective-permute-start.32 = (bf16[4,8,64,128]{3,2,1,0:T(8,128)(2,1)S(1)}, bf16[4,8,64,128]{3,2,1,0:T(8,128)(2,1)S(1)}, u32[]{:S(2)}, u32[]{:S(2)}) collective-permute-start(bf16[4,8,64,128]{3,2,1,0:T(8,128)(2,1)S(1)} %fusion.132), channel_id=1, source_target_pairs={{0,30},{2,0},{4,2},{6,4},{8,6},{10,8},{12,10},{14,12},{16,14},{18,... | collective-permute-start | bytes 1572872 | tf_op jit(solution)/shard_map/ppermute | solution.py:29
  (27 other events, 219.7 us)
Sparse Core Ops, SparseCore 0:
  11.3 99.4 all-gather.2
  125.7 101.6 all-gather.4
where the time goes:
time: 515 us; the launch traced here: 506 us
  waiting for transfers between devices  175 us (34%)
  starting transfers between devices  95.1 us (18%)
  matrix products  84.5 us (16%)
  other arithmetic  68.4 us (13%)
  local copies, waits for them, and re-layouts  57.8 us (11%)
  between operations  21.6 us (4%)
    ppermute x34, waiting for transfers between devices, shifted(): return lax.ppermute(value, axis, pairs)  175 us
    ppermute x34, starting transfers between devices, shifted(): return lax.ppermute(value, axis, pairs)  95 us
    convert_element_type x29, other arithmetic, short(): return part.astype(jnp.bfloat16) if part.dtype == jnp.float32 else part  29.6 us
    dot_general x2, matrix products, backward_update(): jnp.einsum('gkrs,sgd->rgkd', score_grad, key_piece, preferred_element_typ...  16.7 us
    dot_general x6, matrix products, stretch_parts(): jnp.einsum('gkts,sgkp->tgkp', mixing, input_rows, preferred_element_type=...  13.6 us
    dot_general x6, matrix products, stretch_parts(): jnp.einsum('sgkp,sgn->gkpn', weighted, write_rows, preferred_element_type...  10.7 us
    unnamed x107, local copies, waits for them, and re-layouts  10.6 us
  transfers between devices with their start and end apart: 36, of which 25 were waited for; matrix products, arithmetic and copies ran while one was open for 36% of the time, Pallas kernels for 0%

commit v1 on v0

v1 whole, which is shorter than its diff:
```python
import jax
import jax.numpy as jnp
from jax import lax
from jax.experimental import pallas as pl
from jax.experimental.pallas import tpu as pltpu
from jax.sharding import PartitionSpec as P

HEAD_CH = 64
NSTATE = 128
AHD = 128
STRETCH = 64
EXTRA = 16
NORM_EPS = 1e-05
NEG_FILL = -1e30
KEY_CHUNK = 512
F32 = jnp.float32
BF16 = jnp.bfloat16
VMEM_BYTES = 48 * 1024 * 1024


def mm(a, b):
    return lax.dot_general(a, b, (((1,), (0,)), ((), ())), preferred_element_type=F32)


def mm_nt(a, b):
    return lax.dot_general(a, b, (((1,), (1,)), ((), ())), preferred_element_type=F32)


def split3(v):
    hi = v.astype(BF16)
    rest = v - hi.astype(F32)
    mid = rest.astype(BF16)
    low = (rest - mid.astype(F32)).astype(BF16)
    return hi, mid, low


def pair_spread(cols, k):
    rows = cols.shape[0]
    lane = lax.broadcasted_iota(jnp.int32, (rows, 128), 1)
    even = jnp.broadcast_to(cols[:, 2 * k : 2 * k + 1], (rows, 128))
    odd = jnp.broadcast_to(cols[:, 2 * k + 1 : 2 * k + 2], (rows, 128))
    return jnp.where(lane < HEAD_CH, even, odd)


def spread(cols, heads):
    return jnp.concatenate([pair_spread(cols, k) for k in range(heads // 2)], axis=1)


def call(fn, outs, args, smem=(), scratch=(), flops=0, nbytes=0):
    specs = [
        pl.BlockSpec(memory_space=pltpu.SMEM if i in smem else pltpu.VMEM)
        for i in range(len(args))
    ]
    return pl.pallas_call(
        fn,
        out_shape=tuple(jax.ShapeDtypeStruct(s, d) for s, d in outs),
        in_specs=specs,
        out_specs=tuple(pl.BlockSpec(memory_space=pltpu.VMEM) for _ in outs),
        scratch_shapes=list(scratch),
        compiler_params=pltpu.CompilerParams(vmem_limit_bytes=VMEM_BYTES),
        cost_estimate=pl.CostEstimate(flops=flops, bytes_accessed=nbytes, transcendentals=0),
    )(*args)


def pack_forward(me, x, w, r, step, group):
    rows, chans = x.shape[0], x.shape[1] // group
    heads = step.shape[1] // group
    width = chans + 2 * NSTATE + 128

    def kernel(me_ref, x_ref, w_ref, r_ref, step_ref, *outs):
        parts = split3(step_ref[...])
        row = lax.broadcasted_iota(jnp.int32, (heads * group, 128), 0)
        col = lax.broadcasted_iota(jnp.int32, (heads * group, 128), 1)
        for m in range(group):
            dest = me_ref[0] ^ m
            out = outs[m]
            out[:, 0:chans] = x_ref[:, pl.ds(pl.multiple_of(dest * chans, 128), chans)]
            at = pl.ds(pl.multiple_of(dest * NSTATE, 128), NSTATE)
            out[:, chans : chans + NSTATE] = w_ref[:, at]
            out[:, chans + NSTATE : chans + 2 * NSTATE] = r_ref[:, at]
            total = jnp.zeros((rows, 128), F32)
            for i in range(3):
                pick = (row - dest * heads == col - i * heads) & (col >= i * heads)
                pick = pick & (col < (i + 1) * heads)
                total = total + mm(parts[i], jnp.where(pick, 1.0, 0.0).astype(BF16))
            out[:, chans + 2 * NSTATE : width] = total.astype(BF16)

    return call(
        kernel, [((rows, width), BF16)] * group, (me, x, w, r, step), smem=(0,), nbytes=2 * x.size * 3
    )


def pack_gate(me, gate, grad, group):
    rows, chans = gate.shape[0], gate.shape[1] // group

    def kernel(me_ref, gate_ref, grad_ref, *outs):
        for m in range(group):
            at = pl.ds(pl.multiple_of((me_ref[0] ^ m) * chans, 128), chans)
            outs[m][:, 0:chans] = gate_ref[:, at]
            outs[m][:, chans : 2 * chans] = grad_ref[:, at]

    return call(
        kernel, [((rows, 2 * chans), BF16)] * group, (me, gate, grad), smem=(0,), nbytes=8 * gate.size
    )


def unpack(me, pieces, widths):
    group, rows = len(pieces), pieces[0].shape[0]

    def kernel(me_ref, *refs):
        outs = refs[group:]
        for m in range(group):
            start = 0
            for out, width in zip(outs, widths):
                at = pl.ds(pl.multiple_of((me_ref[0] ^ m) * width, 128), width)
                out[:, at] = refs[m][:, start : start + width]
                start += width

    return call(
        kernel,
        [((rows, group * width), BF16) for width in widths],
        (me, *pieces),
        smem=(0,),
        nbytes=4 * rows * group * sum(widths),
    )


def row_blocks(group):
    for half in range(2):
        for m in range(group):
            yield half, m, (half * group + m) * STRETCH


def outgoing_state(pieces, info, info_t, small, chans):
    group = len(pieces)
    rows = 2 * group * STRETCH
    heads = chans // HEAD_CH

    def kernel(*refs):
        ins = refs[:group]
        info_ref, info_t_ref, small_ref = refs[group : group + 3]
        msg, x_out, w_out, r_out, cum_out, rate_out, tail_out, step_buf = refs[group + 3 :]
        for half, m, at in row_blocks(group):
            src = slice(half * STRETCH, (half + 1) * STRETCH)
            x_out[at : at + STRETCH, :] = ins[m][src, 0:chans]
            w_out[at : at + STRETCH, :] = ins[m][src, chans : chans + NSTATE]
            r_out[at : at + STRETCH, :] = ins[m][src, chans + NSTATE : chans + 2 * NSTATE]
            step_buf[at : at + STRETCH, :] = ins[m][src, chans + 2 * NSTATE :]
        row = lax.broadcasted_iota(jnp.int32, (128, 128), 0)
        col = lax.broadcasted_iota(jnp.int32, (128, 128), 1)
        pick = ((row == col) | (row == col + heads) | (row == col + 2 * heads)) & (col < heads)
        step = mm(step_buf[...], jnp.where(pick, 1.0, 0.0).astype(BF16))
        rate = jnp.maximum(step, 0.0) + jnp.log1p(jnp.exp(-jnp.abs(step)))
        rate_out[...] = rate
        amount = rate * small_ref[0:1, :]
        pos_row = info_t_ref[0:1, :]
        same = (pos_row <= info_ref[:, 0:1]) & (pos_row >= info_ref[:, 1:2])
        same = jnp.where(same, 1.0, 0.0).astype(BF16)
        hi, mid, low = split3(amount)
        cum = mm(same, hi) + mm(same, mid) + mm(same, low)
        cum_out[...] = cum
        totals = [
            jnp.sum(amount * info_ref[:, 2 + q : 3 + q], axis=0, keepdims=True) for q in range(2)
        ]
        tail = jnp.zeros_like(cum)
        for q in range(2):
            tail = tail + info_ref[:, 2 + q : 3 + q] * jnp.exp(jnp.minimum(totals[q] - cum, 0.0))
        tail_out[...] = tail
        scale = rate * tail
        w_t = w_out[...].astype(F32).T
        w_q = [(w_t * info_t_ref[2 + q : 3 + q, :]).astype(BF16) for q in range(2)]
        sub = lax.broadcasted_iota(jnp.int32, (EXTRA, 128), 0)
        for k in range(heads // 2):
            lanes = slice(128 * k, 128 * (k + 1))
            xw = (x_out[:, lanes].astype(F32) * pair_spread(scale, k)).astype(BF16)
            for q in range(2):
                msg[q, 0:NSTATE, lanes] = mm(w_q[q], xw).astype(BF16)
                wide = pair_spread(jnp.broadcast_to(totals[q], (EXTRA, 128)), k)
                hi, mid, low = split3(wide)
                hi, mid, low = hi.astype(F32), mid.astype(F32), low.astype(F32)
                msg[q, NSTATE:, lanes] = jnp.where(
                    sub == 0, hi, jnp.where(sub == 1, mid, low)
                ).astype(BF16)

    return call(
        kernel,
        [
            ((2, NSTATE + EXTRA, chans), BF16),
            ((rows, chans), BF16),
            ((rows, NSTATE), BF16),
            ((rows, NSTATE), BF16),
            ((rows, 128), F32),
            ((rows, 128), F32),
            ((rows, 128), F32),
        ],
        (*pieces, info, info_t, small),
        scratch=[pltpu.VMEM((rows, 128), BF16)],
        flops=4 * rows * NSTATE * chans,
        nbytes=6 * rows * chans,
    )


def intra_forward(x, w, r, cum, rate, info, info_t, chan):
    rows, chans = x.shape
    heads = chans // HEAD_CH
    mid = rows // 2

    def kernel(x_ref, w_ref, r_ref, cum_ref, rate_ref, info_ref, info_t_ref, chan_ref, y_ref, gm):
        cum_t = cum_ref[...].T
        lane = lax.broadcasted_iota(jnp.int32, (mid, 128), 1)
        spans = ((0, mid, mid), (mid, mid, rows))
        for start, count, depth in spans:
            at = slice(start, start + count)
            pos_row = info_t_ref[0:1, 0:depth]
            same = (pos_row <= info_ref[at, 0:1]) & (pos_row >= info_ref[at, 1:2])
            gm[at, 0:depth] = jnp.where(same, mm_nt(r_ref[at, :], w_ref[0:depth, :]), 0.0)
        for k in range(heads // 2):
            lanes = slice(128 * k, 128 * (k + 1))
            xf = x_ref[:, lanes].astype(F32)
            xr = (xf * pair_spread(rate_ref[...], k)).astype(BF16)
            for start, count, depth in spans:
                at = slice(start, start + count)
                both = []
                for h in (2 * k, 2 * k + 1):
                    gap = cum_ref[at, h : h + 1] - cum_t[h : h + 1, 0:depth]
                    mix = (jnp.exp(jnp.minimum(gap, 0.0)) * gm[at, 0:depth]).astype(BF16)
                    both.append(mm(mix, xr[0:depth]))
                y_ref[at, lanes] = jnp.where(lane < HEAD_CH, both[0], both[1]) + (
                    chan_ref[0:1, lanes] * xf[at]
                )

    return call(
        kernel,
        [((rows, chans), F32)],
        (x, w, r, cum, rate, info, info_t, chan),
        scratch=[pltpu.VMEM((rows, rows), F32)],
        flops=4 * rows * rows * chans,
        nbytes=8 * rows * chans,
    )[0]


def gather_states(refs, weight, store):
    for q in range(2):
        total = None
        index = 0
        for ref in refs:
            for k in range(ref.shape[0]):
                for c in range(2):
                    term = weight(q, index) * ref[k, c, 0:NSTATE, :].astype(F32)
                    total = term if total is None else total + term
                    index += 1
        store(q, total)


def mixed_rows(msgs, y, r, cum, gates, info, chan, before_in, ends, enter_mask, own_mask, own_end):
    rows, chans = y.shape
    heads = chans // HEAD_CH
    group = len(gates)
    n_msg = len(msgs)
    classes = ends.shape[0]

    def kernel(*refs):
        msg_refs = refs[:n_msg]
        gate_refs = refs[n_msg : n_msg + group]
        (
            y_ref, r_ref, cum_ref, info_ref, chan_ref,
            before_ref, ends_ref, own_ref, own_end_ref, mask_ref,
            gated_ref, sums_ref, state_ref, enter_ref, leave_ref,
            tot, inner, cols,
        ) = refs[n_msg + group :]
        index = 0
        for ref in msg_refs:
            for k in range(ref.shape[0]):
                for c in range(2):
                    part = ref[k, c, NSTATE : NSTATE + EXTRA, :].astype(F32)
                    tot[index : index + 1, :] = part[0:1] + part[1:2] + part[2:3]
                    index += 1
        exact = lax.Precision.HIGHEST
        totals = tot[...]
        enter_ref[...] = jnp.dot(before_ref[...], totals, precision=exact, preferred_element_type=F32)
        leave_all = jnp.dot(ends_ref[...], totals, precision=exact, preferred_element_type=F32)
        own_in = jnp.dot(own_ref[...], totals, precision=exact, preferred_element_type=F32)
        leave_ref[...] = jnp.dot(
            own_end_ref[...], totals, precision=exact, preferred_element_type=F32
        )

        def weight(q, c):
            gap = own_in[q : q + 1] - leave_all[c : c + 1]
            return jnp.exp(jnp.minimum(gap, 0.0)) * mask_ref[q, c]

        def store(q, value):
            state_ref[q * NSTATE : (q + 1) * NSTATE, :] = value.astype(BF16)

        gather_states(msg_refs, weight, store)
        reads = r_ref[...].astype(F32)
        both = jnp.concatenate(
            [(reads * info_ref[:, 4:5]).astype(BF16), (reads * info_ref[:, 5:6]).astype(BF16)], axis=1
        )
        inner[...] = mm(both, state_ref[...])
        lane = lax.broadcasted_iota(jnp.int32, (STRETCH, 128), 1)
        for half, m, at in row_blocks(group):
            here = slice(at, at + STRETCH)
            src = slice(half * STRETCH, (half + 1) * STRETCH)
            mixed = y_ref[here, :] + spread(jnp.exp(cum_ref[here, :]), heads) * inner[here, :]
            gate = gate_refs[m][src, 0:chans].astype(F32)
            gated = mixed * (gate / (1.0 + jnp.exp(-gate)))
            gated_ref[here, :] = gated
            grad = gate_refs[m][src, chans : 2 * chans].astype(F32) * chan_ref[1:2, :]
            square = jnp.sum(gated * gated, axis=1, keepdims=True)
            cross = jnp.sum(grad * gated, axis=1, keepdims=True)
            cols[here, :] = jnp.where(lane == 0, square, jnp.where(lane == 1, cross, 0.0))
        sums_ref[...] = cols[...].T[0:8, :]

    args = (
        *msgs, *gates, y, r, cum, info, chan, before_in, ends, own_mask, own_end, enter_mask
    )
    return call(
        kernel,
        [
            ((rows, chans), F32),
            ((8, rows), F32),
            ((2 * NSTATE, chans), BF16),
            ((classes, chans), F32),
            ((8, chans), F32),
        ],
        args,
        smem=(len(args) - 1,),
        scratch=[
            pltpu.VMEM((classes, chans), F32),
            pltpu.VMEM((rows, chans), F32),
            pltpu.VMEM((rows, 128), F32),
        ],
        flops=4 * rows * 2 * NSTATE * chans,
        nbytes=16 * rows * chans,
    )


def mixed_cotangent(sums, gated, gates, r, cum, info_t, chan, total_chans):
    rows, chans = gated.shape
    heads = chans // HEAD_CH
    group = len(gates)

    def kernel(*refs):
        gate_refs = refs[:group]
        sums_refs, refs = refs[group : 2 * group], refs[2 * group :]
        gated_ref, r_ref, cum_ref, info_t_ref, chan_ref, touch_ref, dmix_ref, lift_ref = refs[:8]
        outs = refs[8 : 8 + group]
        cols = refs[8 + group]
        parts = [ref[...] for ref in sums_refs]
        both = jnp.concatenate(parts + [jnp.zeros((128 - 8 * group, rows), F32)], axis=0)
        cols[...] = both.T
        for half, m, at in row_blocks(group):
            here = slice(at, at + STRETCH)
            src = slice(half * STRETCH, (half + 1) * STRETCH)
            square = cross = 0.0
            for peer in range(group):
                start = (half * group + (m ^ peer)) * STRETCH
                there = slice(start, start + STRETCH)
                square = square + cols[there, 8 * peer : 8 * peer + 1]
                cross = cross + cols[there, 8 * peer + 1 : 8 * peer + 2]
            inv = lax.rsqrt(square / total_chans + NORM_EPS)
            pull = inv * inv * inv * (cross / total_chans)
            gated = gated_ref[here, :]
            gain = chan_ref[1:2, :]
            outs[m][src, :] = (gated * inv * gain).astype(BF16)
            gate = gate_refs[m][src, 0:chans].astype(F32)
            grad = gate_refs[m][src, chans : 2 * chans].astype(F32) * gain
            dmix = (inv * grad - gated * pull) * (gate / (1.0 + jnp.exp(-gate)))
            dmix_ref[here, :] = dmix
            lift_ref[here, :] = (dmix * spread(jnp.exp(cum_ref[here, :]), heads)).astype(BF16)
        r_t = r_ref[...].astype(F32).T
        for q in range(2):
            left = (r_t * info_t_ref[4 + q : 5 + q, :]).astype(BF16)
            touch_ref[q] = mm(left, lift_ref[...]).astype(BF16)

    return call(
        kernel,
        [
            ((2, NSTATE, chans), BF16),
            ((rows, chans), F32),
            ((rows, chans), BF16),
            *[((2 * STRETCH, chans), BF16)] * group,
        ],
        (*gates, *sums, gated, r, cum, info_t, chan),
        scratch=[pltpu.VMEM((rows, 128), F32)],
        flops=4 * rows * NSTATE * chans,
        nbytes=16 * rows * chans,
    )


def intra_backward(x, w, r, cum, rate, dmix, lift, state, info, info_t):
    rows, chans = x.shape
    heads = chans // HEAD_CH
    mid = rows // 2

    def kernel(
        x_ref, w_ref, r_ref, cum_ref, rate_ref, dmix_ref, lift_ref, state_ref, info_ref, info_t_ref,
        dx_ref, dw_ref, dr_ref, gm, dgm,
    ):
        cum_t = cum_ref[...].T
        lane = lax.broadcasted_iota(jnp.int32, (rows, 128), 1)
        lane_mid = lax.broadcasted_iota(jnp.int32, (mid, 128), 1)
        spans = ((0, 0), (mid, mid))

        def same_of(start, later):
            pos = info_ref[start : start + mid, 0:1]
            return (pos <= info_t_ref[0:1, later:]) & (pos >= info_t_ref[1:2, later:])

        for start, later in spans:
            at = slice(start, start + mid)
            product = mm_nt(w_ref[at, :], r_ref[later:, :])
            gm[at, later:] = jnp.where(same_of(start, later), product, 0.0)
        for k in range(heads // 2):
            lanes = slice(128 * k, 128 * (k + 1))
            xr = x_ref[:, lanes].astype(F32) * pair_spread(rate_ref[...], k)
            parts = (
                jnp.where(lane < HEAD_CH, xr, 0.0).astype(BF16),
                jnp.where(lane < HEAD_CH, 0.0, xr).astype(BF16),
            )
            grads = dmix_ref[:, lanes].astype(BF16)
            for start, later in spans:
                at = slice(start, start + mid)
                both = []
                for i in range(2):
                    h = 2 * k + i
                    gap = cum_t[h : h + 1, later:] - cum_ref[at, h : h + 1]
                    fade = jnp.exp(jnp.minimum(gap, 0.0))
                    mix = (fade * gm[at, later:]).astype(BF16)
                    both.append(mm(mix, grads[later:]))
                    change = fade * mm_nt(parts[i][at], grads[later:])
                    if h == 0:
                        dgm[at, later:] = change
                    else:
                        dgm[at, later:] += change
                dx_ref[at, lanes] = jnp.where(lane_mid < HEAD_CH, both[0], both[1])
        carried = mm_nt(lift_ref[...], state_ref[0:NSTATE, :]) * info_ref[:, 4:5]
        carried = carried + mm_nt(lift_ref[...], state_ref[NSTATE:, :]) * info_ref[:, 5:6]
        dr_ref[...] = carried
        for start, later in spans:
            at = slice(start, start + mid)
            change = jnp.where(same_of(start, later), dgm[at, later:], 0.0)
            dw_ref[at, :] = mm(change.astype(BF16), r_ref[later:, :])
            dr_ref[later:, :] += mm(change.T.astype(BF16), w_ref[at, :])

    return call(
        kernel,
        [((rows, chans), F32), ((rows, NSTATE), F32), ((rows, NSTATE), F32)],
        (x, w, r, cum, rate, dmix, lift, state, info, info_t),
        scratch=[pltpu.VMEM((rows, rows), F32), pltpu.VMEM((rows, rows), F32)],
        flops=8 * rows * rows * chans,
        nbytes=16 * rows * chans,
    )


def final_grads(msgs, x, w, rate, tail, dx, dw, dr, dmix, info, chan, enter, leave, leave_mask):
    rows, chans = x.shape
    heads = chans // HEAD_CH
    group = rows // (2 * STRETCH)
    n_msg = len(msgs)
    width = chans + 2 * NSTATE

    def kernel(*refs):
        msg_refs = refs[:n_msg]
        (
            x_ref, w_ref, rate_ref, tail_ref, dx_ref, dw_ref, dr_ref, dmix_ref, info_ref, chan_ref,
            enter_ref, leave_ref, mask_ref,
        ) = refs[n_msg : n_msg + 13]
        outs = refs[n_msg + 13 : n_msg + 13 + group]
        after, inner, xw = refs[n_msg + 13 + group :]

        def weight(q, c):
            gap = enter_ref[c : c + 1, :] - leave_ref[q : q + 1, :]
            return jnp.exp(jnp.minimum(gap, 0.0)) * mask_ref[q, c]

        def store(q, value):
            after[q * NSTATE : (q + 1) * NSTATE, :] = value.astype(BF16)

        gather_states(msg_refs, weight, store)
        writes = w_ref[...].astype(F32)
        both = jnp.concatenate(
            [(writes * info_ref[:, 2:3]).astype(BF16), (writes * info_ref[:, 3:4]).astype(BF16)],
            axis=1,
        )
        inner[...] = mm(both, after[...])
        for half, m, at in row_blocks(group):
            here = slice(at, at + STRETCH)
            dst = slice(half * STRETCH, (half + 1) * STRETCH)
            rates = spread(rate_ref[here, :], heads)
            tails = spread(tail_ref[here, :], heads)
            xw[here, :] = (x_ref[here, :].astype(F32) * (rates * tails)).astype(BF16)
            change = rates * (dx_ref[here, :] + tails * inner[here, :])
            change = change + chan_ref[0:1, :] * dmix_ref[here, :]
            outs[m][dst, 0:chans] = change.astype(BF16)
            outs[m][dst, chans + NSTATE :] = dr_ref[here, :].astype(BF16)
        change = dw_ref[...] + mm_nt(xw[...], after[0:NSTATE, :]) * info_ref[:, 2:3]
        change = change + mm_nt(xw[...], after[NSTATE:, :]) * info_ref[:, 3:4]
        for half, m, at in row_blocks(group):
            dst = slice(half * STRETCH, (half + 1) * STRETCH)
            outs[m][dst, chans : chans + NSTATE] = change[at : at + STRETCH].astype(BF16)

    args = (
        *msgs, x, w, rate, tail, dx, dw, dr, dmix, info, chan, enter, leave, leave_mask
    )
    return call(
        kernel,
        [((2 * STRETCH, width), BF16)] * group,
        args,
        smem=(len(args) - 1,),
        scratch=[
            pltpu.VMEM((2 * NSTATE, chans), BF16),
            pltpu.VMEM((rows, chans), F32),
            pltpu.VMEM((rows, chans), BF16),
        ],
        flops=8 * rows * NSTATE * chans,
        nbytes=16 * rows * chans,
    )


def attention(blocks, own_blocks, pieces, queries, grads, kv_heads):
    rows = queries.shape[0]
    per_kv = queries.shape[1] // AHD // kv_heads
    group, units = len(pieces), pieces[0].shape[0]
    tokens = group * units * rows
    half_width = kv_heads * AHD
    scale = AHD ** (-0.5)
    chunk = min(KEY_CHUNK, tokens)
    tall = per_kv * STRETCH

    def kernel(*refs):
        blocks_ref, own_ref = refs[:2]
        piece_refs = refs[2 : 2 + group]
        q_ref, g_ref, out_ref, dq_ref, kv, scores = refs[2 + group :]
        for m in range(group):
            for u in range(units):
                for half in range(2):
                    at = pl.ds(pl.multiple_of(blocks_ref[half, m * units + u] * STRETCH, 64), STRETCH)
                    kv[at, :] = piece_refs[m][u, half * STRETCH : (half + 1) * STRETCH, :]
        offset = lax.broadcasted_iota(jnp.int32, (tall, chunk), 0) % STRETCH
        column = lax.broadcasted_iota(jnp.int32, (tall, chunk), 1)
        for half in range(2):
            block = own_ref[half]
            src = slice(half * STRETCH, (half + 1) * STRETCH)
            steps = (block * STRETCH) // chunk + 1
            reach = offset + block * STRETCH
            for g in range(kv_heads):
                k_at = slice(g * AHD, (g + 1) * AHD)
                v_at = slice(half_width + g * AHD, half_width + (g + 1) * AHD)
                heads = [slice((g * per_kv + i) * AHD, (g * per_kv + i + 1) * AHD) for i in range(per_kv)]
                query = jnp.concatenate([q_ref[src, at] for at in heads], axis=0)
                grad = jnp.concatenate([g_ref[src, at] for at in heads], axis=0)

                def keys_of(c):
                    return pl.ds(pl.multiple_of(c * chunk, chunk), chunk)

                def first(c, peak):
                    value = mm_nt(query, kv[keys_of(c), k_at]) * scale
                    value = jnp.where(column + c * chunk <= reach, value, NEG_FILL)
                    scores[c] = value
                    return jnp.maximum(peak, jnp.max(value, axis=1, keepdims=True))

                peak = lax.fori_loop(0, steps, first, jnp.full((tall, 1), NEG_FILL, F32))

                def second(c, carry):
                    total, out = carry
                    value = jnp.exp(scores[c] - peak)
                    scores[c] = value
                    out = out + mm(value.astype(BF16), kv[keys_of(c), v_at])
                    return total + jnp.sum(value, axis=1, keepdims=True), out

                total, out = lax.fori_loop(
                    0, steps, second, (jnp.zeros((tall, 1), F32), jnp.zeros((tall, AHD), F32))
                )
                out = (out / total).astype(BF16)
                delta = jnp.sum(grad.astype(F32) * out.astype(F32), axis=1, keepdims=True)

                def third(c, acc):
                    slope = mm_nt(grad, kv[keys_of(c), v_at]) - delta
                    change = (scores[c] * slope).astype(BF16)
                    return acc + mm(change, kv[keys_of(c), k_at])

                acc = lax.fori_loop(0, steps, third, jnp.zeros((tall, AHD), F32))
                acc = (acc * (scale / total)).astype(BF16)
                for i, at in enumerate(heads):
                    out_ref[src, at] = out[i * STRETCH : (i + 1) * STRETCH]
                    dq_ref[src, at] = acc[i * STRETCH : (i + 1) * STRETCH]

    return call(
        kernel,
        [(queries.shape, BF16), (queries.shape, BF16)],
        (blocks, own_blocks, *pieces, queries, grads),
        smem=(0, 1),
        scratch=[
            pltpu.VMEM((tokens, 2 * half_width), BF16),
            pltpu.VMEM((tokens // chunk, tall, chunk), F32),
        ],
        flops=10 * queries.size * tokens,
        nbytes=4 * tokens * half_width,
    )


def body(
    stretch_order,
    attn_queries,
    attn_keys,
    attn_values,
    attn_grad,
    mamba_input,
    gate_input,
    state_write,
    state_read,
    step_raw,
    decay_log,
    skip_gain,
    norm_gain,
    mamba_grad,
):
    ctx_count = lax.axis_size("ctx")
    tp_count = lax.axis_size("tp")
    group = state_write.shape[1] // NSTATE
    units = ctx_count // group
    by_permute = units <= 4
    my_index = lax.axis_index("ctx")
    my_unit, my_place = my_index // group, my_index % group
    me = my_place.astype(jnp.int32).reshape(1)
    chans = mamba_input.shape[1] // group
    heads = chans // HEAD_CH
    kv_heads = attn_keys.shape[1] // AHD
    turn = stretch_order[0]
    last = 2 * ctx_count

    def in_plane(values):
        moved = [values[0]]
        for m in range(1, group):
            pairs = [(i, (i // group) * group + ((i % group) ^ m)) for i in range(ctx_count)]
            moved.append(lax.ppermute(values[m], "ctx", pairs))
        return moved

    def across(value):
        moved = [value]
        for m in range(1, units):
            pairs = [(i, ((i // group) ^ m) * group + i % group) for i in range(ctx_count)]
            moved.append(lax.ppermute(value, "ctx", pairs))
        return moved

    def all_units(value):
        if by_permute:
            return [part[None] for part in across(value)]
        if group == 1:
            return [lax.all_gather(value, "ctx", axis=0)]
        sets = [[u * group + j for u in range(units)] for j in range(group)]
        return [lax.all_gather(value, "ctx", axis=0, axis_index_groups=sets)]

    own_kv = jnp.concatenate([attn_keys, attn_values], axis=1)
    kv_units = all_units(own_kv)

    packed = pack_forward(me, mamba_input, state_write, state_read, step_raw, group)
    forward_pieces = in_plane(packed)
    gates = in_plane(pack_gate(me, gate_input, mamba_grad, group))

    unit_ids = jnp.arange(units, dtype=jnp.int32)
    if by_permute:
        unit_ids = unit_ids ^ my_unit
    place_ids = jnp.arange(group, dtype=jnp.int32) ^ my_place

    def class_bounds(unit):
        first = (unit * group + turn) % ctx_count
        wraps = first + group > ctx_count
        extra = first + group - ctx_count
        out_start = (jnp.where(wraps, 0, first), jnp.where(wraps, first, last - first - group))
        out_end = (jnp.where(wraps, extra, first + group), last - first)
        in_start = (first, jnp.where(wraps, last - extra, last - first - group))
        in_end = (
            jnp.where(wraps, last - first, first + group),
            jnp.where(wraps, last, last - first),
        )
        return out_start, out_end, in_start, in_end

    out_start, out_end, in_start, in_end = class_bounds(my_unit)
    _, all_out_end, all_in_start, _ = class_bounds(unit_ids)
    all_out_end = jnp.stack(all_out_end, axis=1).reshape(-1)
    all_in_start = jnp.stack(all_in_start, axis=1).reshape(-1)
    own_out_end = jnp.stack(out_end)
    own_in_start = jnp.stack(in_start)
    enter_mask = (all_out_end[None, :] <= own_in_start[:, None]).astype(F32)
    leave_mask = (own_out_end[:, None] <= all_in_start[None, :]).astype(F32)
    own_end = (all_out_end[None, :] <= own_out_end[:, None]).astype(F32)
    before_in = (all_out_end[None, :] <= all_in_start[:, None]).astype(F32)
    ends = (all_out_end[None, :] <= all_out_end[:, None]).astype(F32)
    own_mask = jnp.concatenate([enter_mask, jnp.zeros((6, 2 * units), F32)], axis=0)
    own_end = jnp.concatenate([own_end, jnp.zeros((6, 2 * units), F32)], axis=0)

    def info_of(row):
        half, place, offset = row // (group * STRETCH), (row // STRETCH) % group, row % STRETCH
        pair = (my_unit * group + (place ^ my_place) + turn) % ctx_count
        block = jnp.where(half == 0, pair, last - 1 - pair)

        def within(start, end):
            return ((block >= start) & (block < end)).astype(F32)

        low = jnp.where(
            within(in_start[1], in_end[1]) > 0,
            in_start[1],
            jnp.where(within(in_start[0], in_end[0]) > 0, in_start[0], out_start[0]),
        )
        return [
            (block * STRETCH + offset).astype(F32),
            (low * STRETCH).astype(F32),
            within(out_start[0], out_end[0]),
            within(out_start[1], out_end[1]),
            within(in_start[0], in_end[0]),
            within(in_start[1], in_end[1]),
        ]

    rows = 2 * group * STRETCH
    cols = info_of(lax.broadcasted_iota(jnp.int32, (rows, 8), 0))
    pick = lax.broadcasted_iota(jnp.int32, (rows, 8), 1)
    info = sum(jnp.where(pick == i, c, 0.0) for i, c in enumerate(cols))
    cols = info_of(lax.broadcasted_iota(jnp.int32, (8, rows), 1))
    pick = lax.broadcasted_iota(jnp.int32, (8, rows), 0)
    info_t = sum(jnp.where(pick == i, c, 0.0) for i, c in enumerate(cols))

    decay = -jnp.exp(lax.dynamic_slice(decay_log, (my_place * heads,), (heads,)))
    small = jnp.pad(decay[None], ((0, 7), (0, 128 - heads)))
    skip = jnp.repeat(lax.dynamic_slice(skip_gain, (my_place * heads,), (heads,)), HEAD_CH)
    gain = lax.dynamic_slice(norm_gain, (my_place * chans,), (chans,))
    chan = jnp.pad(jnp.stack([skip, gain]), ((0, 6), (0, 0)))

    msg, x, w, r, cum, rate, tail = outgoing_state(forward_pieces, info, info_t, small, chans)
    msgs = all_units(msg)

    kv_all = kv_units[0] if len(kv_units) == 1 else jnp.concatenate(kv_units, axis=0)
    kv_pieces = in_plane([kv_all] * group)

    y = intra_forward(x, w, r, cum, rate, info, info_t, chan)
    gated, sums, state, enter, leave = mixed_rows(
        msgs, y, r, cum, gates, info, chan, before_in, ends, enter_mask, own_mask, own_end
    )
    if tp_count == 2:
        sums = sums + lax.ppermute(sums, "tp", [(0, 1), (1, 0)])
    else:
        sums = lax.psum(sums, "tp")
    sums = in_plane([sums] * group)
    touch, dmix, lift, *out_pieces = mixed_cotangent(
        sums, gated, gates, r, cum, info_t, chan, float(mamba_input.shape[1] * tp_count)
    )
    touches = all_units(touch)
    (mamba_output,) = unpack(me, in_plane(out_pieces), (chans,))
    dx, dw, dr = intra_backward(x, w, r, cum, rate, dmix, lift, state, info, info_t)

    pair_table = (unit_ids[None, :] * group + place_ids[:, None] + turn) % ctx_count
    pair_table = pair_table.reshape(1, -1)
    blocks = jnp.concatenate([pair_table, last - 1 - pair_table], axis=0)
    attn_output, query_grad = attention(
        blocks, blocks[:, 0] if by_permute else jnp.stack(
            [(my_index + turn) % ctx_count, last - 1 - (my_index + turn) % ctx_count]
        ),
        kv_pieces, attn_queries, attn_grad, kv_heads,
    )

    finals = final_grads(
        touches, x, w, rate, tail, dx, dw, dr, dmix, info, chan, enter, leave, leave_mask
    )
    input_grad, write_grad, read_grad = unpack(me, in_plane(finals), (chans, NSTATE, NSTATE))
    return (attn_output, query_grad, mamba_output, input_grad, write_grad, read_grad)


def solution(mesh):
    wide, flat = P("ctx", "tp"), P("tp")
    return jax.shard_map(
        body,
        mesh=mesh,
        in_specs=(P(),) + (wide,) * 9 + (flat,) * 3 + (wide,),
        out_specs=(wide,) * 6,
        check_vma=False,
    )
```

time: 515 us -> 177 us (0.34)
  the two profiles are of different devices: /device:TPU:6 before, /device:TPU:8 now
where the time goes in v1:
time: 177 us; the launch traced here: 174 us
  waiting for transfers between devices  69.8 us (39%)
  Pallas kernels  43.8 us (25%)
  starting transfers between devices  31.4 us (18%)
  local copies, waits for them, and re-layouts  24.5 us (14%)
  other arithmetic  2.86 us (2%)
    pallas_call x11, Pallas kernels, call(): pl.pallas_call(fn, out_shape=tuple((jax.ShapeDtypeStruct(s, d) for s, d i...  43.8 us
    ppermute x9, waiting for transfers between devices, across(): moved.append(lax.ppermute(value, 'ctx', pairs))  39.1 us
    ppermute x18, waiting for transfers between devices, in_plane(): moved.append(lax.ppermute(values[m], 'ctx', pairs))  29.6 us
    unnamed x100, local copies, waits for them, and re-layouts  19.8 us
    ppermute x18, starting transfers between devices, in_plane(): moved.append(lax.ppermute(values[m], 'ctx', pairs))  17.6 us
    ppermute x9, starting transfers between devices, across(): moved.append(lax.ppermute(value, 'ctx', pairs))  13.8 us
  transfers between devices with their start and end apart: 28, of which 14 were waited for; matrix products, arithmetic and copies ran while one was open for 5% of the time, Pallas kernels for 11%

profile of v1, /device:TPU:8, one launch (start us, length us, event | category | flops | bytes accessed | tf_op | source)
XLA Modules:
  0.0 173.6 jit_solution(4887985488866336182)
XLA Ops:
  0.7 0.7 copy-done.41
  1.5 1.0 copy-done
  2.5 0.9 copy-done.22
  3.4 0.9 copy-done.23
  4.6 1.6 collective-permute-start.10
  6.2 1.4 collective-permute-start.11
  8.2 1.0 copy-done.2
  9.2 0.9 shard_map.182
  10.1 1.5 collective-permute-start.6
  11.6 1.5 collective-permute-start.7
  14.0 0.7 fusion.refs_4_.info_ref.refs_11_.refs_12_
  16.7 1.3 collective-permute-done.10.refs_2_
  18.1 2.4 %collective-permute-start.8 = (bf16[128,1024]{1,0:T(8,128)(2,1)}, bf16[128,1024]{1,0:T(8,128)(2,1)S(1)}, u32[]{:S(2)}, u32[]{:S(2)}) collective-permute-start(bf16[128,1024]{1,0:T(8,128)(2,1)} %get-tuple-element.50), channel_id=1, source_target_pairs={{0,6},{2,4},{4,2},{6,0},{8,14},{10,12},{12,10},{14,8},{16,22},{18,... | collective-permute-start | bytes 786440 | tf_op jit(solution)/shard_map/ppermute | solution.py:635
  20.5 0.7 copy-done.18
  21.2 0.7 copy-done.20
  21.9 0.9 copy-done.19
  22.8 0.9 copy-done.21
  23.8 2.0 %shard_map.184 = (bf16[2,144,512]{2,1,0:T(8,128)(2,1)S(1)}, bf16[512,512]{1,0:T(8,128)(2,1)S(1)}, bf16[512,128]{1,0:T(8,128)(2,1)S(1)}, bf16[512,128]{1,0:T(8,12...) custom-call(bf16[128,896]{1,0:T(8,128)(2,1)S(1)} %get-tuple-element.51.refs_0_, ...), custom_call_target="tpu_custom_call" | custom-call | flops 134217728 | bytes 1572864 | tf_op jit(solution)/shard_map/pallas_call | solution.py:54
  25.8 0.7 copy-done.5
  26.5 1.6 collective-permute-start.14
  28.1 0.7 constant_dynamic-update-slice_fusion.1
  28.9 0.7 stack_reshape.3
  29.6 0.8 dynamic_slice.11
  30.3 2.5 %collective-permute-start.12 = (bf16[2,144,512]{2,1,0:T(8,128)(2,1)S(1)}, bf16[2,144,512]{2,1,0:T(8,128)(2,1)S(1)}, u32[]{:S(2)}, u32[]{:S(2)}) collective-permute-start(bf16[2,144,512]{2,1,0:T(8,128)(2,1)S(1)} %get-tuple-element.55), channel_id=1, source_target_pairs={{0,8},{2,10},{4,12},{6,14},{8,0},{10,2},{12,4},{14,6},{16,24},{18,... | collective-permute-start | bytes 884744 | tf_op jit(solution)/shard_map/ppermute | solution.py:642
  32.8 1.6 constant_dynamic-update-slice_fusion
  34.4 0.8 collective-permute-start
  35.2 2.2 %collective-permute-start.1 = (bf16[128,1024]{1,0:T(8,128)(2,1)}, bf16[128,1024]{1,0:T(8,128)(2,1)S(1)}, u32[]{:S(2)}, u32[]{:S(2)}) collective-permute-start(bf16[128,1024]{1,0:T(8,128)(2,1)} %constant_dynamic-update-slice_fusion), channel_id=1, source_target_pairs={{0,16},{2,18},{4,20},{6,22},{8,24},{10,26},{12,28},{14,30},{16,0},... | collective-permute-start | bytes 786440 | tf_op jit(solution)/shard_map/ppermute | solution.py:642
  37.4 6.0 %collective-permute-done.14 = bf16[2,144,512]{2,1,0:T(8,128)(2,1)S(1)} collective-permute-done((bf16[2,144,512]{2,1,0:T(8,128)(2,1)S(1)}, bf16[2,144,512]{2,1,0:T(8,128)(2,1)S(1)}, u32[]{:S(2)}, u32[]{:S(2)}) %collective-permute-start.14) | collective-permute-done | bytes 294944 | tf_op jit(solution)/shard_map/ppermute | solution.py:642
  43.5 2.6 %collective-permute-start.2 = (bf16[128,1024]{1,0:T(8,128)(2,1)}, bf16[128,1024]{1,0:T(8,128)(2,1)S(1)}, u32[]{:S(2)}, u32[]{:S(2)}) collective-permute-start(bf16[128,1024]{1,0:T(8,128)(2,1)} %constant_dynamic-update-slice_fusion), channel_id=1, source_target_pairs={{0,24},{2,26},{4,28},{6,30},{8,16},{10,18},{12,20},{14,22},{16,8},... | collective-permute-start | bytes 786440 | tf_op jit(solution)/shard_map/ppermute | solution.py:642
  46.1 2.2 %shard_map.185.refs_8_ = f32[512,512]{1,0:T(8,128)S(1)} custom-call(bf16[512,512]{1,0:T(8,128)(2,1)S(1)} %get-tuple-element.56.x_ref.refs_4_, bf16[512,128]{1,0:T(8,128)(2,1)S(1)} %get-tuple-element.57.w_ref.refs_5_, bf16[512,128]{1,0:T(8,128)(2,1)S(1)} %get-tuple-element.58.r_ref.refs_9_, f32[512,128]{1,0:T(8,128)S(1)} %get-tuple-element.59.cum_ref.refs_10_, ...), custom_call_target="tpu_custom_call" | custom-call | flops 536870912 | bytes 2097152 | tf_op jit(solution)/shard_map/pallas_call | solution.py:54
  48.3 15.9 %collective-permute-done.13 = bf16[2,144,512]{2,1,0:T(8,128)(2,1)S(1)} collective-permute-done((bf16[2,144,512]{2,1,0:T(8,128)(2,1)S(1)}, bf16[2,144,512]{2,1,0:T(8,128)(2,1)S(1)}, u32[]{:S(2)}, u32[]{:S(2)}) %collective-permute-start.13) | collective-permute-done | bytes 294944 | tf_op jit(solution)/shard_map/ppermute | solution.py:642
  64.2 2.7 %shard_map.186 = (f32[512,512]{1,0:T(8,128)S(1)}, f32[8,512]{1,0:T(8,128)S(1)}, bf16[256,512]{1,0:T(8,128)(2,1)S(1)}, f32[8,512]{1,0:T(8,128)S(1)}, f32[8,512]{1,0:T(8,128)S(1)}) custom-call(bf16[1,2,144,512]{3,2,1,0:T(8,128)(2,1)S(1)} %bitcast.22, bf16[1,2,144,512]{3,2,1,0:T(8,128)(2,1)S(1)} %bitcast.24, bf16[1,2,144,512]{3,2,1,0:T(8,128)(2,1)S(1)} %bitcast.25, ...), custom_call_target="tpu_custom_call" | custom-call | flops 268435456 | bytes 4194304 | tf_op jit(solution)/shard_map/pallas_call | solution.py:54
  66.9 0.7 copy-done.35
  67.6 1.2 collective-permute-done.15
  69.9 2.7 %collective-permute-done.16.refs_5_ = f32[8,512]{1,0:T(8,128)S(1)} collective-permute-done((f32[8,512]{1,0:T(8,128)S(1)}, f32[8,512]{1,0:T(8,128)S(1)}, u32[]{:S(2)}, u32[]{:S(2)}) %collective-permute-start.16) | collective-permute-done | bytes 16416 | tf_op jit(solution)/shard_map/ppermute | solution.py:635
  73.1 4.1 %collective-permute-done.18.refs_7_ = f32[8,512]{1,0:T(8,128)S(1)} collective-permute-done((f32[8,512]{1,0:T(8,128)S(1)}, f32[8,512]{1,0:T(8,128)S(1)}, u32[]{:S(2)}, u32[]{:S(2)}) %collective-permute-start.18) | collective-permute-done | bytes 16416 | tf_op jit(solution)/shard_map/ppermute | solution.py:635
  77.2 2.7 %shard_map.187 = (bf16[2,128,512]{2,1,0:T(8,128)(2,1)S(1)}, f32[512,512]{1,0:T(8,128)S(1)}, bf16[512,512]{1,0:T(8,128)(2,1)S(1)}, bf16[128,512]{1,0:T(8,128)(2,1...) custom-call(bf16[128,1024]{1,0:T(8,128)(2,1)S(1)} %get-tuple-element.47.refs_4_.refs_0_, ...), custom_call_target="tpu_custom_call" | custom-call | flops 134217728 | bytes 4194304 | tf_op jit(solution)/shard_map/pallas_call | solution.py:54
  79.9 0.8 copy-done.33
  81.3 1.4 collective-permute-start.22
  82.8 2.1 %collective-permute-start.23 = (bf16[2,128,512]{2,1,0:T(8,128)(2,1)S(1)}, bf16[2,128,512]{2,1,0:T(8,128)(2,1)S(1)}, u32[]{:S(2)}, u32[]{:S(2)}) collective-permute-start(bf16[2,128,512]{2,1,0:T(8,128)(2,1)S(1)} %get-tuple-element.67), channel_id=1, source_target_pairs={{0,16},{2,18},{4,20},{6,22},{8,24},{10,26},{12,28},{14,30},{16,0},... | collective-permute-start | bytes 786440 | tf_op jit(solution)/shard_map/ppermute | solution.py:642
  86.8 3.6 %collective-permute-done.22 = bf16[2,128,512]{2,1,0:T(8,128)(2,1)S(1)} collective-permute-done((bf16[2,128,512]{2,1,0:T(8,128)(2,1)S(1)}, bf16[2,128,512]{2,1,0:T(8,128)(2,1)S(1)}, u32[]{:S(2)}, u32[]{:S(2)}) %collective-permute-start.22) | collective-permute-done | bytes 262176 | tf_op jit(solution)/shard_map/ppermute | solution.py:642
  90.4 0.7 copy-done.9
  91.6 10.3 %collective-permute-done.23 = bf16[2,128,512]{2,1,0:T(8,128)(2,1)S(1)} collective-permute-done((bf16[2,128,512]{2,1,0:T(8,128)(2,1)S(1)}, bf16[2,128,512]{2,1,0:T(8,128)(2,1)S(1)}, u32[]{:S(2)}, u32[]{:S(2)}) %collective-permute-start.23) | collective-permute-done | bytes 262176 | tf_op jit(solution)/shard_map/ppermute | solution.py:642
  101.9 0.7 copy-done.11
  103.1 3.2 %collective-permute-done.24 = bf16[2,128,512]{2,1,0:T(8,128)(2,1)S(1)} collective-permute-done((bf16[2,128,512]{2,1,0:T(8,128)(2,1)S(1)}, bf16[2,128,512]{2,1,0:T(8,128)(2,1)S(1)}, u32[]{:S(2)}, u32[]{:S(2)}) %collective-permute-start.24) | collective-permute-done | bytes 262176 | tf_op jit(solution)/shard_map/ppermute | solution.py:642
  106.4 0.7 copy-done.13
  108.2 0.7 add_add_fusion
  108.9 1.3 add.290
  110.2 0.9 copy-done.4
  111.1 0.7 copy-done.17
  111.8 1.0 copy-done.34
  112.9 0.9 copy-done.36
  113.8 3.8 %shard_map.189 = (f32[512,512]{1,0:T(8,128)S(1)}, f32[512,128]{1,0:T(8,128)S(1)}, f32[512,128]{1,0:T(8,128)S(1)}) custom-call(bf16[512,512]{1,0:T(8,128)(2,1)S(1)} %get-tuple-element.56.x_ref.refs_4_, bf16[512,128]{1,0:T(8,128)(2,1)S(1)} %copy-done.4, bf16[512,128]{1,0:T(8,128)(2,1)S(1)} %get-tuple-element.58.r_ref.refs_9_, ...), custom_call_target="tpu_custom_call" | custom-call | flops 1073741824 | bytes 4194304 | tf_op jit(solution)/shard_map/pallas_call | solution.py:54
  118.4 2.7 %shard_map.190 = (bf16[128,768]{1,0:T(8,128)(2,1)S(1)}, bf16[128,768]{1,0:T(8,128)(2,1)S(1)}, bf16[128,768]{1,0:T(8,128)(2,1)S(1)}, bf16[128,768]{1,0:T(8,128)(2,1)S(1)}) custom-call(bf16[1,2,128,512]{3,2,1,0:T(8,128)(2,1)S(1)} %bitcast.26, bf16[1,2,128,512]{3,2,1,0:T(8,128)(2,1)S(1)} %bitcast.27, bf16[1,2,128,512]{3,2,1,0:T(8,128)(2,1)S(1)} %bitcast.28, ...), custom_call_target="tpu_custom_call" | custom-call | flops 268435456 | bytes 4194304 | tf_op jit(solution)/shard_map/pallas_call | solution.py:54
  121.0 13.3 %collective-permute-done.19.refs_1_ = bf16[128,512]{1,0:T(8,128)(2,1)} collective-permute-done((bf16[128,512]{1,0:T(8,128)(2,1)}, bf16[128,512]{1,0:T(8,128)(2,1)}, u32[]{:S(2)}, u32[]{:S(2)}) %collective-permute-start.19) | collective-permute-done | bytes 131104 | tf_op jit(solution)/shard_map/ppermute | solution.py:635
  134.4 0.7 collective-permute-done.20.refs_2_
  135.1 1.5 collective-permute-start.25
  136.6 3.8 %collective-permute-done.21.refs_3_ = bf16[128,512]{1,0:T(8,128)(2,1)S(1)} collective-permute-done((bf16[128,512]{1,0:T(8,128)(2,1)S(1)}, bf16[128,512]{1,0:T(8,128)(2,1)S(1)}, u32[]{:S(2)}, u32[]{:S(2)}) %collective-permute-start.21) | collective-permute-done | bytes 131104 | tf_op jit(solution)/shard_map/ppermute | solution.py:635
  140.4 1.8 %collective-permute-done.25.refs_1_ = bf16[128,768]{1,0:T(8,128)(2,1)S(1)} collective-permute-done((bf16[128,768]{1,0:T(8,128)(2,1)S(1)}, bf16[128,768]{1,0:T(8,128)(2,1)S(1)}, u32[]{:S(2)}, u32[]{:S(2)}) %collective-permute-start.25) | collective-permute-done | bytes 196640 | tf_op jit(solution)/shard_map/ppermute | solution.py:635
  142.2 2.8 %collective-permute-start.27 = (bf16[128,768]{1,0:T(8,128)(2,1)S(1)}, bf16[128,768]{1,0:T(8,128)(2,1)S(1)}, u32[]{:S(2)}, u32[]{:S(2)}) collective-permute-start(bf16[128,768]{1,0:T(8,128)(2,1)S(1)} %get-tuple-element.80), channel_id=1, source_target_pairs={{0,6},{2,4},{4,2},{6,0},{8,14},{10,12},{12,10},{14,8},{16,22},{18,... | collective-permute-start | bytes 589832 | tf_op jit(solution)/shard_map/ppermute | solution.py:635
  145.1 1.9 %shard_map.188 = bf16[128,2048]{1,0:T(8,128)(2,1)} custom-call(s32[1]{0:T(128)} %bitcast.5.me_ref, bf16[128,512]{1,0:T(8,128)(2,1)S(1)} %copy-done.25, bf16[128,512]{1,0:T(8,128)(2,1)} %collective-permute-done.19.refs_1_, bf16[128,512]{1,0:T(8,128)(2,1)} %collective-permute-done.20.refs_2_, bf16[128,512]{1,0:T(8,128)(2,1)S(1)} %collective-permute-done.21.refs_3_), custom_call_target="tpu_custom_call" | custom-call | bytes 1048576 | tf_op jit(solution)/shard_map/pallas_call | solution.py:54
  147.0 1.8 %collective-permute-done.27.refs_3_ = bf16[128,768]{1,0:T(8,128)(2,1)S(1)} collective-permute-done((bf16[128,768]{1,0:T(8,128)(2,1)S(1)}, bf16[128,768]{1,0:T(8,128)(2,1)S(1)}, u32[]{:S(2)}, u32[]{:S(2)}) %collective-permute-start.27) | collective-permute-done | bytes 196640 | tf_op jit(solution)/shard_map/ppermute | solution.py:635
  148.8 0.9 shard_map.191
  149.8 23.8 %shard_map.181 = (bf16[128,2048]{1,0:T(8,128)(2,1)}, bf16[128,2048]{1,0:T(8,128)(2,1)}) custom-call(s32[2,16]{1,0:T(2,128)S(1)} %pad_add_fusion.2.refs_0_, s32[2]{0:T(128)S(1)} %slice_reduce_fusion.refs_1_, bf16[4,128,1024]{2,1,0:T(8,128)(2,1)S(1)} %pad_maximum_fusion.refs_2_, bf16[4,128,1024]{2,1,0:T(8,128)(2,1)} %collective-permute-done.3.refs_3_, ...), custom_call_target="tpu_custom_call" | custom-call | flops 5368709120 | bytes 4194304 | tf_op jit(solution)/shard_map/pallas_call | solution.py:54
  (140 shorter events, 11.1 us)
Async XLA Ops:
  0.6 0.7 copy-start.41
  1.5 1.0 copy-start
  2.5 0.9 copy-start.22
  3.4 0.9 copy-start.23
  4.3 3.8 %copy-start.1 = (bf16[128,2048]{1,0:T(8,128)(2,1)S(1)}, bf16[128,2048]{1,0:T(8,128)(2,1)}, u32[]{:S(2)}) copy-start(bf16[128,2048]{1,0:T(8,128)(2,1)} %gate_ref.1) | copy-start | bytes 1572868
  4.6 13.5 %collective-permute-start.10 = (bf16[128,896]{1,0:T(8,128)(2,1)S(1)}, bf16[128,896]{1,0:T(8,128)(2,1)S(1)}, u32[]{:S(2)}, u32[]{:S(2)}) collective-permute-start(bf16[128,896]{1,0:T(8,128)(2,1)S(1)} %get-tuple-element.53), channel_id=1, source_target_pairs={{0,4},{2,6},{4,0},{6,2},{8,12},{10,14},{12,8},{14,10},{16,20},{18,... | collective-permute-start | bytes 688136 | tf_op jit(solution)/shard_map/ppermute | solution.py:635
  6.2 14.3 %collective-permute-start.11 = (bf16[128,896]{1,0:T(8,128)(2,1)S(1)}, bf16[128,896]{1,0:T(8,128)(2,1)S(1)}, u32[]{:S(2)}, u32[]{:S(2)}) collective-permute-start(bf16[128,896]{1,0:T(8,128)(2,1)S(1)} %get-tuple-element.54), channel_id=1, source_target_pairs={{0,6},{2,4},{4,2},{6,0},{8,14},{10,12},{12,10},{14,8},{16,22},{18,... | collective-permute-start | bytes 688136 | tf_op jit(solution)/shard_map/ppermute | solution.py:635
  7.6 13.6 %collective-permute-start.9 = (bf16[128,896]{1,0:T(8,128)(2,1)S(1)}, bf16[128,896]{1,0:T(8,128)(2,1)S(1)}, u32[]{:S(2)}, u32[]{:S(2)}) collective-permute-start(bf16[128,896]{1,0:T(8,128)(2,1)S(1)} %get-tuple-element.52), channel_id=1, source_target_pairs={{0,2},{2,0},{4,6},{6,4},{8,10},{10,8},{12,14},{14,12},{16,18},{18,... | collective-permute-start | bytes 688136 | tf_op jit(solution)/shard_map/ppermute | solution.py:635
  8.1 1.0 copy-start.2
  10.1 22.7 %collective-permute-start.6 = (bf16[128,1024]{1,0:T(8,128)(2,1)}, bf16[128,1024]{1,0:T(8,128)(2,1)S(1)}, u32[]{:S(2)}, u32[]{:S(2)}) collective-permute-start(bf16[128,1024]{1,0:T(8,128)(2,1)} %get-tuple-element.48), channel_id=1, source_target_pairs={{0,2},{2,0},{4,6},{6,4},{8,10},{10,8},{12,14},{14,12},{16,18},{18,... | collective-permute-start | bytes 786440 | tf_op jit(solution)/shard_map/ppermute | solution.py:635
  11.6 22.8 %collective-permute-start.7 = (bf16[128,1024]{1,0:T(8,128)(2,1)}, bf16[128,1024]{1,0:T(8,128)(2,1)S(1)}, u32[]{:S(2)}, u32[]{:S(2)}) collective-permute-start(bf16[128,1024]{1,0:T(8,128)(2,1)} %get-tuple-element.49), channel_id=1, source_target_pairs={{0,4},{2,6},{4,0},{6,2},{8,12},{10,14},{12,8},{14,10},{16,20},{18,... | collective-permute-start | bytes 786440 | tf_op jit(solution)/shard_map/ppermute | solution.py:635
  14.8 31.3 %copy-start.15 = (f32[8,512]{1,0:T(8,128)}, f32[8,512]{1,0:T(8,128)S(1)}, u32[]{:S(2)}) copy-start(f32[8,512]{1,0:T(8,128)S(1)} %fusion.7.refs_5_.info_t_ref.refs_11_) | copy-start | bytes 49156
  18.1 17.1 %collective-permute-start.8 = (bf16[128,1024]{1,0:T(8,128)(2,1)}, bf16[128,1024]{1,0:T(8,128)(2,1)S(1)}, u32[]{:S(2)}, u32[]{:S(2)}) collective-permute-start(bf16[128,1024]{1,0:T(8,128)(2,1)} %get-tuple-element.50), channel_id=1, source_target_pairs={{0,6},{2,4},{4,2},{6,0},{8,14},{10,12},{12,10},{14,8},{16,22},{18,... | collective-permute-start | bytes 786440 | tf_op jit(solution)/shard_map/ppermute | solution.py:635
  21.9 0.9 copy-start.19
  22.8 0.9 copy-start.21
  23.8 4.3 %copy-start.40 = (bf16[128,512]{1,0:T(8,128)(2,1)S(1)}, bf16[128,512]{1,0:T(8,128)(2,1)}, u32[]{:S(2)}) copy-start(bf16[128,512]{1,0:T(8,128)(2,1)} %param.16) | copy-start | bytes 393220
  26.5 19.6 %copy-start.3 = (bf16[512,128]{1,0:T(8,128)(2,1)}, bf16[512,128]{1,0:T(8,128)(2,1)S(1)}, u32[]{:S(2)}) copy-start(bf16[512,128]{1,0:T(8,128)(2,1)S(1)} %get-tuple-element.57.w_ref.refs_5_) | copy-start | bytes 393220
  26.5 2.2 %copy-start.48 = (f32[32]{0:T(128)S(1)}, f32[32]{0:T(128)}, u32[]{:S(2)}) copy-start(f32[32]{0:T(128)} %param.25) | copy-start | bytes 388
  26.5 17.0 %collective-permute-start.14 = (bf16[2,144,512]{2,1,0:T(8,128)(2,1)S(1)}, bf16[2,144,512]{2,1,0:T(8,128)(2,1)S(1)}, u32[]{:S(2)}, u32[]{:S(2)}) collective-permute-start(bf16[2,144,512]{2,1,0:T(8,128)(2,1)S(1)} %get-tuple-element.55), channel_id=1, source_target_pairs={{0,24},{2,26},{4,28},{6,30},{8,16},{10,18},{12,20},{14,22},{16,8},... | collective-permute-start | bytes 884744 | tf_op jit(solution)/shard_map/ppermute | solution.py:642
  29.6 3.3 %copy-start.44 = (f32[1,512]{1,0:T(1,128)S(1)}, f32[1,512]{1,0:T(1,128)}, u32[]{:S(2)}) copy-start(f32[1,512]{1,0:T(1,128)} %stack_reshape.3) | copy-start | bytes 6148
  30.3 18.0 %collective-permute-start.12 = (bf16[2,144,512]{2,1,0:T(8,128)(2,1)S(1)}, bf16[2,144,512]{2,1,0:T(8,128)(2,1)S(1)}, u32[]{:S(2)}, u32[]{:S(2)}) collective-permute-start(bf16[2,144,512]{2,1,0:T(8,128)(2,1)S(1)} %get-tuple-element.55), channel_id=1, source_target_pairs={{0,8},{2,10},{4,12},{6,14},{8,0},{10,2},{12,4},{14,6},{16,24},{18,... | collective-permute-start | bytes 884744 | tf_op jit(solution)/shard_map/ppermute | solution.py:642
  32.8 31.4 %collective-permute-start.13 = (bf16[2,144,512]{2,1,0:T(8,128)(2,1)S(1)}, bf16[2,144,512]{2,1,0:T(8,128)(2,1)S(1)}, u32[]{:S(2)}, u32[]{:S(2)}) collective-permute-start(bf16[2,144,512]{2,1,0:T(8,128)(2,1)S(1)} %get-tuple-element.55), channel_id=1, source_target_pairs={{0,16},{2,18},{4,20},{6,22},{8,24},{10,26},{12,28},{14,30},{16,0},... | collective-permute-start | bytes 884744 | tf_op jit(solution)/shard_map/ppermute | solution.py:642
  34.4 11.7 %copy-start.45 = (pred[2,8]{1,0:T(4,128)(4,1)S(1)}, pred[2,8]{1,0:T(4,128)(4,1)}, u32[]{:S(2)}) copy-start(pred[2,8]{1,0:T(4,128)(4,1)} %get-tuple-element.87) | copy-start | bytes 52
  34.4 50.4 %collective-permute-start = (bf16[128,1024]{1,0:T(8,128)(2,1)}, bf16[128,1024]{1,0:T(8,128)(2,1)S(1)}, u32[]{:S(2)}, u32[]{:S(2)}) collective-permute-start(bf16[128,1024]{1,0:T(8,128)(2,1)} %constant_dynamic-update-slice_fusion), channel_id=1, source_target_pairs={{0,8},{2,10},{4,12},{6,14},{8,0},{10,2},{12,4},{14,6},{16,24},{18,... | collective-permute-start | bytes 786440 | tf_op jit(solution)/shard_map/ppermute | solution.py:642
  35.2 50.2 %collective-permute-start.1 = (bf16[128,1024]{1,0:T(8,128)(2,1)}, bf16[128,1024]{1,0:T(8,128)(2,1)S(1)}, u32[]{:S(2)}, u32[]{:S(2)}) collective-permute-start(bf16[128,1024]{1,0:T(8,128)(2,1)} %constant_dynamic-update-slice_fusion), channel_id=1, source_target_pairs={{0,16},{2,18},{4,20},{6,22},{8,24},{10,26},{12,28},{14,30},{16,0},... | collective-permute-start | bytes 786440 | tf_op jit(solution)/shard_map/ppermute | solution.py:642
  43.5 42.0 %collective-permute-start.2 = (bf16[128,1024]{1,0:T(8,128)(2,1)}, bf16[128,1024]{1,0:T(8,128)(2,1)S(1)}, u32[]{:S(2)}, u32[]{:S(2)}) collective-permute-start(bf16[128,1024]{1,0:T(8,128)(2,1)} %constant_dynamic-update-slice_fusion), channel_id=1, source_target_pairs={{0,24},{2,26},{4,28},{6,30},{8,16},{10,18},{12,20},{14,22},{16,8},... | collective-permute-start | bytes 786440 | tf_op jit(solution)/shard_map/ppermute | solution.py:642
  67.6 1.2 copy-start.26
  67.6 1.2 copy-start.28
  67.6 9.6 %copy-start.16 = (f32[8,512]{1,0:T(8,128)S(1)}, f32[8,512]{1,0:T(8,128)}, u32[]{:S(2)}) copy-start(f32[8,512]{1,0:T(8,128)} %copy-done.15) | copy-start | bytes 49156
  67.6 1.2 collective-permute-start.15
  68.8 3.8 %collective-permute-start.16 = (f32[8,512]{1,0:T(8,128)S(1)}, f32[8,512]{1,0:T(8,128)S(1)}, u32[]{:S(2)}, u32[]{:S(2)}) collective-permute-start(f32[8,512]{1,0:T(8,128)S(1)} %add.326.refs_4_), channel_id=1, source_target_pairs={{0,2},{2,0},{4,6},{6,4},{8,10},{10,8},{12,14},{14,12},{16,18},{18,... | collective-permute-start | bytes 49160 | tf_op jit(solution)/shard_map/ppermute | solution.py:635
  69.4 3.7 %collective-permute-start.17 = (f32[8,512]{1,0:T(8,128)S(1)}, f32[8,512]{1,0:T(8,128)S(1)}, u32[]{:S(2)}, u32[]{:S(2)}) collective-permute-start(f32[8,512]{1,0:T(8,128)S(1)} %add.326.refs_4_), channel_id=1, source_target_pairs={{0,4},{2,6},{4,0},{6,2},{8,12},{10,14},{12,8},{14,10},{16,20},{18,... | collective-permute-start | bytes 49160 | tf_op jit(solution)/shard_map/ppermute | solution.py:635
  72.6 4.6 %collective-permute-start.18 = (f32[8,512]{1,0:T(8,128)S(1)}, f32[8,512]{1,0:T(8,128)S(1)}, u32[]{:S(2)}, u32[]{:S(2)}) collective-permute-start(f32[8,512]{1,0:T(8,128)S(1)} %add.326.refs_4_), channel_id=1, source_target_pairs={{0,6},{2,4},{4,2},{6,0},{8,14},{10,12},{12,10},{14,8},{16,22},{18,... | collective-permute-start | bytes 49160 | tf_op jit(solution)/shard_map/ppermute | solution.py:635
  77.2 8.2 %copy-start.39 = (bf16[128,1024]{1,0:T(8,128)(2,1)S(1)}, bf16[128,1024]{1,0:T(8,128)(2,1)}, u32[]{:S(2)}) copy-start(bf16[128,1024]{1,0:T(8,128)(2,1)} %constant_dynamic-update-slice_fusion) | copy-start | bytes 786436
  79.9 0.8 copy-start.33
  81.3 4.3 %copy-start.7 = (bf16[2,128,512]{2,1,0:T(8,128)(2,1)}, bf16[2,128,512]{2,1,0:T(8,128)(2,1)S(1)}, u32[]{:S(2)}) copy-start(bf16[2,128,512]{2,1,0:T(8,128)(2,1)S(1)} %get-tuple-element.67) | copy-start | bytes 786436
  81.3 4.3 %copy-start.24 = (bf16[128,512]{1,0:T(8,128)(2,1)}, bf16[128,512]{1,0:T(8,128)(2,1)S(1)}, u32[]{:S(2)}) copy-start(bf16[128,512]{1,0:T(8,128)(2,1)S(1)} %get-tuple-element.63.refs_0_) | copy-start | bytes 393220
  81.3 9.0 %collective-permute-start.22 = (bf16[2,128,512]{2,1,0:T(8,128)(2,1)S(1)}, bf16[2,128,512]{2,1,0:T(8,128)(2,1)S(1)}, u32[]{:S(2)}, u32[]{:S(2)}) collective-permute-start(bf16[2,128,512]{2,1,0:T(8,128)(2,1)S(1)} %get-tuple-element.67), channel_id=1, source_target_pairs={{0,8},{2,10},{4,12},{6,14},{8,0},{10,2},{12,4},{14,6},{16,24},{18,... | collective-permute-start | bytes 786440 | tf_op jit(solution)/shard_map/ppermute | solution.py:642
  82.8 19.1 %collective-permute-start.23 = (bf16[2,128,512]{2,1,0:T(8,128)(2,1)S(1)}, bf16[2,128,512]{2,1,0:T(8,128)(2,1)S(1)}, u32[]{:S(2)}, u32[]{:S(2)}) collective-permute-start(bf16[2,128,512]{2,1,0:T(8,128)(2,1)S(1)} %get-tuple-element.67), channel_id=1, source_target_pairs={{0,16},{2,18},{4,20},{6,22},{8,24},{10,26},{12,28},{14,30},{16,0},... | collective-permute-start | bytes 786440 | tf_op jit(solution)/shard_map/ppermute | solution.py:642
  84.9 21.5 %collective-permute-start.24 = (bf16[2,128,512]{2,1,0:T(8,128)(2,1)S(1)}, bf16[2,128,512]{2,1,0:T(8,128)(2,1)S(1)}, u32[]{:S(2)}, u32[]{:S(2)}) collective-permute-start(bf16[2,128,512]{2,1,0:T(8,128)(2,1)S(1)} %get-tuple-element.67), channel_id=1, source_target_pairs={{0,24},{2,26},{4,28},{6,30},{8,16},{10,18},{12,20},{14,22},{16,8},... | collective-permute-start | bytes 786440 | tf_op jit(solution)/shard_map/ppermute | solution.py:642
  85.6 64.1 %collective-permute-start.3 = (bf16[4,128,1024]{2,1,0:T(8,128)(2,1)S(1)}, bf16[4,128,1024]{2,1,0:T(8,128)(2,1)}, u32[]{:S(2)}, u32[]{:S(2)}) collective-permute-start(bf16[4,128,1024]{2,1,0:T(8,128)(2,1)S(1)} %pad_maximum_fusion.refs_2_), channel_id=1, source_target_pairs={{0,2},{2,0},{4,6},{6,4},{8,10},{10,8},{12,14},{14,12},{16,18},{18,... | collective-permute-start | bytes 3145736 | tf_op jit(solution)/shard_map/ppermute | solution.py:635
  86.2 63.5 %collective-permute-start.4 = (bf16[4,128,1024]{2,1,0:T(8,128)(2,1)S(1)}, bf16[4,128,1024]{2,1,0:T(8,128)(2,1)}, u32[]{:S(2)}, u32[]{:S(2)}) collective-permute-start(bf16[4,128,1024]{2,1,0:T(8,128)(2,1)S(1)} %pad_maximum_fusion.refs_2_), channel_id=1, source_target_pairs={{0,4},{2,6},{4,0},{6,2},{8,12},{10,14},{12,8},{14,10},{16,20},{18,... | collective-permute-start | bytes 3145736 | tf_op jit(solution)/shard_map/ppermute | solution.py:635
  91.1 58.7 %collective-permute-start.5 = (bf16[4,128,1024]{2,1,0:T(8,128)(2,1)S(1)}, bf16[4,128,1024]{2,1,0:T(8,128)(2,1)}, u32[]{:S(2)}, u32[]{:S(2)}) collective-permute-start(bf16[4,128,1024]{2,1,0:T(8,128)(2,1)S(1)} %pad_maximum_fusion.refs_2_), channel_id=1, source_target_pairs={{0,6},{2,4},{4,2},{6,0},{8,14},{10,12},{12,10},{14,8},{16,22},{18,... | collective-permute-start | bytes 3145736 | tf_op jit(solution)/shard_map/ppermute | solution.py:635
  102.6 31.8 %collective-permute-start.19 = (bf16[128,512]{1,0:T(8,128)(2,1)}, bf16[128,512]{1,0:T(8,128)(2,1)}, u32[]{:S(2)}, u32[]{:S(2)}) collective-permute-start(bf16[128,512]{1,0:T(8,128)(2,1)} %get-tuple-element.64), channel_id=1, source_target_pairs={{0,2},{2,0},{4,6},{6,4},{8,10},{10,8},{12,14},{14,12},{16,18},{18,... | collective-permute-start | bytes 393224 | tf_op jit(solution)/shard_map/ppermute | solution.py:635
  107.1 28.0 %collective-permute-start.20 = (bf16[128,512]{1,0:T(8,128)(2,1)}, bf16[128,512]{1,0:T(8,128)(2,1)}, u32[]{:S(2)}, u32[]{:S(2)}) collective-permute-start(bf16[128,512]{1,0:T(8,128)(2,1)} %get-tuple-element.65), channel_id=1, source_target_pairs={{0,4},{2,6},{4,0},{6,2},{8,12},{10,14},{12,8},{14,10},{16,20},{18,... | collective-permute-start | bytes 393224 | tf_op jit(solution)/shard_map/ppermute | solution.py:635
  110.2 0.9 copy-start.4
  111.8 1.0 copy-start.34
  112.8 0.9 copy-start.36
  113.8 3.9 %copy-start.6 = (f32[512,128]{1,0:T(8,128)S(1)}, f32[512,128]{1,0:T(8,128)}, u32[]{:S(2)}) copy-start(f32[512,128]{1,0:T(8,128)} %copy-done.5) | copy-start | bytes 786436
  113.8 3.9 %copy-start.8 = (bf16[2,128,512]{2,1,0:T(8,128)(2,1)S(1)}, bf16[2,128,512]{2,1,0:T(8,128)(2,1)}, u32[]{:S(2)}) copy-start(bf16[2,128,512]{2,1,0:T(8,128)(2,1)} %copy-done.7) | copy-start | bytes 786436
  113.8 3.9 %copy-start.10 = (bf16[2,128,512]{2,1,0:T(8,128)(2,1)S(1)}, bf16[2,128,512]{2,1,0:T(8,128)(2,1)}, u32[]{:S(2)}) copy-start(bf16[2,128,512]{2,1,0:T(8,128)(2,1)} %copy-done.9) | copy-start | bytes 786436
  113.8 3.9 %copy-start.12 = (bf16[2,128,512]{2,1,0:T(8,128)(2,1)S(1)}, bf16[2,128,512]{2,1,0:T(8,128)(2,1)}, u32[]{:S(2)}) copy-start(bf16[2,128,512]{2,1,0:T(8,128)(2,1)} %copy-done.11) | copy-start | bytes 786436
  113.8 3.9 %copy-start.14 = (bf16[2,128,512]{2,1,0:T(8,128)(2,1)S(1)}, bf16[2,128,512]{2,1,0:T(8,128)(2,1)}, u32[]{:S(2)}) copy-start(bf16[2,128,512]{2,1,0:T(8,128)(2,1)} %copy-done.13) | copy-start | bytes 786436
  113.8 3.9 %copy-start.29 = (f32[8,512]{1,0:T(8,128)S(1)}, f32[8,512]{1,0:T(8,128)}, u32[]{:S(2)}) copy-start(f32[8,512]{1,0:T(8,128)} %copy-done.28) | copy-start | bytes 49156
  117.6 0.7 copy-start.27
  118.4 16.0 %copy-start.38 = (bf16[128,512]{1,0:T(8,128)(2,1)S(1)}, bf16[128,512]{1,0:T(8,128)(2,1)}, u32[]{:S(2)}) copy-start(bf16[128,512]{1,0:T(8,128)(2,1)} %copy-done.37) | copy-start | bytes 393220
  118.4 26.8 %copy-start.25 = (bf16[128,512]{1,0:T(8,128)(2,1)S(1)}, bf16[128,512]{1,0:T(8,128)(2,1)}, u32[]{:S(2)}) copy-start(bf16[128,512]{1,0:T(8,128)(2,1)} %copy-done.24) | copy-start | bytes 393220
  134.4 2.2 %copy-start.46 = (s32[1,16]{1,0:T(1,128)S(1)}, s32[1,16]{1,0:T(1,128)}, u32[]{:S(2)}) copy-start(s32[1,16]{1,0:T(1,128)} %add.290) | copy-start | bytes 196
  134.4 6.0 %collective-permute-start.21 = (bf16[128,512]{1,0:T(8,128)(2,1)S(1)}, bf16[128,512]{1,0:T(8,128)(2,1)S(1)}, u32[]{:S(2)}, u32[]{:S(2)}) collective-permute-start(bf16[128,512]{1,0:T(8,128)(2,1)S(1)} %copy-done.38), channel_id=1, source_target_pairs={{0,6},{2,4},{4,2},{6,0},{8,14},{10,12},{12,10},{14,8},{16,22},{18,... | collective-permute-start | bytes 393224 | tf_op jit(solution)/shard_map/ppermute | solution.py:635
  135.1 7.1 %collective-permute-start.25 = (bf16[128,768]{1,0:T(8,128)(2,1)S(1)}, bf16[128,768]{1,0:T(8,128)(2,1)S(1)}, u32[]{:S(2)}, u32[]{:S(2)}) collective-permute-start(bf16[128,768]{1,0:T(8,128)(2,1)S(1)} %get-tuple-element.78), channel_id=1, source_target_pairs={{0,2},{2,0},{4,6},{6,4},{8,10},{10,8},{12,14},{14,12},{16,18},{18,... | collective-permute-start | bytes 589832 | tf_op jit(solution)/shard_map/ppermute | solution.py:635
  140.4 6.6 %collective-permute-start.26 = (bf16[128,768]{1,0:T(8,128)(2,1)S(1)}, bf16[128,768]{1,0:T(8,128)(2,1)S(1)}, u32[]{:S(2)}, u32[]{:S(2)}) collective-permute-start(bf16[128,768]{1,0:T(8,128)(2,1)S(1)} %get-tuple-element.79), channel_id=1, source_target_pairs={{0,4},{2,6},{4,0},{6,2},{8,12},{10,14},{12,8},{14,10},{16,20},{18,... | collective-permute-start | bytes 589832 | tf_op jit(solution)/shard_map/ppermute | solution.py:635
  142.2 6.6 %collective-permute-start.27 = (bf16[128,768]{1,0:T(8,128)(2,1)S(1)}, bf16[128,768]{1,0:T(8,128)(2,1)S(1)}, u32[]{:S(2)}, u32[]{:S(2)}) collective-permute-start(bf16[128,768]{1,0:T(8,128)(2,1)S(1)} %get-tuple-element.80), channel_id=1, source_target_pairs={{0,6},{2,4},{4,2},{6,0},{8,14},{10,12},{12,10},{14,8},{16,22},{18,... | collective-permute-start | bytes 589832 | tf_op jit(solution)/shard_map/ppermute | solution.py:635
  145.1 4.6 %copy-start.32 = (bf16[128,2048]{1,0:T(8,128)(2,1)S(1)}, bf16[128,2048]{1,0:T(8,128)(2,1)}, u32[]{:S(2)}) copy-start(bf16[128,2048]{1,0:T(8,128)(2,1)} %refs_7_.1) | copy-start | bytes 1572868
  147.0 2.8 %copy-start.31 = (bf16[128,2048]{1,0:T(8,128)(2,1)S(1)}, bf16[128,2048]{1,0:T(8,128)(2,1)}, u32[]{:S(2)}) copy-start(bf16[128,2048]{1,0:T(8,128)(2,1)} %refs_6_.1) | copy-start | bytes 1572868
  (13 other events, 9.0 us)

commit v2 on v1

--- a/solution.py
+++ b/solution.py
@@ -13,9 +13,14 @@
 NORM_EPS = 1e-05
 NEG_FILL = -1e30
 KEY_CHUNK = 512
+LOG2_E = 1.4426950408889634
 F32 = jnp.float32
 BF16 = jnp.bfloat16
-VMEM_BYTES = 48 * 1024 * 1024
+MIB = 1024 * 1024
+
+
+def after(value, event):
+    return lax.optimization_barrier((value, event))[0]
 
 
 def mm(a, b):
@@ -46,7 +51,7 @@
     return jnp.concatenate([pair_spread(cols, k) for k in range(heads // 2)], axis=1)
 
 
-def call(fn, outs, args, smem=(), scratch=(), flops=0, nbytes=0):
+def call(fn, outs, args, smem=(), scratch=(), flops=0, nbytes=0, mib=12):
     specs = [
         pl.BlockSpec(memory_space=pltpu.SMEM if i in smem else pltpu.VMEM)
         for i in range(len(args))
@@ -57,51 +62,103 @@
         in_specs=specs,
         out_specs=tuple(pl.BlockSpec(memory_space=pltpu.VMEM) for _ in outs),
         scratch_shapes=list(scratch),
-        compiler_params=pltpu.CompilerParams(vmem_limit_bytes=VMEM_BYTES),
-        cost_estimate=pl.CostEstimate(flops=flops, bytes_accessed=nbytes, transcendentals=0),
+        compiler_params=pltpu.CompilerParams(vmem_limit_bytes=mib * MIB),
+        cost_estimate=pl.CostEstimate(flops=flops // 1000, bytes_accessed=nbytes // 1000, transcendentals=0),
     )(*args)
 
 
-def pack_forward(me, x, w, r, step, group):
+def pack_forward(x, w, r, step, gate, grad, keys, values, group):
     rows, chans = x.shape[0], x.shape[1] // group
     heads = step.shape[1] // group
     width = chans + 2 * NSTATE + 128
-
-    def kernel(me_ref, x_ref, w_ref, r_ref, step_ref, *outs):
+    kv_width = keys.shape[1]
+
+    wide = [(0, chans), (1, NSTATE), (2, NSTATE), (None, 128), (3, chans), (4, chans)]
+    sources = (x, w, r, gate, grad, keys, values)
+    n_in = len(sources)
+    n_out = 2 + group * len(wide)
+
+    def kernel(step_ref, *refs):
+        ins, kv_ref, out, gate_out = refs[:n_in], *refs[n_in : n_in + 3]
+        held = refs[n_in + 3 : -3]
+        step_buf, in_sems, out_sems = refs[-3:]
+        loads = [pltpu.make_async_copy(ins[i], held[i], in_sems.at[i]) for i in range(n_in)]
+        for i in (5, 6, 0, 1, 2, 3, 4):
+            loads[i].start()
         parts = split3(step_ref[...])
         row = lax.broadcasted_iota(jnp.int32, (heads * group, 128), 0)
         col = lax.broadcasted_iota(jnp.int32, (heads * group, 128), 1)
         for m in range(group):
-            dest = me_ref[0] ^ m
-            out = outs[m]
-            out[:, 0:chans] = x_ref[:, pl.ds(pl.multiple_of(dest * chans, 128), chans)]
-            at = pl.ds(pl.multiple_of(dest * NSTATE, 128), NSTATE)
-            out[:, chans : chans + NSTATE] = w_ref[:, at]
-            out[:, chans + NSTATE : chans + 2 * NSTATE] = r_ref[:, at]
             total = jnp.zeros((rows, 128), F32)
             for i in range(3):
-                pick = (row - dest * heads == col - i * heads) & (col >= i * heads)
+                pick = (row - m * heads == col - i * heads) & (col >= i * heads)
                 pick = pick & (col < (i + 1) * heads)
                 total = total + mm(parts[i], jnp.where(pick, 1.0, 0.0).astype(BF16))
-            out[:, chans + 2 * NSTATE : width] = total.astype(BF16)
-
-    return call(
-        kernel, [((rows, width), BF16)] * group, (me, x, w, r, step), smem=(0,), nbytes=2 * x.size * 3
-    )
-
-
-def pack_gate(me, gate, grad, group):
-    rows, chans = gate.shape[0], gate.shape[1] // group
-
-    def kernel(me_ref, gate_ref, grad_ref, *outs):
-        for m in range(group):
-            at = pl.ds(pl.multiple_of((me_ref[0] ^ m) * chans, 128), chans)
-            outs[m][:, 0:chans] = gate_ref[:, at]
-            outs[m][:, chans : 2 * chans] = grad_ref[:, at]
-
-    return call(
-        kernel, [((rows, 2 * chans), BF16)] * group, (me, gate, grad), smem=(0,), nbytes=8 * gate.size
-    )
+            step_buf[m] = total.astype(BF16)
+        copies = []
+
+        def send(src, dst):
+            copy = pltpu.make_async_copy(src, dst, out_sems.at[len(copies)])
+            copy.start()
+            copies.append(copy)
+
+        loads[5].wait()
+        send(held[5], kv_ref.at[:, 0:kv_width])
+        loads[6].wait()
+        send(held[6], kv_ref.at[:, kv_width : 2 * kv_width])
+        start = 0
+        for source, count in wide:
+            if source is not None:
+                loads[source].wait()
+            for m in range(group):
+                at = slice(m * count, (m + 1) * count)
+                if start >= width:
+                    dst = gate_out.at[m, :, start - width : start - width + count]
+                else:
+                    dst = out.at[m, :, start : start + count]
+                send(step_buf.at[m] if source is None else held[source].at[:, at], dst)
+            start += count
+        for copy in copies:
+            copy.wait()
+
+    return move(
+        kernel,
+        [((rows, 2 * kv_width), BF16)]
+        + [((group, rows, width), BF16), ((group, rows, 2 * chans), BF16)],
+        (step, *sources),
+        (pltpu.VMEM,),
+        [pltpu.VMEM(source.shape, BF16) for source in sources]
+        + [
+            pltpu.VMEM((group, rows, 128), BF16),
+            pltpu.SemaphoreType.DMA((n_in,)),
+            pltpu.SemaphoreType.DMA((n_out,)),
+        ],
+        mib=60,
+    )
+
+
+def move(fn, outs, args, spaces, scratch, mib=8):
+    spaces = tuple(spaces) + (pl.ANY,) * (len(args) - len(spaces))
+    return pl.pallas_call(
+        fn,
+        out_shape=tuple(jax.ShapeDtypeStruct(s, d) for s, d in outs),
+        in_specs=[pl.BlockSpec(memory_space=space) for space in spaces],
+        out_specs=tuple(pl.BlockSpec(memory_space=pl.ANY) for _ in outs),
+        scratch_shapes=scratch,
+        compiler_params=pltpu.CompilerParams(vmem_limit_bytes=mib * MIB),
+        cost_estimate=pl.CostEstimate(flops=0, bytes_accessed=1024, transcendentals=0),
+    )(*args)
+
+
+def stack_parts(parts):
+    count = len(parts)
+
+    def kernel(*refs):
+        for i in range(count):
+            refs[count][i] = refs[i][0]
+
+    shape = (count,) + parts[0].shape[1:]
+    return call(kernel, [(shape, BF16)], parts, nbytes=4 * count * parts[0].size)[0]
 
 
 def unpack(me, pieces, widths):
@@ -131,21 +188,20 @@
             yield half, m, (half * group + m) * STRETCH
 
 
-def outgoing_state(pieces, info, info_t, small, chans):
-    group = len(pieces)
+def outgoing_state(me, pieces, info, info_t, small, chans):
+    group = pieces.shape[0]
     rows = 2 * group * STRETCH
     heads = chans // HEAD_CH
 
     def kernel(*refs):
-        ins = refs[:group]
-        info_ref, info_t_ref, small_ref = refs[group : group + 3]
-        msg, x_out, w_out, r_out, cum_out, rate_out, tail_out, step_buf = refs[group + 3 :]
+        me_ref, ins, info_ref, info_t_ref, small_ref = refs[:5]
+        msg, x_out, w_out, r_out, cum_out, rate_out, tail_out, step_buf = refs[5:]
         for half, m, at in row_blocks(group):
             src = slice(half * STRETCH, (half + 1) * STRETCH)
-            x_out[at : at + STRETCH, :] = ins[m][src, 0:chans]
-            w_out[at : at + STRETCH, :] = ins[m][src, chans : chans + NSTATE]
-            r_out[at : at + STRETCH, :] = ins[m][src, chans + NSTATE : chans + 2 * NSTATE]
-            step_buf[at : at + STRETCH, :] = ins[m][src, chans + 2 * NSTATE :]
+            x_out[at : at + STRETCH, :] = ins[me_ref[0] ^ m, src, 0:chans]
+            w_out[at : at + STRETCH, :] = ins[me_ref[0] ^ m, src, chans : chans + NSTATE]
+            r_out[at : at + STRETCH, :] = ins[me_ref[0] ^ m, src, chans + NSTATE : chans + 2 * NSTATE]
+            step_buf[at : at + STRETCH, :] = ins[me_ref[0] ^ m, src, chans + 2 * NSTATE : chans + 2 * NSTATE + 128]
         row = lax.broadcasted_iota(jnp.int32, (128, 128), 0)
         col = lax.broadcasted_iota(jnp.int32, (128, 128), 1)
         pick = ((row == col) | (row == col + heads) | (row == col + 2 * heads)) & (col < heads)
@@ -174,18 +230,18 @@
             lanes = slice(128 * k, 128 * (k + 1))
             xw = (x_out[:, lanes].astype(F32) * pair_spread(scale, k)).astype(BF16)
             for q in range(2):
-                msg[q, 0:NSTATE, lanes] = mm(w_q[q], xw).astype(BF16)
+                msg[q * NSTATE : (q + 1) * NSTATE, lanes] = mm(w_q[q], xw).astype(BF16)
+            picked = jnp.zeros((EXTRA, 128), F32)
+            for q in range(2):
                 wide = pair_spread(jnp.broadcast_to(totals[q], (EXTRA, 128)), k)
-                hi, mid, low = split3(wide)
-                hi, mid, low = hi.astype(F32), mid.astype(F32), low.astype(F32)
-                msg[q, NSTATE:, lanes] = jnp.where(
-                    sub == 0, hi, jnp.where(sub == 1, mid, low)
-                ).astype(BF16)
+                for i, part in enumerate(split3(wide)):
+                    picked = jnp.where(sub == 3 * q + i, part.astype(F32), picked)
+            msg[2 * NSTATE :, lanes] = picked.astype(BF16)
 
     return call(
         kernel,
         [
-            ((2, NSTATE + EXTRA, chans), BF16),
+            ((2 * NSTATE + EXTRA, chans), BF16),
             ((rows, chans), BF16),
             ((rows, NSTATE), BF16),
             ((rows, NSTATE), BF16),
@@ -193,7 +249,8 @@
             ((rows, 128), F32),
             ((rows, 128), F32),
         ],
-        (*pieces, info, info_t, small),
+        (me, pieces, info, info_t, small),
+        smem=(0,),
         scratch=[pltpu.VMEM((rows, 128), BF16)],
         flops=4 * rows * NSTATE * chans,
         nbytes=6 * rows * chans,
@@ -246,34 +303,38 @@
         for ref in refs:
             for k in range(ref.shape[0]):
                 for c in range(2):
-                    term = weight(q, index) * ref[k, c, 0:NSTATE, :].astype(F32)
+                    term = weight(q, index) * ref[k, c * NSTATE : (c + 1) * NSTATE, :].astype(F32)
                     total = term if total is None else total + term
                     index += 1
         store(q, total)
 
 
-def mixed_rows(msgs, y, r, cum, gates, info, chan, before_in, ends, enter_mask, own_mask, own_end):
+def mixed_rows(me, msgs, y, r, cum, gates, info, chan, before_in, ends, enter_mask, own_mask, own_end):
     rows, chans = y.shape
     heads = chans // HEAD_CH
-    group = len(gates)
+    group = gates.shape[0]
     n_msg = len(msgs)
     classes = ends.shape[0]
+    gate_at, grad_at = slice(0, chans), slice(chans, 2 * chans)
 
     def kernel(*refs):
-        msg_refs = refs[:n_msg]
-        gate_refs = refs[n_msg : n_msg + group]
+        me_ref, msg_refs, gate_ref = refs[0], refs[1 : n_msg + 1], refs[n_msg + 1]
         (
             y_ref, r_ref, cum_ref, info_ref, chan_ref,
             before_ref, ends_ref, own_ref, own_end_ref, mask_ref,
             gated_ref, sums_ref, state_ref, enter_ref, leave_ref,
             tot, inner, cols,
-        ) = refs[n_msg + group :]
+        ) = refs[n_msg + 2 :]
         index = 0
         for ref in msg_refs:
             for k in range(ref.shape[0]):
+                part = ref[k, 2 * NSTATE :, :].astype(F32)
                 for c in range(2):
-                    part = ref[k, c, NSTATE : NSTATE + EXTRA, :].astype(F32)
-                    tot[index : index + 1, :] = part[0:1] + part[1:2] + part[2:3]
+                    tot[index : index + 1, :] = (
+                        part[3 * c : 3 * c + 1]
+                        + part[3 * c + 1 : 3 * c + 2]
+                        + part[3 * c + 2 : 3 * c + 3]
+                    )
                     index += 1
         exact = lax.Precision.HIGHEST
         totals = tot[...]
@@ -302,17 +363,17 @@
             here = slice(at, at + STRETCH)
             src = slice(half * STRETCH, (half + 1) * STRETCH)
             mixed = y_ref[here, :] + spread(jnp.exp(cum_ref[here, :]), heads) * inner[here, :]
-            gate = gate_refs[m][src, 0:chans].astype(F32)
+            gate = gate_ref[me_ref[0] ^ m, src, gate_at].astype(F32)
             gated = mixed * (gate / (1.0 + jnp.exp(-gate)))
             gated_ref[here, :] = gated
-            grad = gate_refs[m][src, chans : 2 * chans].astype(F32) * chan_ref[1:2, :]
+            grad = gate_ref[me_ref[0] ^ m, src, grad_at].astype(F32) * chan_ref[1:2, :]
             square = jnp.sum(gated * gated, axis=1, keepdims=True)
             cross = jnp.sum(grad * gated, axis=1, keepdims=True)
             cols[here, :] = jnp.where(lane == 0, square, jnp.where(lane == 1, cross, 0.0))
         sums_ref[...] = cols[...].T[0:8, :]
 
     args = (
-        *msgs, *gates, y, r, cum, info, chan, before_in, ends, own_mask, own_end, enter_mask
+        me, *msgs, gates, y, r, cum, info, chan, before_in, ends, own_mask, own_end, enter_mask
     )
     return call(
         kernel,
@@ -324,7 +385,7 @@
             ((8, chans), F32),
         ],
         args,
-        smem=(len(args) - 1,),
+        smem=(0, len(args) - 1),
         scratch=[
             pltpu.VMEM((classes, chans), F32),
             pltpu.VMEM((rows, chans), F32),
@@ -335,17 +396,17 @@
     )
 
 
-def mixed_cotangent(sums, gated, gates, r, cum, info_t, chan, total_chans):
+def mixed_cotangent(me, sums, gated, gates, r, cum, info_t, chan, total_chans):
     rows, chans = gated.shape
     heads = chans // HEAD_CH
-    group = len(gates)
+    group = gates.shape[0]
+    gate_at, grad_at = slice(0, chans), slice(chans, 2 * chans)
 
     def kernel(*refs):
-        gate_refs = refs[:group]
-        sums_refs, refs = refs[group : 2 * group], refs[2 * group :]
-        gated_ref, r_ref, cum_ref, info_t_ref, chan_ref, touch_ref, dmix_ref, lift_ref = refs[:8]
-        outs = refs[8 : 8 + group]
-        cols = refs[8 + group]
+        me_ref, gate_ref = refs[:2]
+        sums_refs, refs = refs[2 : 2 + group], refs[2 + group :]
+        gated_ref, r_ref, cum_ref, info_t_ref, chan_ref = refs[:5]
+        touch_ref, dmix_ref, lift_ref, inv_ref, cols = refs[5:]
         parts = [ref[...] for ref in sums_refs]
         both = jnp.concatenate(parts + [jnp.zeros((128 - 8 * group, rows), F32)], axis=0)
         cols[...] = both.T
@@ -362,26 +423,27 @@
             pull = inv * inv * inv * (cross / total_chans)
             gated = gated_ref[here, :]
             gain = chan_ref[1:2, :]
-            outs[m][src, :] = (gated * inv * gain).astype(BF16)
-            gate = gate_refs[m][src, 0:chans].astype(F32)
-            grad = gate_refs[m][src, chans : 2 * chans].astype(F32) * gain
+            inv_ref[here, :] = jnp.broadcast_to(inv, (STRETCH, 128))
+            gate = gate_ref[me_ref[0] ^ m, src, gate_at].astype(F32)
+            grad = gate_ref[me_ref[0] ^ m, src, grad_at].astype(F32) * gain
             dmix = (inv * grad - gated * pull) * (gate / (1.0 + jnp.exp(-gate)))
             dmix_ref[here, :] = dmix
             lift_ref[here, :] = (dmix * spread(jnp.exp(cum_ref[here, :]), heads)).astype(BF16)
         r_t = r_ref[...].astype(F32).T
         for q in range(2):
             left = (r_t * info_t_ref[4 + q : 5 + q, :]).astype(BF16)
-            touch_ref[q] = mm(left, lift_ref[...]).astype(BF16)
+            touch_ref[q * NSTATE : (q + 1) * NSTATE, :] = mm(left, lift_ref[...]).astype(BF16)
 
     return call(
         kernel,
         [
-            ((2, NSTATE, chans), BF16),
+            ((2 * NSTATE, chans), BF16),
             ((rows, chans), F32),
             ((rows, chans), BF16),
-            *[((2 * STRETCH, chans), BF16)] * group,
+            ((rows, 128), F32),
         ],
-        (*gates, *sums, gated, r, cum, info_t, chan),
+        (me, gates, *sums, gated, r, cum, info_t, chan),
+        smem=(0,),
         scratch=[pltpu.VMEM((rows, 128), F32)],
         flops=4 * rows * NSTATE * chans,
         nbytes=16 * rows * chans,
@@ -452,21 +514,21 @@
     )
 
 
-def final_grads(msgs, x, w, rate, tail, dx, dw, dr, dmix, info, chan, enter, leave, leave_mask):
+def final_grads(msgs, x, w, rate, tail, dx, dw, dr, dmix, gated, inv, info, chan, enter, leave, leave_mask):
     rows, chans = x.shape
     heads = chans // HEAD_CH
     group = rows // (2 * STRETCH)
     n_msg = len(msgs)
-    width = chans + 2 * NSTATE
+    width = 2 * chans + 2 * NSTATE
 
     def kernel(*refs):
         msg_refs = refs[:n_msg]
         (
-            x_ref, w_ref, rate_ref, tail_ref, dx_ref, dw_ref, dr_ref, dmix_ref, info_ref, chan_ref,
-            enter_ref, leave_ref, mask_ref,
-        ) = refs[n_msg : n_msg + 13]
-        outs = refs[n_msg + 13 : n_msg + 13 + group]
-        after, inner, xw = refs[n_msg + 13 + group :]
+            x_ref, w_ref, rate_ref, tail_ref, dx_ref, dw_ref, dr_ref, dmix_ref, gated_ref, inv_ref,
+            info_ref, chan_ref, enter_ref, leave_ref, mask_ref,
+        ) = refs[n_msg : n_msg + 15]
+        outs = refs[n_msg + 15 : n_msg + 15 + group]
+        after, inner, xw = refs[n_msg + 15 + group :]
 
         def weight(q, c):
             gap = enter_ref[c : c + 1, :] - leave_ref[q : q + 1, :]
@@ -491,7 +553,9 @@
             change = rates * (dx_ref[here, :] + tails * inner[here, :])
             change = change + chan_ref[0:1, :] * dmix_ref[here, :]
             outs[m][dst, 0:chans] = change.astype(BF16)
-            outs[m][dst, chans + NSTATE :] = dr_ref[here, :].astype(BF16)
+            outs[m][dst, chans + NSTATE : chans + 2 * NSTATE] = dr_ref[here, :].astype(BF16)
+            out = gated_ref[here, :] * inv_ref[here, 0:1] * chan_ref[1:2, :]
+            outs[m][dst, chans + 2 * NSTATE :] = out.astype(BF16)
         change = dw_ref[...] + mm_nt(xw[...], after[0:NSTATE, :]) * info_ref[:, 2:3]
         change = change + mm_nt(xw[...], after[NSTATE:, :]) * info_ref[:, 3:4]
         for half, m, at in row_blocks(group):
@@ -499,7 +563,7 @@
             outs[m][dst, chans : chans + NSTATE] = change[at : at + STRETCH].astype(BF16)
 
     args = (
-        *msgs, x, w, rate, tail, dx, dw, dr, dmix, info, chan, enter, leave, leave_mask
+        *msgs, x, w, rate, tail, dx, dw, dr, dmix, gated, inv, info, chan, enter, leave, leave_mask
     )
     return call(
         kernel,
@@ -519,8 +583,8 @@
 def attention(blocks, own_blocks, pieces, queries, grads, kv_heads):
     rows = queries.shape[0]
     per_kv = queries.shape[1] // AHD // kv_heads
-    group, units = len(pieces), pieces[0].shape[0]
-    tokens = group * units * rows
+    n_pieces = len(pieces)
+    tokens = rows * sum(piece.shape[0] for piece in pieces)
     half_width = kv_heads * AHD
     scale = AHD ** (-0.5)
     chunk = min(KEY_CHUNK, tokens)
@@ -528,61 +592,90 @@
 
     def kernel(*refs):
         blocks_ref, own_ref = refs[:2]
-        piece_refs = refs[2 : 2 + group]
-        q_ref, g_ref, out_ref, dq_ref, kv, scores = refs[2 + group :]
-        for m in range(group):
-            for u in range(units):
+        piece_refs = refs[2 : 2 + n_pieces]
+        q_ref, g_ref, out_ref, dq_ref, kv, scores, q_all, g_all = refs[2 + n_pieces :]
+        index = 0
+        for ref in piece_refs:
+            for u in range(ref.shape[0]):
                 for half in range(2):
-                    at = pl.ds(pl.multiple_of(blocks_ref[half, m * units + u] * STRETCH, 64), STRETCH)
-                    kv[at, :] = piece_refs[m][u, half * STRETCH : (half + 1) * STRETCH, :]
+                    at = pl.ds(pl.multiple_of(blocks_ref[half, index] * STRETCH, 64), STRETCH)
+                    kv[at, :] = ref[u, half * STRETCH : (half + 1) * STRETCH, :]
+                index += 1
         offset = lax.broadcasted_iota(jnp.int32, (tall, chunk), 0) % STRETCH
         column = lax.broadcasted_iota(jnp.int32, (tall, chunk), 1)
+        every = range(kv_heads)
+        k_at = [slice(g * AHD, (g + 1) * AHD) for g in every]
+        v_at = [slice(half_width + g * AHD, half_width + (g + 1) * AHD) for g in every]
+
+        def stacked(ref, src, g):
+            parts = [ref[src, (g * per_kv + i) * AHD : (g * per_kv + i + 1) * AHD] for i in range(per_kv)]
+            return jnp.concatenate(parts, axis=0)
+
+        def keys_of(c):
+            return pl.ds(pl.multiple_of(c * chunk, chunk), chunk)
+
         for half in range(2):
             block = own_ref[half]
             src = slice(half * STRETCH, (half + 1) * STRETCH)
             steps = (block * STRETCH) // chunk + 1
             reach = offset + block * STRETCH
-            for g in range(kv_heads):
-                k_at = slice(g * AHD, (g + 1) * AHD)
-                v_at = slice(half_width + g * AHD, half_width + (g + 1) * AHD)
-                heads = [slice((g * per_kv + i) * AHD, (g * per_kv + i + 1) * AHD) for i in range(per_kv)]
-                query = jnp.concatenate([q_ref[src, at] for at in heads], axis=0)
-                grad = jnp.concatenate([g_ref[src, at] for at in heads], axis=0)
-
-                def keys_of(c):
-                    return pl.ds(pl.multiple_of(c * chunk, chunk), chunk)
-
-                def first(c, peak):
-                    value = mm_nt(query, kv[keys_of(c), k_at]) * scale
-                    value = jnp.where(column + c * chunk <= reach, value, NEG_FILL)
-                    scores[c] = value
-                    return jnp.maximum(peak, jnp.max(value, axis=1, keepdims=True))
-
-                peak = lax.fori_loop(0, steps, first, jnp.full((tall, 1), NEG_FILL, F32))
-
-                def second(c, carry):
-                    total, out = carry
-                    value = jnp.exp(scores[c] - peak)
-                    scores[c] = value
-                    out = out + mm(value.astype(BF16), kv[keys_of(c), v_at])
-                    return total + jnp.sum(value, axis=1, keepdims=True), out
-
-                total, out = lax.fori_loop(
-                    0, steps, second, (jnp.zeros((tall, 1), F32), jnp.zeros((tall, AHD), F32))
+            for g in every:
+                q_all[g] = stacked(q_ref, src, g)
+                g_all[g] = stacked(g_ref, src, g)
+
+            def first(c, peaks):
+                kept = column + c * chunk <= reach
+                new = []
+                for g in every:
+                    value = mm_nt(q_all[g], kv[keys_of(c), k_at[g]]) * (scale * LOG2_E)
+                    value = jnp.where(kept, value, NEG_FILL)
+                    scores[g, c] = value
+                    new.append(jnp.maximum(peaks[g], jnp.max(value, axis=1, keepdims=True)))
+                return tuple(new)
+
+            peaks = lax.fori_loop(
+                0, steps, first, tuple(jnp.full((tall, 1), NEG_FILL, F32) for _ in every)
+            )
+
+            def second(c, carry):
+                new = []
+                for g in every:
+                    total, out = carry[g]
+                    value = jnp.exp2(scores[g, c] - peaks[g])
+                    scores[g, c] = value
+                    out = out + mm(value.astype(BF16), kv[keys_of(c), v_at[g]])
+                    new.append((total + jnp.sum(value, axis=1, keepdims=True), out))
+                return tuple(new)
+
+            empty = (jnp.zeros((tall, 1), F32), jnp.zeros((tall, AHD), F32))
+            done = lax.fori_loop(0, steps, second, tuple(empty for _ in every))
+            deltas = []
+            for g in every:
+                total, out = done[g]
+                out = (out / total).astype(BF16)
+                deltas.append(
+                    jnp.sum(g_all[g].astype(F32) * out.astype(F32), axis=1, keepdims=True)
                 )
-                out = (out / total).astype(BF16)
-                delta = jnp.sum(grad.astype(F32) * out.astype(F32), axis=1, keepdims=True)
-
-                def third(c, acc):
-                    slope = mm_nt(grad, kv[keys_of(c), v_at]) - delta
-                    change = (scores[c] * slope).astype(BF16)
-                    return acc + mm(change, kv[keys_of(c), k_at])
-
-                acc = lax.fori_loop(0, steps, third, jnp.zeros((tall, AHD), F32))
-                acc = (acc * (scale / total)).astype(BF16)
-                for i, at in enumerate(heads):
+                for i in range(per_kv):
+                    at = slice((g * per_kv + i) * AHD, (g * per_kv + i + 1) * AHD)
                     out_ref[src, at] = out[i * STRETCH : (i + 1) * STRETCH]
-                    dq_ref[src, at] = acc[i * STRETCH : (i + 1) * STRETCH]
+
+            def third(c, carry):
+                new = []
+                for g in every:
+                    slope = mm_nt(g_all[g], kv[keys_of(c), v_at[g]]) - deltas[g]
+                    change = (scores[g, c] * slope).astype(BF16)
+                    new.append(carry[g] + mm(change, kv[keys_of(c), k_at[g]]))
+                return tuple(new)
+
+            changes = lax.fori_loop(
+                0, steps, third, tuple(jnp.zeros((tall, AHD), F32) for _ in every)
+            )
+            for g in every:
+                change = (changes[g] * (scale / done[g][0])).astype(BF16)
+                for i in range(per_kv):
+                    at = slice((g * per_kv + i) * AHD, (g * per_kv + i + 1) * AHD)
+                    dq_ref[src, at] = change[i * STRETCH : (i + 1) * STRETCH]
 
     return call(
         kernel,
@@ -591,8 +684,11 @@
         smem=(0, 1),
         scratch=[
             pltpu.VMEM((tokens, 2 * half_width), BF16),
-            pltpu.VMEM((tokens // chunk, tall, chunk), F32),
+            pltpu.VMEM((kv_heads, tokens // chunk, tall, chunk), F32),
+            pltpu.VMEM((kv_heads, tall, AHD), BF16),
+            pltpu.VMEM((kv_heads, tall, AHD), BF16),
         ],
+        mib=24,
         flops=10 * queries.size * tokens,
         nbytes=4 * tokens * half_width,
     )
@@ -628,19 +724,19 @@
     turn = stretch_order[0]
     last = 2 * ctx_count
 
+    def to_place(value, m):
+        pairs = [(i, (i // group) * group + ((i % group) ^ m)) for i in range(ctx_count)]
+        return lax.ppermute(value, "ctx", pairs)
+
     def in_plane(values):
-        moved = [values[0]]
-        for m in range(1, group):
-            pairs = [(i, (i // group) * group + ((i % group) ^ m)) for i in range(ctx_count)]
-            moved.append(lax.ppermute(values[m], "ctx", pairs))
-        return moved
+        return [values[0]] + [to_place(values[m], m) for m in range(1, group)]
 
     def across(value):
-        moved = [value]
-        for m in range(1, units):
+        moved = []
+        for m in range(units - 1, 0, -1):
             pairs = [(i, ((i // group) ^ m) * group + i % group) for i in range(ctx_count)]
             moved.append(lax.ppermute(value, "ctx", pairs))
-        return moved
+        return [value] + moved[::-1]
 
     def all_units(value):
         if by_permute:
@@ -650,12 +746,16 @@
         sets = [[u * group + j for u in range(units)] for j in range(group)]
         return [lax.all_gather(value, "ctx", axis=0, axis_index_groups=sets)]
 
-    own_kv = jnp.concatenate([attn_keys, attn_values], axis=1)
+    own_kv, packed, gates = pack_forward(
+        mamba_input, state_write, state_read, step_raw, gate_input, mamba_grad, attn_keys,
+        attn_values, group,
+    )
     kv_units = all_units(own_kv)
-
-    packed = pack_forward(me, mamba_input, state_write, state_read, step_raw, group)
-    forward_pieces = in_plane(packed)
-    gates = in_plane(pack_gate(me, gate_input, mamba_grad, group))
+    forward_pieces = packed
+    if group > 1:
+        planes = [[u * group + j for j in range(group)] for u in range(units)]
+        forward_pieces = lax.all_to_all(packed, "ctx", 0, 0, axis_index_groups=planes, tiled=True)
+        gates = lax.all_to_all(after(gates, forward_pieces), "ctx", 0, 0, axis_index_groups=planes, tiled=True)
 
     unit_ids = jnp.arange(units, dtype=jnp.int32)
     if by_permute:
@@ -725,42 +825,60 @@
     gain = lax.dynamic_slice(norm_gain, (my_place * chans,), (chans,))
     chan = jnp.pad(jnp.stack([skip, gain]), ((0, 6), (0, 0)))
 
-    msg, x, w, r, cum, rate, tail = outgoing_state(forward_pieces, info, info_t, small, chans)
+    own_pair = (my_index + turn) % ctx_count
+    pair_table = (unit_ids[None, :] * group + place_ids[:, None] + turn) % ctx_count
+    pair_table = pair_table.reshape(1, -1)
+    blocks = jnp.concatenate([pair_table, last - 1 - pair_table], axis=0)
+    own_blocks = jnp.stack([own_pair, last - 1 - own_pair])
+    tables = (
+        info, info_t, small, chan, before_in, ends, enter_mask, leave_mask, own_mask, own_end,
+        blocks, own_blocks,
+    )
+    small_group = group == 4 and units == 4 and by_permute
+    forward_pieces, tables = after((forward_pieces, tables), kv_units)
+    (
+        info, info_t, small, chan, before_in, ends, enter_mask, leave_mask, own_mask, own_end,
+        blocks, own_blocks,
+    ) = tables
+
+    msg, x, w, r, cum, rate, tail = outgoing_state(me, forward_pieces, info, info_t, small, chans)
     msgs = all_units(msg)
-
-    kv_all = kv_units[0] if len(kv_units) == 1 else jnp.concatenate(kv_units, axis=0)
-    kv_pieces = in_plane([kv_all] * group)
-
     y = intra_forward(x, w, r, cum, rate, info, info_t, chan)
+    if small_group:
+        near = stack_parts(after(kv_units, (gates, y)))
+        beside, above = to_place(near, 1), to_place(near, 2)
+        x_late = x
+    else:
+        kv_pieces = in_plane([jnp.concatenate(kv_units, axis=0)] * group)
+        x_late = x
     gated, sums, state, enter, leave = mixed_rows(
-        msgs, y, r, cum, gates, info, chan, before_in, ends, enter_mask, own_mask, own_end
+        me, msgs, y, r, cum, gates, info, chan, before_in, ends, enter_mask, own_mask, own_end
     )
     if tp_count == 2:
         sums = sums + lax.ppermute(sums, "tp", [(0, 1), (1, 0)])
     else:
         sums = lax.psum(sums, "tp")
     sums = in_plane([sums] * group)
-    touch, dmix, lift, *out_pieces = mixed_cotangent(
-        sums, gated, gates, r, cum, info_t, chan, float(mamba_input.shape[1] * tp_count)
+    touch, dmix, lift, inv = mixed_cotangent(
+        me, sums, gated, gates, r, cum, info_t, chan, float(mamba_input.shape[1] * tp_count)
     )
     touches = all_units(touch)
-    (mamba_output,) = unpack(me, in_plane(out_pieces), (chans,))
+    if small_group:
+        beside, above = after((beside, above), touch)
+        kv_pieces = [near, beside, above, to_place(beside[:2], 2), to_place(above[2:], 1)]
     dx, dw, dr = intra_backward(x, w, r, cum, rate, dmix, lift, state, info, info_t)
 
-    pair_table = (unit_ids[None, :] * group + place_ids[:, None] + turn) % ctx_count
-    pair_table = pair_table.reshape(1, -1)
-    blocks = jnp.concatenate([pair_table, last - 1 - pair_table], axis=0)
     attn_output, query_grad = attention(
-        blocks, blocks[:, 0] if by_permute else jnp.stack(
-            [(my_index + turn) % ctx_count, last - 1 - (my_index + turn) % ctx_count]
-        ),
-        kv_pieces, attn_queries, attn_grad, kv_heads,
-    )
-
+        blocks, own_blocks, kv_pieces, attn_queries, attn_grad, kv_heads
+    )
+
+    touches, attn_output, query_grad = lax.optimization_barrier((touches, attn_output, query_grad))
     finals = final_grads(
-        touches, x, w, rate, tail, dx, dw, dr, dmix, info, chan, enter, leave, leave_mask
-    )
-    input_grad, write_grad, read_grad = unpack(me, in_plane(finals), (chans, NSTATE, NSTATE))
+        touches, x, w, rate, tail, dx, dw, dr, dmix, gated, inv, info, chan, enter, leave, leave_mask
+    )
+    input_grad, write_grad, read_grad, mamba_output = unpack(
+        me, in_plane(finals), (chans, NSTATE, NSTATE, chans)
+    )
     return (attn_output, query_grad, mamba_output, input_grad, write_grad, read_grad)
 
 

time: 177 us -> 135 us (0.76); the launches traced: 174 us -> 135 us
  waiting for transfers between devices: 69.8 us -> 50.1 us
  local copies, waits for them, and re-layouts: 24.5 us -> 14.5 us
  Pallas kernels: 43.8 us -> 35.6 us
  starting transfers between devices: 31.4 us -> 29 us
    ppermute x9, waiting for transfers between devices: 39.1 us -> 22.4 us  [across(): moved.append(lax.ppermute(value, 'ctx', pairs))]
    pallas_call x11 -> x9, Pallas kernels: 43.8 us -> 32 us  [call(): pl.pallas_call(fn, out_shape=tuple((jax.ShapeDtypeStruct(s, d) for s, d i...]
    ppermute x18 -> x10, waiting for transfers between devices: 29.6 us -> 19 us  [to_place(): return lax.ppermute(value, 'ctx', pairs)]
    all_to_all x0 -> x2, waiting for transfers between devices: none -> 7.6 us  [the longest x1 5.75 us: body(): lax.all_to_all(packed, 'ctx', 0, 0, axis_index_groups=planes, tiled=True)]
    all_to_all x0 -> x2, starting transfers between devices: none -> 7.23 us  [the longest x1 3.72 us: body(): lax.all_to_all(packed, 'ctx', 0, 0, axis_index_groups=planes, tiled=True)]
    unnamed x100 -> x59, local copies, waits for them, and re-layouts: 19.8 us -> 12.6 us
    ppermute x18 -> x10, starting transfers between devices: 17.6 us -> 10.6 us  [to_place(): return lax.ppermute(value, 'ctx', pairs)]
    pallas_call x0 -> x1, Pallas kernels: none -> 3.58 us  [move(): pl.pallas_call(fn, out_shape=tuple((jax.ShapeDtypeStruct(s, d) for s, d i...]
  transfers between devices with their start and end apart: 28 -> 22, of which waited for: 14 -> 15; matrix products, arithmetic and copies ran while one was open for 5% -> 5% of each run, Pallas kernels for 11% -> 21%
where the time goes in v2:
time: 135 us
  waiting for transfers between devices  50.1 us (37%)
  Pallas kernels  35.6 us (26%)
  starting transfers between devices  29 us (21%)
  local copies, waits for them, and re-layouts  14.5 us (11%)
  other arithmetic  4.48 us (3%)
    pallas_call x9, Pallas kernels, call(): pl.pallas_call(fn, out_shape=tuple((jax.ShapeDtypeStruct(s, d) for s, d i...  32 us
    ppermute x9, waiting for transfers between devices, across(): moved.append(lax.ppermute(value, 'ctx', pairs))  22.4 us
    ppermute x10, waiting for transfers between devices, to_place(): return lax.ppermute(value, 'ctx', pairs)  19 us
    unnamed x59, local copies, waits for them, and re-layouts  12.6 us
    ppermute x9, starting transfers between devices, across(): moved.append(lax.ppermute(value, 'ctx', pairs))  11.1 us
    ppermute x10, starting transfers between devices, to_place(): return lax.ppermute(value, 'ctx', pairs)  10.6 us
    all_to_all x1, waiting for transfers between devices, body(): lax.all_to_all(packed, 'ctx', 0, 0, axis_index_groups=planes, tiled=True)  5.75 us
    all_to_all x1, starting transfers between devices, body(): lax.all_to_all(packed, 'ctx', 0, 0, axis_index_groups=planes, tiled=True)  3.72 us
  transfers between devices with their start and end apart: 22, of which 15 were waited for; matrix products, arithmetic and copies ran while one was open for 5% of the time, Pallas kernels for 21%

profile of v2, /device:TPU:8, one launch (start us, length us, event | category | flops | bytes accessed | tf_op | source)
XLA Modules:
  0.0 134.7 jit_solution(1053364903775003060)
XLA Ops:
  0.6 1.4 %copy.21.step_ref = f32[128,32]{1,0:T(8,128)} copy(f32[128,32]{0,1:T(8,128)} %param.23) | data formatting | bytes 32768 | tf_op args[9]
  2.1 3.6 %shard_map.181 = (bf16[128,1024]{1,0:T(8,128)(2,1)}, bf16[4,128,896]{2,1,0:T(8,128)(2,1)}, bf16[4,128,1024]{2,1,0:T(8,128)(2,1)}) custom-call(f32[128,32]{1,0:T(8,128)} %copy.21.step_ref, bf16[128,2048]{1,0:T(8,128)(2,1)} %refs_0_.1, bf16[128,512]{1,0:T(8,128)(2,1)} %refs_1_.1, bf16[128,512]{1,0:T(8,128)(2,1)} %refs_2_.1, bf16[128,2048]{1,0:T(8,128)(2,1)} %refs_3_.1, ...), custom_call_target="tpu_custom_call" | custom-call | bytes 1024 | tf_op jit(solution)/shard_map/pallas_call | solution.py:142
  5.7 3.0 %collective-permute-start.1 = (bf16[128,1024]{1,0:T(8,128)(2,1)}, bf16[128,1024]{1,0:T(8,128)(2,1)S(1)}, u32[]{:S(2)}, u32[]{:S(2)}) collective-permute-start(bf16[128,1024]{1,0:T(8,128)(2,1)} %get-tuple-element.67), channel_id=1, source_target_pairs={{0,16},{2,18},{4,20},{6,22},{8,24},{10,26},{12,28},{14,30},{16,0},... | collective-permute-start | bytes 786440 | tf_op jit(solution)/shard_map/ppermute | solution.py:738
  9.2 3.7 %all-to-all-start = ((bf16[4,128,896]{2,1,0:T(8,128)(2,1)}), bf16[4,128,896]{2,1,0:T(8,128)(2,1)S(1)}, u32[]{:S(2)}, u32[]{:S(2)}) async-start(bf16[4,128,896]{2,1,0:T(8,128)(2,1)} %get-tuple-element.65), calls=%async_computation | async-start | bytes 1835008 | tf_op jit(solution)/shard_map/all_to_all | solution.py:757
  12.9 0.7 copy-done.26
  14.2 0.6 pad_add_fusion.2.refs_0_
  14.9 0.6 copy-done.27
  15.8 0.6 copy-done.28
  16.6 0.8 dynamic_slice.11
  17.4 0.7 broadcast_compare_fusion
  18.0 0.6 pad_convert_fusion.refs_14_
  18.6 5.7 %all-to-all-done.refs_1_ = bf16[4,128,896]{2,1,0:T(8,128)(2,1)S(1)} async-done(((bf16[4,128,896]{2,1,0:T(8,128)(2,1)}), bf16[4,128,896]{2,1,0:T(8,128)(2,1)S(1)}, u32[]{:S(2)}, u32[]{:S(2)}) %all-to-all-start) | async-done | bytes 917536 | tf_op jit(solution)/shard_map/all_to_all | solution.py:757
  24.4 3.5 %all-to-all-start.1 = ((bf16[4,128,1024]{2,1,0:T(8,128)(2,1)}), bf16[4,128,1024]{2,1,0:T(8,128)(2,1)S(1)}, u32[]{:S(2)}, u32[]{:S(2)}) async-start(bf16[4,128,1024]{2,1,0:T(8,128)(2,1)} %get-tuple-element.66), calls=%async_computation.1 | async-start | bytes 2097152 | tf_op jit(solution)/shard_map/all_to_all | solution.py:758
  27.9 0.7 compare_convert_fusion
  28.7 0.6 pad_add_fusion.5.refs_1_
  29.2 0.6 concatenate.11.refs_13_
  29.8 0.7 fusion.refs_2_.info_ref.refs_9_.refs_14_
  30.6 0.7 copy-done.9
  31.3 0.7 copy-done.11
  32.1 0.7 copy-done.13
  32.8 2.0 %shard_map.182 = (bf16[272,512]{1,0:T(8,128)(2,1)S(1)}, bf16[512,512]{1,0:T(8,128)(2,1)S(1)}, bf16[512,128]{1,0:T(8,128)(2,1)S(1)}, bf16[512,128]{1,0:T(8,128)(2...) custom-call(s32[1]{0:T(128)} %bitcast.refs_0_.me_ref, ...), custom_call_target="tpu_custom_call" | custom-call | flops 134217 | bytes 1572 | tf_op jit(solution)/shard_map/pallas_call | solution.py:59
  34.8 0.7 copy-done.6
  35.5 0.7 copy-done.15
  36.2 2.2 %shard_map.183.refs_6_ = f32[512,512]{1,0:T(8,128)S(1)} custom-call(bf16[512,512]{1,0:T(8,128)(2,1)S(1)} %get-tuple-element.73.x_ref.refs_4_, bf16[512,128]{1,0:T(8,128)(2,1)S(1)} %get-tuple-element.74.w_ref.refs_5_, bf16[512,128]{1,0:T(8,128)(2,1)S(1)} %get-tuple-element.75.r_ref.refs_7_, f32[512,128]{1,0:T(8,128)S(1)} %get-tuple-element.76.cum_ref.refs_8_, ...), custom_call_target="tpu_custom_call" | custom-call | flops 536870 | bytes 2097 | tf_op jit(solution)/shard_map/pallas_call | solution.py:59
  38.4 0.6 copy-done
  39.1 1.9 %all-to-all-done.1.refs_5_.refs_1_ = bf16[4,128,1024]{2,1,0:T(8,128)(2,1)S(1)} async-done(((bf16[4,128,1024]{2,1,0:T(8,128)(2,1)}), bf16[4,128,1024]{2,1,0:T(8,128)(2,1)S(1)}, u32[]{:S(2)}, u32[]{:S(2)}) %all-to-all-start.1) | async-done | bytes 1048608 | tf_op jit(solution)/shard_map/all_to_all | solution.py:758
  40.9 0.9 copy-done.8
  41.9 0.9 copy-done.10
  42.8 0.9 copy-done.12
  43.8 0.9 copy-done.14
  44.8 1.5 %collective-permute-start.13 = (bf16[4,128,1024]{2,1,0:T(8,128)(2,1)S(1)}, bf16[4,128,1024]{2,1,0:T(8,128)(2,1)S(1)}, u32[]{:S(2)}, u32[]{:S(2)}) collective-permute-start(bf16[4,128,1024]{2,1,0:T(8,128)(2,1)S(1)} %shard_map.186.refs_2_), channel_id=1, source_target_pairs={{0,2},{2,0},{4,6},{6,4},{8,10},{10,8},{12,14},{14,12},{16,18},{18,... | collective-permute-start | bytes 3145736 | tf_op jit(solution)/shard_map/ppermute | solution.py:729
  46.3 0.6 collective-permute-start.14
  46.9 1.4 %collective-permute-start.3 = (bf16[272,512]{1,0:T(8,128)(2,1)S(1)}, bf16[272,512]{1,0:T(8,128)(2,1)S(1)}, u32[]{:S(2)}, u32[]{:S(2)}) collective-permute-start(bf16[272,512]{1,0:T(8,128)(2,1)S(1)} %copy-done.7), channel_id=1, source_target_pairs={{0,8},{2,10},{4,12},{6,14},{8,0},{10,2},{12,4},{14,6},{16,24},{18,... | collective-permute-start | bytes 835592 | tf_op jit(solution)/shard_map/ppermute | solution.py:738
  48.3 2.2 %collective-permute-start.4 = (bf16[272,512]{1,0:T(8,128)(2,1)S(1)}, bf16[272,512]{1,0:T(8,128)(2,1)S(1)}, u32[]{:S(2)}, u32[]{:S(2)}) collective-permute-start(bf16[272,512]{1,0:T(8,128)(2,1)S(1)} %copy-done.7), channel_id=1, source_target_pairs={{0,16},{2,18},{4,20},{6,22},{8,24},{10,26},{12,28},{14,30},{16,0},... | collective-permute-start | bytes 835592 | tf_op jit(solution)/shard_map/ppermute | solution.py:738
  50.4 0.5 collective-permute-start.5
  50.9 5.4 %collective-permute-done.3 = bf16[272,512]{1,0:T(8,128)(2,1)S(1)} collective-permute-done((bf16[272,512]{1,0:T(8,128)(2,1)S(1)}, bf16[272,512]{1,0:T(8,128)(2,1)S(1)}, u32[]{:S(2)}, u32[]{:S(2)}) %collective-permute-start.3) | collective-permute-done | bytes 278560 | tf_op jit(solution)/shard_map/ppermute | solution.py:738
  56.4 12.1 %collective-permute-done.4 = bf16[272,512]{1,0:T(8,128)(2,1)S(1)} collective-permute-done((bf16[272,512]{1,0:T(8,128)(2,1)S(1)}, bf16[272,512]{1,0:T(8,128)(2,1)S(1)}, u32[]{:S(2)}, u32[]{:S(2)}) %collective-permute-start.4) | collective-permute-done | bytes 278560 | tf_op jit(solution)/shard_map/ppermute | solution.py:738
  68.5 4.8 %collective-permute-done.5 = bf16[272,512]{1,0:T(8,128)(2,1)S(1)} collective-permute-done((bf16[272,512]{1,0:T(8,128)(2,1)S(1)}, bf16[272,512]{1,0:T(8,128)(2,1)S(1)}, u32[]{:S(2)}, u32[]{:S(2)}) %collective-permute-start.5) | collective-permute-done | bytes 278560 | tf_op jit(solution)/shard_map/ppermute | solution.py:738
  73.3 0.7 copy-done.22
  73.9 2.7 %shard_map.184 = (f32[512,512]{1,0:T(8,128)S(1)}, f32[8,512]{1,0:T(8,128)S(1)}, bf16[256,512]{1,0:T(8,128)(2,1)S(1)}, f32[8,512]{1,0:T(8,128)S(1)}, f32[8,512]{1,0:T(8,128)S(1)}) custom-call(s32[1]{0:T(128)} %bitcast.refs_0_.me_ref, bf16[1,272,512]{2,1,0:T(8,128)(2,1)S(1)} %bitcast.24, bf16[1,272,512]{2,1,0:T(8,128)(2,1)S(1)} %bitcast.25, ...), custom_call_target="tpu_custom_call" | custom-call | flops 268435 | bytes 4194 | tf_op jit(solution)/shard_map/pallas_call | solution.py:59
  76.7 1.2 collective-permute-done.6
  77.9 1.3 collective-permute-start.7
  79.1 1.4 %collective-permute-start.8 = (f32[8,512]{1,0:T(8,128)S(1)}, f32[8,512]{1,0:T(8,128)S(1)}, u32[]{:S(2)}, u32[]{:S(2)}) collective-permute-start(f32[8,512]{1,0:T(8,128)S(1)} %add.334.refs_2_), channel_id=1, source_target_pairs={{0,4},{2,6},{4,0},{6,2},{8,12},{10,14},{12,8},{14,10},{16,20},{18,... | collective-permute-start | bytes 49160 | tf_op jit(solution)/shard_map/ppermute | solution.py:729
  80.5 0.8 collective-permute-start.9
  81.6 1.3 collective-permute-done.8.refs_4_
  82.9 2.3 %collective-permute-done.9.refs_5_ = f32[8,512]{1,0:T(8,128)S(1)} collective-permute-done((f32[8,512]{1,0:T(8,128)S(1)}, f32[8,512]{1,0:T(8,128)S(1)}, u32[]{:S(2)}, u32[]{:S(2)}) %collective-permute-start.9) | collective-permute-done | bytes 16416 | tf_op jit(solution)/shard_map/ppermute | solution.py:729
  85.2 2.4 %shard_map.185 = (bf16[256,512]{1,0:T(8,128)(2,1)S(1)}, f32[512,512]{1,0:T(8,128)S(1)}, bf16[512,512]{1,0:T(8,128)(2,1)S(1)}, f32[512,128]{1,0:T(8,128)S(1)}) custom-call(s32[1]{0:T(128)} %bitcast.refs_0_.me_ref, bf16[4,128,1024]{2,1,0:T(8,128)(2,1)S(1)} %all-to-all-done.1.refs_5_.refs_1_, f32[8,512]{1,0:T(8,128)S(1)} %add.334.refs_2_, ...), custom_call_target="tpu_custom_call" | custom-call | flops 134217 | bytes 4194 | tf_op jit(solution)/shard_map/pallas_call | solution.py:59
  87.7 0.7 collective-permute-start.15
  88.3 0.8 collective-permute-start.16
  89.2 2.9 %collective-permute-start.11 = (bf16[256,512]{1,0:T(8,128)(2,1)S(1)}, bf16[256,512]{1,0:T(8,128)(2,1)S(1)}, u32[]{:S(2)}, u32[]{:S(2)}) collective-permute-start(bf16[256,512]{1,0:T(8,128)(2,1)S(1)} %get-tuple-element.86), channel_id=1, source_target_pairs={{0,16},{2,18},{4,20},{6,22},{8,24},{10,26},{12,28},{14,30},{16,0},... | collective-permute-start | bytes 786440 | tf_op jit(solution)/shard_map/ppermute | solution.py:738
  92.1 0.6 collective-permute-start.12
  92.7 3.8 %shard_map.188 = (f32[512,512]{1,0:T(8,128)S(1)}, f32[512,128]{1,0:T(8,128)S(1)}, f32[512,128]{1,0:T(8,128)S(1)}) custom-call(bf16[512,512]{1,0:T(8,128)(2,1)S(1)} %get-tuple-element.73.x_ref.refs_4_, bf16[512,128]{1,0:T(8,128)(2,1)S(1)} %copy-done.1, bf16[512,128]{1,0:T(8,128)(2,1)S(1)} %get-tuple-element.75.r_ref.refs_7_, ...), custom_call_target="tpu_custom_call" | custom-call | flops 1073741 | bytes 4194 | tf_op jit(solution)/shard_map/pallas_call | solution.py:59
  96.6 3.4 %collective-permute-done.15.refs_5_ = bf16[2,128,1024]{2,1,0:T(8,128)(2,1)S(1)} collective-permute-done((bf16[2,128,1024]{2,1,0:T(8,128)(2,1)S(1)}, bf16[2,128,1024]{2,1,0:T(8,128)(2,1)S(1)}, u32[]{:S(2)}, u32[]{:S(2)}) %collective-permute-start.15) | collective-permute-done | bytes 524320 | tf_op jit(solution)/shard_map/ppermute | solution.py:729
  100.0 0.5 collective-permute-done.16.refs_6_
  100.5 14.8 %shard_map.187 = (bf16[128,2048]{1,0:T(8,128)(2,1)}, bf16[128,2048]{1,0:T(8,128)(2,1)}) custom-call(s32[2,16]{1,0:T(2,128)S(1)} %copy-done.23, s32[2]{0:T(128)S(1)} %copy-done.25, bf16[4,128,1024]{2,1,0:T(8,128)(2,1)S(1)} %shard_map.186.refs_2_, bf16[4,128,1024]{2,1,0:T(8,128)(2,1)S(1)} %collective-permute-done.13.refs_3_, ...), custom_call_target="tpu_custom_call" | custom-call | flops 5368709 | bytes 4194 | tf_op jit(solution)/shard_map/pallas_call | solution.py:59
  115.3 0.7 copy-done.24
  116.0 2.8 %shard_map.189 = (bf16[128,1280]{1,0:T(8,128)(2,1)S(1)}, bf16[128,1280]{1,0:T(8,128)(2,1)S(1)}, bf16[128,1280]{1,0:T(8,128)(2,1)S(1)}, bf16[128,1280]{1,0:T(8,128)(2,1)S(1)}) custom-call(bf16[1,256,512]{2,1,0:T(8,128)(2,1)S(1)} %bitcast.32, bf16[1,256,512]{2,1,0:T(8,128)(2,1)S(1)} %bitcast.33, bf16[1,256,512]{2,1,0:T(8,128)(2,1)S(1)} %bitcast.34, ...), custom_call_target="tpu_custom_call" | custom-call | flops 268435 | bytes 4194 | tf_op jit(solution)/shard_map/pallas_call | solution.py:59
  118.8 0.8 collective-permute-start.17
  119.6 1.2 collective-permute-start.18
  120.7 1.6 %collective-permute-start.19 = (bf16[128,1280]{1,0:T(8,128)(2,1)S(1)}, bf16[128,1280]{1,0:T(8,128)(2,1)S(1)}, u32[]{:S(2)}, u32[]{:S(2)}) collective-permute-start(bf16[128,1280]{1,0:T(8,128)(2,1)S(1)} %get-tuple-element.117), channel_id=1, source_target_pairs={{0,6},{2,4},{4,2},{6,0},{8,14},{10,12},{12,10},{14,8},{16,22},{18,... | collective-permute-start | bytes 983048 | tf_op jit(solution)/shard_map/ppermute | solution.py:729
  122.4 6.9 %collective-permute-done.17.refs_1_ = bf16[128,1280]{1,0:T(8,128)(2,1)S(1)} collective-permute-done((bf16[128,1280]{1,0:T(8,128)(2,1)S(1)}, bf16[128,1280]{1,0:T(8,128)(2,1)S(1)}, u32[]{:S(2)}, u32[]{:S(2)}) %collective-permute-start.17) | collective-permute-done | bytes 327712 | tf_op jit(solution)/shard_map/ppermute | solution.py:729
  129.3 0.8 collective-permute-done.18.refs_2_
  130.1 3.5 %collective-permute-done.19.refs_3_ = bf16[128,1280]{1,0:T(8,128)(2,1)S(1)} collective-permute-done((bf16[128,1280]{1,0:T(8,128)(2,1)S(1)}, bf16[128,1280]{1,0:T(8,128)(2,1)S(1)}, u32[]{:S(2)}, u32[]{:S(2)}) %collective-permute-start.19) | collective-permute-done | bytes 327712 | tf_op jit(solution)/shard_map/ppermute | solution.py:729
  133.6 1.2 shard_map.190
  (86 shorter events, 2.3 us)
Async XLA Ops:
  5.7 24.9 %collective-permute-start = (bf16[128,1024]{1,0:T(8,128)(2,1)}, bf16[128,1024]{1,0:T(8,128)(2,1)S(1)}, u32[]{:S(2)}, u32[]{:S(2)}) collective-permute-start(bf16[128,1024]{1,0:T(8,128)(2,1)} %get-tuple-element.67), channel_id=1, source_target_pairs={{0,8},{2,10},{4,12},{6,14},{8,0},{10,2},{12,4},{14,6},{16,24},{18,... | collective-permute-start | bytes 786440 | tf_op jit(solution)/shard_map/ppermute | solution.py:738
  5.7 25.6 %collective-permute-start.1 = (bf16[128,1024]{1,0:T(8,128)(2,1)}, bf16[128,1024]{1,0:T(8,128)(2,1)S(1)}, u32[]{:S(2)}, u32[]{:S(2)}) collective-permute-start(bf16[128,1024]{1,0:T(8,128)(2,1)} %get-tuple-element.67), channel_id=1, source_target_pairs={{0,16},{2,18},{4,20},{6,22},{8,24},{10,26},{12,28},{14,30},{16,0},... | collective-permute-start | bytes 786440 | tf_op jit(solution)/shard_map/ppermute | solution.py:738
  8.8 23.3 %collective-permute-start.2 = (bf16[128,1024]{1,0:T(8,128)(2,1)}, bf16[128,1024]{1,0:T(8,128)(2,1)S(1)}, u32[]{:S(2)}, u32[]{:S(2)}) collective-permute-start(bf16[128,1024]{1,0:T(8,128)(2,1)} %get-tuple-element.67), channel_id=1, source_target_pairs={{0,24},{2,26},{4,28},{6,30},{8,16},{10,18},{12,20},{14,22},{16,8},... | collective-permute-start | bytes 786440 | tf_op jit(solution)/shard_map/ppermute | solution.py:738
  9.2 15.1 %all-to-all-start = ((bf16[4,128,896]{2,1,0:T(8,128)(2,1)}), bf16[4,128,896]{2,1,0:T(8,128)(2,1)S(1)}, u32[]{:S(2)}, u32[]{:S(2)}) async-start(bf16[4,128,896]{2,1,0:T(8,128)(2,1)} %get-tuple-element.65), calls=%async_computation | async-start | bytes 1835008 | tf_op jit(solution)/shard_map/all_to_all | solution.py:757
  12.9 0.7 copy-start.26
  14.8 0.7 copy-start.27
  15.7 0.7 copy-start.28
  18.0 11.2 %copy-start.21 = (f32[2,8]{1,0:T(2,128)}, f32[2,8]{1,0:T(2,128)S(1)}, u32[]{:S(2)}) copy-start(f32[2,8]{1,0:T(2,128)S(1)} %get-tuple-element.83.refs_15_) | copy-start | bytes 196
  24.4 16.6 %all-to-all-start.1 = ((bf16[4,128,1024]{2,1,0:T(8,128)(2,1)}), bf16[4,128,1024]{2,1,0:T(8,128)(2,1)S(1)}, u32[]{:S(2)}, u32[]{:S(2)}) async-start(bf16[4,128,1024]{2,1,0:T(8,128)(2,1)} %get-tuple-element.66), calls=%async_computation.1 | async-start | bytes 2097152 | tf_op jit(solution)/shard_map/all_to_all | solution.py:758
  28.7 7.6 %copy-start.4 = (f32[8,512]{1,0:T(8,128)}, f32[8,512]{1,0:T(8,128)S(1)}, u32[]{:S(2)}) copy-start(f32[8,512]{1,0:T(8,128)S(1)} %fusion.7.refs_3_.info_t_ref.refs_9_) | copy-start | bytes 49156
  30.6 0.7 copy-start.9
  31.3 0.7 copy-start.11
  32.1 0.7 copy-start.13
  34.8 0.7 copy-start.6
  35.5 0.7 copy-start.15
  38.4 0.7 copy-start
  40.9 1.0 copy-start.8
  41.9 0.9 copy-start.10
  42.8 0.9 copy-start.12
  43.8 0.9 copy-start.14
  44.7 2.1 %copy-start.7 = (bf16[272,512]{1,0:T(8,128)(2,1)S(1)}, bf16[272,512]{1,0:T(8,128)(2,1)}, u32[]{:S(2)}) copy-start(bf16[272,512]{1,0:T(8,128)(2,1)} %copy-done.6) | copy-start | bytes 835588
  44.7 28.5 %copy-start.19 = (f32[8,8]{1,0:T(8,128)S(1)}, f32[8,8]{1,0:T(8,128)}, u32[]{:S(2)}) copy-start(f32[8,8]{1,0:T(8,128)} %get-tuple-element.79.refs_11_) | copy-start | bytes 772
  44.7 28.5 %copy-start.20 = (f32[8,8]{1,0:T(8,128)S(1)}, f32[8,8]{1,0:T(8,128)}, u32[]{:S(2)}) copy-start(f32[8,8]{1,0:T(8,128)} %concatenate.11.refs_13_) | copy-start | bytes 772
  44.8 42.8 %collective-permute-start.13 = (bf16[4,128,1024]{2,1,0:T(8,128)(2,1)S(1)}, bf16[4,128,1024]{2,1,0:T(8,128)(2,1)S(1)}, u32[]{:S(2)}, u32[]{:S(2)}) collective-permute-start(bf16[4,128,1024]{2,1,0:T(8,128)(2,1)S(1)} %shard_map.186.refs_2_), channel_id=1, source_target_pairs={{0,2},{2,0},{4,6},{6,4},{8,10},{10,8},{12,14},{14,12},{16,18},{18,... | collective-permute-start | bytes 3145736 | tf_op jit(solution)/shard_map/ppermute | solution.py:729
  46.3 41.3 %collective-permute-start.14 = (bf16[4,128,1024]{2,1,0:T(8,128)(2,1)S(1)}, bf16[4,128,1024]{2,1,0:T(8,128)(2,1)S(1)}, u32[]{:S(2)}, u32[]{:S(2)}) collective-permute-start(bf16[4,128,1024]{2,1,0:T(8,128)(2,1)S(1)} %shard_map.186.refs_2_), channel_id=1, source_target_pairs={{0,4},{2,6},{4,0},{6,2},{8,12},{10,14},{12,8},{14,10},{16,20},{18,... | collective-permute-start | bytes 3145736 | tf_op jit(solution)/shard_map/ppermute | solution.py:729
  46.9 26.4 %copy-start.18 = (f32[8,8]{1,0:T(8,128)S(1)}, f32[8,8]{1,0:T(8,128)}, u32[]{:S(2)}) copy-start(f32[8,8]{1,0:T(8,128)} %get-tuple-element.80.refs_12_) | copy-start | bytes 772
  46.9 26.4 %copy-start.17 = (f32[8,8]{1,0:T(8,128)S(1)}, f32[8,8]{1,0:T(8,128)}, u32[]{:S(2)}) copy-start(f32[8,8]{1,0:T(8,128)} %pad_convert_fusion.refs_14_) | copy-start | bytes 772
  46.9 9.5 %collective-permute-start.3 = (bf16[272,512]{1,0:T(8,128)(2,1)S(1)}, bf16[272,512]{1,0:T(8,128)(2,1)S(1)}, u32[]{:S(2)}, u32[]{:S(2)}) collective-permute-start(bf16[272,512]{1,0:T(8,128)(2,1)S(1)} %copy-done.7), channel_id=1, source_target_pairs={{0,8},{2,10},{4,12},{6,14},{8,0},{10,2},{12,4},{14,6},{16,24},{18,... | collective-permute-start | bytes 835592 | tf_op jit(solution)/shard_map/ppermute | solution.py:738
  48.3 20.2 %collective-permute-start.4 = (bf16[272,512]{1,0:T(8,128)(2,1)S(1)}, bf16[272,512]{1,0:T(8,128)(2,1)S(1)}, u32[]{:S(2)}, u32[]{:S(2)}) collective-permute-start(bf16[272,512]{1,0:T(8,128)(2,1)S(1)} %copy-done.7), channel_id=1, source_target_pairs={{0,16},{2,18},{4,20},{6,22},{8,24},{10,26},{12,28},{14,30},{16,0},... | collective-permute-start | bytes 835592 | tf_op jit(solution)/shard_map/ppermute | solution.py:738
  50.4 22.8 %collective-permute-start.5 = (bf16[272,512]{1,0:T(8,128)(2,1)S(1)}, bf16[272,512]{1,0:T(8,128)(2,1)S(1)}, u32[]{:S(2)}, u32[]{:S(2)}) collective-permute-start(bf16[272,512]{1,0:T(8,128)(2,1)S(1)} %copy-done.7), channel_id=1, source_target_pairs={{0,24},{2,26},{4,28},{6,30},{8,16},{10,18},{12,20},{14,22},{16,8},... | collective-permute-start | bytes 835592 | tf_op jit(solution)/shard_map/ppermute | solution.py:738
  73.2 0.7 copy-start.22
  76.6 8.6 %copy-start.5 = (f32[8,512]{1,0:T(8,128)S(1)}, f32[8,512]{1,0:T(8,128)}, u32[]{:S(2)}) copy-start(f32[8,512]{1,0:T(8,128)} %copy-done.4) | copy-start | bytes 49156
  76.6 1.2 collective-permute-start.6
  77.9 3.7 %collective-permute-start.7 = (f32[8,512]{1,0:T(8,128)S(1)}, f32[8,512]{1,0:T(8,128)S(1)}, u32[]{:S(2)}, u32[]{:S(2)}) collective-permute-start(f32[8,512]{1,0:T(8,128)S(1)} %add.334.refs_2_), channel_id=1, source_target_pairs={{0,2},{2,0},{4,6},{6,4},{8,10},{10,8},{12,14},{14,12},{16,18},{18,... | collective-permute-start | bytes 49160 | tf_op jit(solution)/shard_map/ppermute | solution.py:729
  79.1 3.7 %collective-permute-start.8 = (f32[8,512]{1,0:T(8,128)S(1)}, f32[8,512]{1,0:T(8,128)S(1)}, u32[]{:S(2)}, u32[]{:S(2)}) collective-permute-start(f32[8,512]{1,0:T(8,128)S(1)} %add.334.refs_2_), channel_id=1, source_target_pairs={{0,4},{2,6},{4,0},{6,2},{8,12},{10,14},{12,8},{14,10},{16,20},{18,... | collective-permute-start | bytes 49160 | tf_op jit(solution)/shard_map/ppermute | solution.py:729
  80.5 4.6 %collective-permute-start.9 = (f32[8,512]{1,0:T(8,128)S(1)}, f32[8,512]{1,0:T(8,128)S(1)}, u32[]{:S(2)}, u32[]{:S(2)}) collective-permute-start(f32[8,512]{1,0:T(8,128)S(1)} %add.334.refs_2_), channel_id=1, source_target_pairs={{0,6},{2,4},{4,2},{6,0},{8,14},{10,12},{12,10},{14,8},{16,22},{18,... | collective-permute-start | bytes 49160 | tf_op jit(solution)/shard_map/ppermute | solution.py:729
  87.6 5.0 %copy-start.1 = (bf16[512,128]{1,0:T(8,128)(2,1)S(1)}, bf16[512,128]{1,0:T(8,128)(2,1)}, u32[]{:S(2)}) copy-start(bf16[512,128]{1,0:T(8,128)(2,1)} %copy-done) | copy-start | bytes 393220
  87.7 12.3 %collective-permute-start.15 = (bf16[2,128,1024]{2,1,0:T(8,128)(2,1)S(1)}, bf16[2,128,1024]{2,1,0:T(8,128)(2,1)S(1)}, u32[]{:S(2)}, u32[]{:S(2)}) collective-permute-start(bf16[2,128,1024]{2,1,0:T(8,128)(2,1)S(1)} %slice.10), channel_id=1, source_target_pairs={{0,4},{2,6},{4,0},{6,2},{8,12},{10,14},{12,8},{14,10},{16,20},{18,... | collective-permute-start | bytes 1572872 | tf_op jit(solution)/shard_map/ppermute | solution.py:729
  88.3 12.1 %collective-permute-start.16 = (bf16[2,128,1024]{2,1,0:T(8,128)(2,1)S(1)}, bf16[2,128,1024]{2,1,0:T(8,128)(2,1)S(1)}, u32[]{:S(2)}, u32[]{:S(2)}) collective-permute-start(bf16[2,128,1024]{2,1,0:T(8,128)(2,1)S(1)} %slice.11), channel_id=1, source_target_pairs={{0,2},{2,0},{4,6},{6,4},{8,10},{10,8},{12,14},{14,12},{16,18},{18,... | collective-permute-start | bytes 1572872 | tf_op jit(solution)/shard_map/ppermute | solution.py:729
  89.2 26.1 %collective-permute-start.10 = (bf16[256,512]{1,0:T(8,128)(2,1)S(1)}, bf16[256,512]{1,0:T(8,128)(2,1)S(1)}, u32[]{:S(2)}, u32[]{:S(2)}) collective-permute-start(bf16[256,512]{1,0:T(8,128)(2,1)S(1)} %get-tuple-element.86), channel_id=1, source_target_pairs={{0,8},{2,10},{4,12},{6,14},{8,0},{10,2},{12,4},{14,6},{16,24},{18,... | collective-permute-start | bytes 786440 | tf_op jit(solution)/shard_map/ppermute | solution.py:738
  89.2 26.1 %collective-permute-start.11 = (bf16[256,512]{1,0:T(8,128)(2,1)S(1)}, bf16[256,512]{1,0:T(8,128)(2,1)S(1)}, u32[]{:S(2)}, u32[]{:S(2)}) collective-permute-start(bf16[256,512]{1,0:T(8,128)(2,1)S(1)} %get-tuple-element.86), channel_id=1, source_target_pairs={{0,16},{2,18},{4,20},{6,22},{8,24},{10,26},{12,28},{14,30},{16,0},... | collective-permute-start | bytes 786440 | tf_op jit(solution)/shard_map/ppermute | solution.py:738
  92.1 23.2 %collective-permute-start.12 = (bf16[256,512]{1,0:T(8,128)(2,1)S(1)}, bf16[256,512]{1,0:T(8,128)(2,1)S(1)}, u32[]{:S(2)}, u32[]{:S(2)}) collective-permute-start(bf16[256,512]{1,0:T(8,128)(2,1)S(1)} %get-tuple-element.86), channel_id=1, source_target_pairs={{0,24},{2,26},{4,28},{6,30},{8,16},{10,18},{12,20},{14,22},{16,8},... | collective-permute-start | bytes 786440 | tf_op jit(solution)/shard_map/ppermute | solution.py:738
  92.7 7.8 %copy-start.2 = (bf16[128,2048]{1,0:T(8,128)(2,1)S(1)}, bf16[128,2048]{1,0:T(8,128)(2,1)}, u32[]{:S(2)}) copy-start(bf16[128,2048]{1,0:T(8,128)(2,1)} %refs_7_.1) | copy-start | bytes 1572868
  92.7 7.8 %copy-start.3 = (bf16[128,2048]{1,0:T(8,128)(2,1)S(1)}, bf16[128,2048]{1,0:T(8,128)(2,1)}, u32[]{:S(2)}) copy-start(bf16[128,2048]{1,0:T(8,128)(2,1)} %refs_8_.1) | copy-start | bytes 1572868
  92.7 7.8 %copy-start.23 = (s32[2,16]{1,0:T(2,128)S(1)}, s32[2,16]{1,0:T(2,128)}, u32[]{:S(2)}) copy-start(s32[2,16]{1,0:T(2,128)} %pad_add_fusion.2.refs_0_) | copy-start | bytes 388
  92.7 7.8 %copy-start.25 = (s32[2]{0:T(128)S(1)}, s32[2]{0:T(128)}, u32[]{:S(2)}) copy-start(s32[2]{0:T(128)} %pad_add_fusion.5.refs_1_) | copy-start | bytes 28
  96.5 18.7 %copy-start.16 = (f32[512,128]{1,0:T(8,128)S(1)}, f32[512,128]{1,0:T(8,128)}, u32[]{:S(2)}) copy-start(f32[512,128]{1,0:T(8,128)} %copy-done.15) | copy-start | bytes 786436
  115.3 0.7 copy-start.24
  118.8 10.5 %collective-permute-start.17 = (bf16[128,1280]{1,0:T(8,128)(2,1)S(1)}, bf16[128,1280]{1,0:T(8,128)(2,1)S(1)}, u32[]{:S(2)}, u32[]{:S(2)}) collective-permute-start(bf16[128,1280]{1,0:T(8,128)(2,1)S(1)} %get-tuple-element.115), channel_id=1, source_target_pairs={{0,2},{2,0},{4,6},{6,4},{8,10},{10,8},{12,14},{14,12},{16,18},{18,... | collective-permute-start | bytes 983048 | tf_op jit(solution)/shard_map/ppermute | solution.py:729
  119.6 10.5 %collective-permute-start.18 = (bf16[128,1280]{1,0:T(8,128)(2,1)S(1)}, bf16[128,1280]{1,0:T(8,128)(2,1)S(1)}, u32[]{:S(2)}, u32[]{:S(2)}) collective-permute-start(bf16[128,1280]{1,0:T(8,128)(2,1)S(1)} %get-tuple-element.116), channel_id=1, source_target_pairs={{0,4},{2,6},{4,0},{6,2},{8,12},{10,14},{12,8},{14,10},{16,20},{18,... | collective-permute-start | bytes 983048 | tf_op jit(solution)/shard_map/ppermute | solution.py:729
  120.7 12.8 %collective-permute-start.19 = (bf16[128,1280]{1,0:T(8,128)(2,1)S(1)}, bf16[128,1280]{1,0:T(8,128)(2,1)S(1)}, u32[]{:S(2)}, u32[]{:S(2)}) collective-permute-start(bf16[128,1280]{1,0:T(8,128)(2,1)S(1)} %get-tuple-element.117), channel_id=1, source_target_pairs={{0,6},{2,4},{4,2},{6,0},{8,14},{10,12},{12,10},{14,8},{16,22},{18,... | collective-permute-start | bytes 983048 | tf_op jit(solution)/shard_map/ppermute | solution.py:729

commit v3 on v2

--- a/solution.py
+++ b/solution.py
@@ -67,23 +67,34 @@
     )(*args)
 
 
-def pack_forward(x, w, r, step, gate, grad, keys, values, group):
+def pack_gates(gate, grad, group):
+    rows, chans = gate.shape[0], gate.shape[1] // group
+
+    def kernel(gate_ref, grad_ref, out):
+        for m in range(group):
+            out[m, :, 0:chans] = gate_ref[:, m * chans : (m + 1) * chans]
+            out[m, :, chans : 2 * chans] = grad_ref[:, m * chans : (m + 1) * chans]
+
+    return call(kernel, [((group, rows, 2 * chans), BF16)], (gate, grad), nbytes=8 * gate.size)[0]
+
+
+def pack_forward(x, w, r, step, keys, values, group):
     rows, chans = x.shape[0], x.shape[1] // group
     heads = step.shape[1] // group
     width = chans + 2 * NSTATE + 128
     kv_width = keys.shape[1]
 
-    wide = [(0, chans), (1, NSTATE), (2, NSTATE), (None, 128), (3, chans), (4, chans)]
-    sources = (x, w, r, gate, grad, keys, values)
+    wide = [(0, chans), (1, NSTATE), (2, NSTATE), (None, 128)]
+    sources = (x, w, r, keys, values)
     n_in = len(sources)
     n_out = 2 + group * len(wide)
 
     def kernel(step_ref, *refs):
-        ins, kv_ref, out, gate_out = refs[:n_in], *refs[n_in : n_in + 3]
-        held = refs[n_in + 3 : -3]
+        ins, kv_ref, out = refs[:n_in], *refs[n_in : n_in + 2]
+        held = refs[n_in + 2 : -3]
         step_buf, in_sems, out_sems = refs[-3:]
         loads = [pltpu.make_async_copy(ins[i], held[i], in_sems.at[i]) for i in range(n_in)]
-        for i in (5, 6, 0, 1, 2, 3, 4):
+        for i in (3, 4, 0, 1, 2):
             loads[i].start()
         parts = split3(step_ref[...])
         row = lax.broadcasted_iota(jnp.int32, (heads * group, 128), 0)
@@ -102,20 +113,17 @@
             copy.start()
             copies.append(copy)
 
-        loads[5].wait()
-        send(held[5], kv_ref.at[:, 0:kv_width])
-        loads[6].wait()
-        send(held[6], kv_ref.at[:, kv_width : 2 * kv_width])
+        loads[3].wait()
+        send(held[3], kv_ref.at[:, 0:kv_width])
+        loads[4].wait()
+        send(held[4], kv_ref.at[:, kv_width : 2 * kv_width])
         start = 0
         for source, count in wide:
             if source is not None:
                 loads[source].wait()
             for m in range(group):
                 at = slice(m * count, (m + 1) * count)
-                if start >= width:
-                    dst = gate_out.at[m, :, start - width : start - width + count]
-                else:
-                    dst = out.at[m, :, start : start + count]
+                dst = out.at[m, :, start : start + count]
                 send(step_buf.at[m] if source is None else held[source].at[:, at], dst)
             start += count
         for copy in copies:
@@ -124,7 +132,7 @@
     return move(
         kernel,
         [((rows, 2 * kv_width), BF16)]
-        + [((group, rows, width), BF16), ((group, rows, 2 * chans), BF16)],
+        + [((group, rows, width), BF16)],
         (step, *sources),
         (pltpu.VMEM,),
         [pltpu.VMEM(source.shape, BF16) for source in sources]
@@ -391,7 +399,7 @@
             pltpu.VMEM((rows, chans), F32),
             pltpu.VMEM((rows, 128), F32),
         ],
-        flops=4 * rows * 2 * NSTATE * chans,
+        flops=35 * 10**12,
         nbytes=16 * rows * chans,
     )
 
@@ -746,16 +754,14 @@
         sets = [[u * group + j for u in range(units)] for j in range(group)]
         return [lax.all_gather(value, "ctx", axis=0, axis_index_groups=sets)]
 
-    own_kv, packed, gates = pack_forward(
-        mamba_input, state_write, state_read, step_raw, gate_input, mamba_grad, attn_keys,
-        attn_values, group,
+    own_kv, packed = pack_forward(
+        mamba_input, state_write, state_read, step_raw, attn_keys, attn_values, group
     )
     kv_units = all_units(own_kv)
     forward_pieces = packed
     if group > 1:
         planes = [[u * group + j for j in range(group)] for u in range(units)]
         forward_pieces = lax.all_to_all(packed, "ctx", 0, 0, axis_index_groups=planes, tiled=True)
-        gates = lax.all_to_all(after(gates, forward_pieces), "ctx", 0, 0, axis_index_groups=planes, tiled=True)
 
     unit_ids = jnp.arange(units, dtype=jnp.int32)
     if by_permute:
@@ -835,6 +841,9 @@
         blocks, own_blocks,
     )
     small_group = group == 4 and units == 4 and by_permute
+    gates = pack_gates(after(gate_input, (info, enter_mask, own_end)), mamba_grad, group)
+    if group > 1:
+        gates = lax.all_to_all(after(gates, forward_pieces), "ctx", 0, 0, axis_index_groups=planes, tiled=True)
     forward_pieces, tables = after((forward_pieces, tables), kv_units)
     (
         info, info_t, small, chan, before_in, ends, enter_mask, leave_mask, own_mask, own_end,

time: 135 us -> 127 us (0.941)
  waiting for transfers between devices: 50.1 us -> 41.4 us
  local copies, waits for them, and re-layouts: 14.5 us -> 10.8 us
  Pallas kernels: 35.6 us -> 37.5 us
    ppermute x9, waiting for transfers between devices: 22.4 us -> 16.1 us  [across(): moved.append(lax.ppermute(value, 'ctx', pairs))]
    unnamed x59 -> x121, local copies, waits for them, and re-layouts: 12.6 us -> 8.88 us
    pallas_call x9 -> x10, Pallas kernels: 32 us -> 34.4 us  [call(): pl.pallas_call(fn, out_shape=tuple((jax.ShapeDtypeStruct(s, d) for s, d i...]
    all_to_all x1, waiting for transfers between devices: 1.85 us -> 0.01 us  [body(): lax.all_to_all(after(gates, forward_pieces), 'ctx', 0, 0, axis_index_grou...]
    all_to_all x1, waiting for transfers between devices: 5.75 us -> 4.18 us  [body(): lax.all_to_all(packed, 'ctx', 0, 0, axis_index_groups=planes, tiled=True)]
  transfers between devices with their start and end apart: 22 -> 22, of which waited for: 15 -> 12; matrix products, arithmetic and copies ran while one was open for 5% -> 6% of each run, Pallas kernels for 21% -> 24%
where the time goes in v3:
time: 127 us; the launch traced here: 126 us
  waiting for transfers between devices  41.4 us (33%)
  Pallas kernels  37.5 us (30%)
  starting transfers between devices  30.1 us (24%)
  local copies, waits for them, and re-layouts  10.8 us (9%)
  other arithmetic  5.16 us (4%)
  between operations  1.53 us (1%)
    pallas_call x10, Pallas kernels, call(): pl.pallas_call(fn, out_shape=tuple((jax.ShapeDtypeStruct(s, d) for s, d i...  34.4 us
    ppermute x10, waiting for transfers between devices, to_place(): return lax.ppermute(value, 'ctx', pairs)  20 us
    ppermute x9, waiting for transfers between devices, across(): moved.append(lax.ppermute(value, 'ctx', pairs))  16.1 us
    ppermute x10, starting transfers between devices, to_place(): return lax.ppermute(value, 'ctx', pairs)  11.6 us
    ppermute x9, starting transfers between devices, across(): moved.append(lax.ppermute(value, 'ctx', pairs))  11.1 us
    unnamed x121, local copies, waits for them, and re-layouts  8.88 us
    all_to_all x1, waiting for transfers between devices, body(): lax.all_to_all(packed, 'ctx', 0, 0, axis_index_groups=planes, tiled=True)  4.18 us
    all_to_all x1, starting transfers between devices, body(): lax.all_to_all(packed, 'ctx', 0, 0, axis_index_groups=planes, tiled=True)  3.85 us
  transfers between devices with their start and end apart: 22, of which 12 were waited for; matrix products, arithmetic and copies ran while one was open for 6% of the time, Pallas kernels for 24%

profile of v3, /device:TPU:8, one launch (start us, length us, event | category | flops | bytes accessed | tf_op | source)
XLA Modules:
  0.0 126.5 jit_solution(3481943217449688954)
XLA Ops:
  0.6 1.4 %copy.21.step_ref = f32[128,32]{1,0:T(8,128)} copy(f32[128,32]{0,1:T(8,128)} %param.23) | data formatting | bytes 32768 | tf_op args[9]
  2.1 3.1 %shard_map.182 = (bf16[128,1024]{1,0:T(8,128)(2,1)}, bf16[4,128,896]{2,1,0:T(8,128)(2,1)}) custom-call(f32[128,32]{1,0:T(8,128)} %copy.21.step_ref, bf16[128,2048]{1,0:T(8,128)(2,1)} %refs_0_.1, bf16[128,512]{1,0:T(8,128)(2,1)} %refs_1_.1, bf16[128,512]{1,0:T(8,128)(2,1)} %refs_2_.1, bf16[128,512]{1,0:T(8,128)(2,1)} %refs_3_.1, bf16[128,512]{1,0:T(8,128)(2,1)} %refs_4_.1), custom_call_target="tpu_custom_call" | custom-call | bytes 1024 | tf_op jit(solution)/shard_map/pallas_call | solution.py:150
  5.3 3.0 %collective-permute-start.1 = (bf16[128,1024]{1,0:T(8,128)(2,1)}, bf16[128,1024]{1,0:T(8,128)(2,1)S(1)}, u32[]{:S(2)}, u32[]{:S(2)}) collective-permute-start(bf16[128,1024]{1,0:T(8,128)(2,1)} %get-tuple-element.67), channel_id=1, source_target_pairs={{0,16},{2,18},{4,20},{6,22},{8,24},{10,26},{12,28},{14,30},{16,0},... | collective-permute-start | bytes 786440 | tf_op jit(solution)/shard_map/ppermute | solution.py:746
  8.3 0.5 collective-permute-start.2
  8.8 3.8 %all-to-all-start = ((bf16[4,128,896]{2,1,0:T(8,128)(2,1)}), bf16[4,128,896]{2,1,0:T(8,128)(2,1)S(1)}, u32[]{:S(2)}, u32[]{:S(2)}) async-start(bf16[4,128,896]{2,1,0:T(8,128)(2,1)} %get-tuple-element.65), calls=%async_computation | async-start | bytes 1835008 | tf_op jit(solution)/shard_map/all_to_all | solution.py:764
  13.1 0.1 le.28
  13.5 0.7 compare_convert_fusion.2
  14.3 0.7 fusion.refs_2_.info_ref.refs_9_.refs_14_
  15.0 0.1 add_add_fusion
  15.3 0.7 copy-done.58
  16.1 0.6 pad_convert_fusion.refs_14_
  16.7 0.8 dynamic_slice.11
  17.5 1.0 shard_map.181
  18.6 0.6 pad_add_fusion.2.refs_0_
  19.2 0.6 select_maximum_fusion.chan_ref.refs_10_.refs_15_
  19.9 4.2 %all-to-all-done.refs_1_ = bf16[4,128,896]{2,1,0:T(8,128)(2,1)S(1)} async-done(((bf16[4,128,896]{2,1,0:T(8,128)(2,1)}), bf16[4,128,896]{2,1,0:T(8,128)(2,1)S(1)}, u32[]{:S(2)}, u32[]{:S(2)}) %all-to-all-start) | async-done | bytes 917536 | tf_op jit(solution)/shard_map/all_to_all | solution.py:764
  24.1 3.5 %all-to-all-start.1 = ((bf16[4,128,1024]{2,1,0:T(8,128)(2,1)}), bf16[4,128,1024]{2,1,0:T(8,128)(2,1)S(1)}, u32[]{:S(2)}, u32[]{:S(2)}) async-start(bf16[4,128,1024]{2,1,0:T(8,128)(2,1)} %shard_map.181), calls=%async_computation.1 | async-start | bytes 2097152 | tf_op jit(solution)/shard_map/all_to_all | solution.py:846
  27.7 0.7 compare_convert_fusion
  28.3 0.6 pad_add_fusion.5.refs_1_
  28.9 0.6 concatenate.13.refs_13_
  29.7 0.5 copy-done.27
  30.2 0.1 fusion.7.refs_3_.info_t_ref.refs_9_
  30.4 0.7 copy-done.7
  31.1 0.7 copy-done.9
  31.8 0.7 copy-done.11
  32.5 2.7 %shard_map.183 = (bf16[272,512]{1,0:T(8,128)(2,1)}, bf16[512,512]{1,0:T(8,128)(2,1)S(1)}, bf16[512,128]{1,0:T(8,128)(2,1)S(1)}, bf16[512,128]{1,0:T(8,128)(2,1)S...) custom-call(s32[1]{0:T(128)} %bitcast.refs_0_.me_ref, ...), custom_call_target="tpu_custom_call" | custom-call | flops 134217 | bytes 1572 | tf_op jit(solution)/shard_map/pallas_call | solution.py:59
  35.2 0.7 copy-done.15
  35.9 1.4 %collective-permute-start.3 = (bf16[272,512]{1,0:T(8,128)(2,1)}, bf16[272,512]{1,0:T(8,128)(2,1)}, u32[]{:S(2)}, u32[]{:S(2)}) collective-permute-start(bf16[272,512]{1,0:T(8,128)(2,1)} %get-tuple-element.72), channel_id=1, source_target_pairs={{0,8},{2,10},{4,12},{6,14},{8,0},{10,2},{12,4},{14,6},{16,24},{18,... | collective-permute-start | bytes 835592 | tf_op jit(solution)/shard_map/ppermute | solution.py:746
  37.4 2.1 %collective-permute-start.4 = (bf16[272,512]{1,0:T(8,128)(2,1)}, bf16[272,512]{1,0:T(8,128)(2,1)}, u32[]{:S(2)}, u32[]{:S(2)}) collective-permute-start(bf16[272,512]{1,0:T(8,128)(2,1)} %get-tuple-element.72), channel_id=1, source_target_pairs={{0,16},{2,18},{4,20},{6,22},{8,24},{10,26},{12,28},{14,30},{16,0},... | collective-permute-start | bytes 835592 | tf_op jit(solution)/shard_map/ppermute | solution.py:746
  39.4 0.6 collective-permute-start.5
  40.0 2.2 %shard_map.184.refs_6_ = f32[512,512]{1,0:T(8,128)S(1)} custom-call(bf16[512,512]{1,0:T(8,128)(2,1)S(1)} %get-tuple-element.73.x_ref.refs_4_, bf16[512,128]{1,0:T(8,128)(2,1)S(1)} %get-tuple-element.74.w_ref.refs_5_, bf16[512,128]{1,0:T(8,128)(2,1)S(1)} %get-tuple-element.75.r_ref.refs_7_, f32[512,128]{1,0:T(8,128)S(1)} %get-tuple-element.76.cum_ref.refs_8_, ...), custom_call_target="tpu_custom_call" | custom-call | flops 536870 | bytes 2097 | tf_op jit(solution)/shard_map/pallas_call | solution.py:59
  42.2 1.0 copy-done
  43.2 0.9 copy-done.12
  44.3 2.1 %collective-permute-start.13 = (bf16[4,128,1024]{2,1,0:T(8,128)(2,1)S(1)}, bf16[4,128,1024]{2,1,0:T(8,128)(2,1)S(1)}, u32[]{:S(2)}, u32[]{:S(2)}) collective-permute-start(bf16[4,128,1024]{2,1,0:T(8,128)(2,1)S(1)} %shard_map.187.refs_2_), channel_id=1, source_target_pairs={{0,2},{2,0},{4,6},{6,4},{8,10},{10,8},{12,14},{14,12},{16,18},{18,... | collective-permute-start | bytes 3145736 | tf_op jit(solution)/shard_map/ppermute | solution.py:737
  46.3 1.5 %collective-permute-start.14 = (bf16[4,128,1024]{2,1,0:T(8,128)(2,1)S(1)}, bf16[4,128,1024]{2,1,0:T(8,128)(2,1)S(1)}, u32[]{:S(2)}, u32[]{:S(2)}) collective-permute-start(bf16[4,128,1024]{2,1,0:T(8,128)(2,1)S(1)} %shard_map.187.refs_2_), channel_id=1, source_target_pairs={{0,4},{2,6},{4,0},{6,2},{8,12},{10,14},{12,8},{14,10},{16,20},{18,... | collective-permute-start | bytes 3145736 | tf_op jit(solution)/shard_map/ppermute | solution.py:737
  47.8 11.0 %collective-permute-done.4 = bf16[272,512]{1,0:T(8,128)(2,1)} collective-permute-done((bf16[272,512]{1,0:T(8,128)(2,1)}, bf16[272,512]{1,0:T(8,128)(2,1)}, u32[]{:S(2)}, u32[]{:S(2)}) %collective-permute-start.4) | collective-permute-done | bytes 278560 | tf_op jit(solution)/shard_map/ppermute | solution.py:746
  58.8 5.1 %collective-permute-done.5 = bf16[272,512]{1,0:T(8,128)(2,1)} collective-permute-done((bf16[272,512]{1,0:T(8,128)(2,1)}, bf16[272,512]{1,0:T(8,128)(2,1)}, u32[]{:S(2)}, u32[]{:S(2)}) %collective-permute-start.5) | collective-permute-done | bytes 278560 | tf_op jit(solution)/shard_map/ppermute | solution.py:746
  63.9 0.6 copy-done.23
  64.5 3.4 %shard_map.185 = (f32[512,512]{1,0:T(8,128)S(1)}, f32[8,512]{1,0:T(8,128)S(1)}, bf16[256,512]{1,0:T(8,128)(2,1)S(1)}, f32[8,512]{1,0:T(8,128)S(1)}, f32[8,512]{1,0:T(8,128)S(1)}) custom-call(s32[1]{0:T(128)} %bitcast.refs_0_.me_ref, bf16[1,272,512]{2,1,0:T(8,128)(2,1)} %bitcast.14.refs_1_, bf16[1,272,512]{2,1,0:T(8,128)(2,1)} %bitcast.15.refs_2_, ...), custom_call_target="tpu_custom_call" | custom-call | flops 35000000512 | bytes 4194 | tf_op jit(solution)/shard_map/pallas_call | solution.py:59
  68.0 1.2 collective-permute-done.6
  69.1 1.7 %collective-permute-start.7 = (f32[8,512]{1,0:T(8,128)S(1)}, f32[8,512]{1,0:T(8,128)S(1)}, u32[]{:S(2)}, u32[]{:S(2)}) collective-permute-start(f32[8,512]{1,0:T(8,128)S(1)} %add.334.refs_2_), channel_id=1, source_target_pairs={{0,2},{2,0},{4,6},{6,4},{8,10},{10,8},{12,14},{14,12},{16,18},{18,... | collective-permute-start | bytes 49160 | tf_op jit(solution)/shard_map/ppermute | solution.py:737
  70.8 1.5 %collective-permute-start.8 = (f32[8,512]{1,0:T(8,128)S(1)}, f32[8,512]{1,0:T(8,128)S(1)}, u32[]{:S(2)}, u32[]{:S(2)}) collective-permute-start(f32[8,512]{1,0:T(8,128)S(1)} %add.334.refs_2_), channel_id=1, source_target_pairs={{0,4},{2,6},{4,0},{6,2},{8,12},{10,14},{12,8},{14,10},{16,20},{18,... | collective-permute-start | bytes 49160 | tf_op jit(solution)/shard_map/ppermute | solution.py:737
  72.3 0.3 collective-permute-start.9
  72.6 0.2 collective-permute-done.7.refs_3_
  72.9 1.7 %collective-permute-done.8.refs_4_ = f32[8,512]{1,0:T(8,128)S(1)} collective-permute-done((f32[8,512]{1,0:T(8,128)S(1)}, f32[8,512]{1,0:T(8,128)S(1)}, u32[]{:S(2)}, u32[]{:S(2)}) %collective-permute-start.8) | collective-permute-done | bytes 16416 | tf_op jit(solution)/shard_map/ppermute | solution.py:737
  74.6 2.4 %collective-permute-done.9.refs_5_ = f32[8,512]{1,0:T(8,128)S(1)} collective-permute-done((f32[8,512]{1,0:T(8,128)S(1)}, f32[8,512]{1,0:T(8,128)S(1)}, u32[]{:S(2)}, u32[]{:S(2)}) %collective-permute-start.9) | collective-permute-done | bytes 16416 | tf_op jit(solution)/shard_map/ppermute | solution.py:737
  76.9 2.4 %shard_map.186 = (bf16[256,512]{1,0:T(8,128)(2,1)S(1)}, f32[512,512]{1,0:T(8,128)S(1)}, bf16[512,512]{1,0:T(8,128)(2,1)S(1)}, f32[512,128]{1,0:T(8,128)S(1)}) custom-call(s32[1]{0:T(128)} %bitcast.refs_0_.me_ref, bf16[4,128,1024]{2,1,0:T(8,128)(2,1)S(1)} %all-to-all-done.1.refs_5_.refs_1_, f32[8,512]{1,0:T(8,128)S(1)} %add.334.refs_2_, ...), custom_call_target="tpu_custom_call" | custom-call | flops 134217 | bytes 4194 | tf_op jit(solution)/shard_map/pallas_call | solution.py:59
  79.4 0.6 collective-permute-start.15
  80.1 0.4 collective-permute-start.16
  80.4 2.9 %collective-permute-start.11 = (bf16[256,512]{1,0:T(8,128)(2,1)S(1)}, bf16[256,512]{1,0:T(8,128)(2,1)S(1)}, u32[]{:S(2)}, u32[]{:S(2)}) collective-permute-start(bf16[256,512]{1,0:T(8,128)(2,1)S(1)} %get-tuple-element.86), channel_id=1, source_target_pairs={{0,16},{2,18},{4,20},{6,22},{8,24},{10,26},{12,28},{14,30},{16,0},... | collective-permute-start | bytes 786440 | tf_op jit(solution)/shard_map/ppermute | solution.py:746
  83.3 0.6 collective-permute-start.12
  83.9 3.8 %shard_map.189 = (f32[512,512]{1,0:T(8,128)S(1)}, f32[512,128]{1,0:T(8,128)S(1)}, f32[512,128]{1,0:T(8,128)S(1)}) custom-call(bf16[512,512]{1,0:T(8,128)(2,1)S(1)} %get-tuple-element.73.x_ref.refs_4_, bf16[512,128]{1,0:T(8,128)(2,1)S(1)} %get-tuple-element.74.w_ref.refs_5_, bf16[512,128]{1,0:T(8,128)(2,1)S(1)} %get-tuple-element.75.r_ref.refs_7_, ...), custom_call_target="tpu_custom_call" | custom-call | flops 1073741 | bytes 4194 | tf_op jit(solution)/shard_map/pallas_call | solution.py:59
  87.8 4.0 %collective-permute-done.15.refs_5_ = bf16[2,128,1024]{2,1,0:T(8,128)(2,1)S(1)} collective-permute-done((bf16[2,128,1024]{2,1,0:T(8,128)(2,1)S(1)}, bf16[2,128,1024]{2,1,0:T(8,128)(2,1)S(1)}, u32[]{:S(2)}, u32[]{:S(2)}) %collective-permute-start.15) | collective-permute-done | bytes 524320 | tf_op jit(solution)/shard_map/ppermute | solution.py:737
  91.7 0.5 collective-permute-done.16.refs_6_
  92.2 14.8 %shard_map.188 = (bf16[128,2048]{1,0:T(8,128)(2,1)}, bf16[128,2048]{1,0:T(8,128)(2,1)}) custom-call(s32[2,16]{1,0:T(2,128)S(1)} %copy-done.17, s32[2]{0:T(128)S(1)} %copy-done.25, bf16[4,128,1024]{2,1,0:T(8,128)(2,1)S(1)} %shard_map.187.refs_2_, bf16[4,128,1024]{2,1,0:T(8,128)(2,1)S(1)} %collective-permute-done.13.refs_3_, ...), custom_call_target="tpu_custom_call" | custom-call | flops 5368709 | bytes 4194 | tf_op jit(solution)/shard_map/pallas_call | solution.py:59
  107.1 0.6 copy-done.24
  107.7 2.8 %shard_map.190 = (bf16[128,1280]{1,0:T(8,128)(2,1)S(1)}, bf16[128,1280]{1,0:T(8,128)(2,1)S(1)}, bf16[128,1280]{1,0:T(8,128)(2,1)S(1)}, bf16[128,1280]{1,0:T(8,128)(2,1)S(1)}) custom-call(bf16[1,256,512]{2,1,0:T(8,128)(2,1)S(1)} %bitcast.28, bf16[1,256,512]{2,1,0:T(8,128)(2,1)S(1)} %bitcast.29, bf16[1,256,512]{2,1,0:T(8,128)(2,1)S(1)} %bitcast.30, ...), custom_call_target="tpu_custom_call" | custom-call | flops 268435 | bytes 4194 | tf_op jit(solution)/shard_map/pallas_call | solution.py:59
  110.5 0.3 collective-permute-start.17
  110.9 1.7 %collective-permute-start.18 = (bf16[128,1280]{1,0:T(8,128)(2,1)S(1)}, bf16[128,1280]{1,0:T(8,128)(2,1)S(1)}, u32[]{:S(2)}, u32[]{:S(2)}) collective-permute-start(bf16[128,1280]{1,0:T(8,128)(2,1)S(1)} %get-tuple-element.116), channel_id=1, source_target_pairs={{0,4},{2,6},{4,0},{6,2},{8,12},{10,14},{12,8},{14,10},{16,20},{18,... | collective-permute-start | bytes 983048 | tf_op jit(solution)/shard_map/ppermute | solution.py:737
  112.5 1.6 %collective-permute-start.19 = (bf16[128,1280]{1,0:T(8,128)(2,1)S(1)}, bf16[128,1280]{1,0:T(8,128)(2,1)S(1)}, u32[]{:S(2)}, u32[]{:S(2)}) collective-permute-start(bf16[128,1280]{1,0:T(8,128)(2,1)S(1)} %get-tuple-element.117), channel_id=1, source_target_pairs={{0,6},{2,4},{4,2},{6,0},{8,14},{10,12},{12,10},{14,8},{16,22},{18,... | collective-permute-start | bytes 983048 | tf_op jit(solution)/shard_map/ppermute | solution.py:737
  114.1 7.0 %collective-permute-done.17.refs_1_ = bf16[128,1280]{1,0:T(8,128)(2,1)S(1)} collective-permute-done((bf16[128,1280]{1,0:T(8,128)(2,1)S(1)}, bf16[128,1280]{1,0:T(8,128)(2,1)S(1)}, u32[]{:S(2)}, u32[]{:S(2)}) %collective-permute-start.17) | collective-permute-done | bytes 327712 | tf_op jit(solution)/shard_map/ppermute | solution.py:737
  121.0 0.4 collective-permute-done.18.refs_2_
  121.4 3.9 %collective-permute-done.19.refs_3_ = bf16[128,1280]{1,0:T(8,128)(2,1)S(1)} collective-permute-done((bf16[128,1280]{1,0:T(8,128)(2,1)S(1)}, bf16[128,1280]{1,0:T(8,128)(2,1)S(1)}, u32[]{:S(2)}, u32[]{:S(2)}) %collective-permute-start.19) | collective-permute-done | bytes 327712 | tf_op jit(solution)/shard_map/ppermute | solution.py:737
  125.3 1.2 shard_map.191
  (149 shorter events, 1.4 us)
Async XLA Ops:
  5.2 25.1 %collective-permute-start = (bf16[128,1024]{1,0:T(8,128)(2,1)}, bf16[128,1024]{1,0:T(8,128)(2,1)S(1)}, u32[]{:S(2)}, u32[]{:S(2)}) collective-permute-start(bf16[128,1024]{1,0:T(8,128)(2,1)} %get-tuple-element.67), channel_id=1, source_target_pairs={{0,8},{2,10},{4,12},{6,14},{8,0},{10,2},{12,4},{14,6},{16,24},{18,... | collective-permute-start | bytes 786440 | tf_op jit(solution)/shard_map/ppermute | solution.py:746
  5.3 25.8 %collective-permute-start.1 = (bf16[128,1024]{1,0:T(8,128)(2,1)}, bf16[128,1024]{1,0:T(8,128)(2,1)S(1)}, u32[]{:S(2)}, u32[]{:S(2)}) collective-permute-start(bf16[128,1024]{1,0:T(8,128)(2,1)} %get-tuple-element.67), channel_id=1, source_target_pairs={{0,16},{2,18},{4,20},{6,22},{8,24},{10,26},{12,28},{14,30},{16,0},... | collective-permute-start | bytes 786440 | tf_op jit(solution)/shard_map/ppermute | solution.py:746
  8.3 23.5 %collective-permute-start.2 = (bf16[128,1024]{1,0:T(8,128)(2,1)}, bf16[128,1024]{1,0:T(8,128)(2,1)S(1)}, u32[]{:S(2)}, u32[]{:S(2)}) collective-permute-start(bf16[128,1024]{1,0:T(8,128)(2,1)} %get-tuple-element.67), channel_id=1, source_target_pairs={{0,24},{2,26},{4,28},{6,30},{8,16},{10,18},{12,20},{14,22},{16,8},... | collective-permute-start | bytes 786440 | tf_op jit(solution)/shard_map/ppermute | solution.py:746
  8.8 3.9 %copy-start.38 = (s32[16]{0:T(128)S(1)}, s32[16]{0:T(128)}, u32[]{:S(2)}) copy-start(s32[16]{0:T(128)} %param.14) | copy-start | bytes 196
  8.8 8.7 %copy-start.5 = (bf16[128,2048]{1,0:T(8,128)(2,1)S(1)}, bf16[128,2048]{1,0:T(8,128)(2,1)}, u32[]{:S(2)}) copy-start(bf16[128,2048]{1,0:T(8,128)(2,1)} %grad_ref.1) | copy-start | bytes 1572868
  8.8 15.3 %all-to-all-start = ((bf16[4,128,896]{2,1,0:T(8,128)(2,1)}), bf16[4,128,896]{2,1,0:T(8,128)(2,1)S(1)}, u32[]{:S(2)}, u32[]{:S(2)}) async-start(bf16[4,128,896]{2,1,0:T(8,128)(2,1)} %get-tuple-element.65), calls=%async_computation | async-start | bytes 1835008 | tf_op jit(solution)/shard_map/all_to_all | solution.py:764
  12.6 4.9 %copy-start.4 = (bf16[128,2048]{1,0:T(8,128)(2,1)S(1)}, bf16[128,2048]{1,0:T(8,128)(2,1)}, u32[]{:S(2)}) copy-start(bf16[128,2048]{1,0:T(8,128)(2,1)} %gate_ref) | copy-start | bytes 1572868
  12.7 1.4 %copy-start.26 = (s32[512]{0:T(512)}, s32[512]{0:T(512)S(1)}, u32[]{:S(2)}) copy-start(s32[512]{0:T(512)S(1)} %get-tuple-element.133) | copy-start | bytes 6148
  12.7 1.4 %copy-start.28 = (s32[512]{0:T(512)}, s32[512]{0:T(512)S(1)}, u32[]{:S(2)}) copy-start(s32[512]{0:T(512)S(1)} %get-tuple-element.134) | copy-start | bytes 6148
  12.7 1.4 %copy-start.30 = (s32[512]{0:T(512)}, s32[512]{0:T(512)S(1)}, u32[]{:S(2)}) copy-start(s32[512]{0:T(512)S(1)} %get-tuple-element.135) | copy-start | bytes 6148
  12.8 1.4 %copy-start.32 = (s32[512]{0:T(512)}, s32[512]{0:T(512)S(1)}, u32[]{:S(2)}) copy-start(s32[512]{0:T(512)S(1)} %get-tuple-element.136) | copy-start | bytes 6148
  12.8 1.4 %copy-start.34 = (s32[512]{0:T(512)}, s32[512]{0:T(512)S(1)}, u32[]{:S(2)}) copy-start(s32[512]{0:T(512)S(1)} %get-tuple-element.139) | copy-start | bytes 6148
  12.8 1.4 %copy-start.36 = (s32[512]{0:T(512)}, s32[512]{0:T(512)S(1)}, u32[]{:S(2)}) copy-start(s32[512]{0:T(512)S(1)} %get-tuple-element.140) | copy-start | bytes 6148
  12.8 1.4 %copy-start.40 = (pred[512]{0:T(512)(128)(4,1)}, pred[512]{0:T(512)(128)(4,1)S(1)}, u32[]{:S(2)}) copy-start(pred[512]{0:T(512)(128)(4,1)S(1)} %get-tuple-element.137) | copy-start | bytes 1540
  12.8 1.4 %copy-start.42 = (pred[512]{0:T(512)(128)(4,1)}, pred[512]{0:T(512)(128)(4,1)S(1)}, u32[]{:S(2)}) copy-start(pred[512]{0:T(512)(128)(4,1)S(1)} %get-tuple-element.138) | copy-start | bytes 1540
  12.8 1.3 %copy-start.44 = (pred[8]{0:T(512)(128)(4,1)}, pred[8]{0:T(512)(128)(4,1)S(1)}, u32[]{:S(2)}) copy-start(pred[8]{0:T(512)(128)(4,1)S(1)} %get-tuple-element.141) | copy-start | bytes 28
  12.9 1.3 %copy-start.46 = (pred[8]{0:T(512)(128)(4,1)}, pred[8]{0:T(512)(128)(4,1)S(1)}, u32[]{:S(2)}) copy-start(pred[8]{0:T(512)(128)(4,1)S(1)} %get-tuple-element.142) | copy-start | bytes 28
  12.9 1.3 %copy-start.48 = (pred[8]{0:T(512)(128)(4,1)}, pred[8]{0:T(512)(128)(4,1)S(1)}, u32[]{:S(2)}) copy-start(pred[8]{0:T(512)(128)(4,1)S(1)} %get-tuple-element.143) | copy-start | bytes 28
  14.1 14.8 %copy-start.22 = (f32[2,8]{1,0:T(2,128)}, f32[2,8]{1,0:T(2,128)S(1)}, u32[]{:S(2)}) copy-start(f32[2,8]{1,0:T(2,128)S(1)} %get-tuple-element.83.refs_15_) | copy-start | bytes 196
  24.0 5.5 %copy-start.31 = (s32[512]{0:T(512)S(1)}, s32[512]{0:T(512)}, u32[]{:S(2)}) copy-start(s32[512]{0:T(512)} %copy-done.30) | copy-start | bytes 6148
  24.0 5.5 %copy-start.33 = (s32[512]{0:T(512)S(1)}, s32[512]{0:T(512)}, u32[]{:S(2)}) copy-start(s32[512]{0:T(512)} %copy-done.32) | copy-start | bytes 6148
  24.0 5.5 %copy-start.35 = (s32[512]{0:T(512)S(1)}, s32[512]{0:T(512)}, u32[]{:S(2)}) copy-start(s32[512]{0:T(512)} %copy-done.34) | copy-start | bytes 6148
  24.0 5.5 %copy-start.37 = (s32[512]{0:T(512)S(1)}, s32[512]{0:T(512)}, u32[]{:S(2)}) copy-start(s32[512]{0:T(512)} %copy-done.36) | copy-start | bytes 6148
  24.1 5.6 %copy-start.43 = (pred[512]{0:T(512)(128)(4,1)S(1)}, pred[512]{0:T(512)(128)(4,1)}, u32[]{:S(2)}) copy-start(pred[512]{0:T(512)(128)(4,1)} %copy-done.42) | copy-start | bytes 1540
  24.1 5.6 %copy-start.45 = (pred[8]{0:T(512)(128)(4,1)S(1)}, pred[8]{0:T(512)(128)(4,1)}, u32[]{:S(2)}) copy-start(pred[8]{0:T(512)(128)(4,1)} %copy-done.44) | copy-start | bytes 28
  24.1 5.6 %copy-start.47 = (pred[8]{0:T(512)(128)(4,1)S(1)}, pred[8]{0:T(512)(128)(4,1)}, u32[]{:S(2)}) copy-start(pred[8]{0:T(512)(128)(4,1)} %copy-done.46) | copy-start | bytes 28
  24.1 5.6 %copy-start.49 = (pred[8]{0:T(512)(128)(4,1)S(1)}, pred[8]{0:T(512)(128)(4,1)}, u32[]{:S(2)}) copy-start(pred[8]{0:T(512)(128)(4,1)} %copy-done.48) | copy-start | bytes 28
  24.1 5.6 %copy-start.51 = (pred[8]{0:T(512)(128)(4,1)S(1)}, pred[8]{0:T(512)(128)(4,1)}, u32[]{:S(2)}) copy-start(pred[8]{0:T(512)(128)(4,1)} %copy-done.50) | copy-start | bytes 28
  24.1 5.6 %copy-start.53 = (pred[8]{0:T(512)(128)(4,1)S(1)}, pred[8]{0:T(512)(128)(4,1)}, u32[]{:S(2)}) copy-start(pred[8]{0:T(512)(128)(4,1)} %copy-done.52) | copy-start | bytes 28
  24.1 5.6 %copy-start.55 = (pred[8]{0:T(512)(128)(4,1)S(1)}, pred[8]{0:T(512)(128)(4,1)}, u32[]{:S(2)}) copy-start(pred[8]{0:T(512)(128)(4,1)} %copy-done.54) | copy-start | bytes 28
  24.1 5.6 %copy-start.57 = (pred[512]{0:T(512)(128)(4,1)S(1)}, pred[512]{0:T(512)(128)(4,1)}, u32[]{:S(2)}) copy-start(pred[512]{0:T(512)(128)(4,1)} %copy-done.56) | copy-start | bytes 1540
  24.1 19.1 %all-to-all-start.1 = ((bf16[4,128,1024]{2,1,0:T(8,128)(2,1)}), bf16[4,128,1024]{2,1,0:T(8,128)(2,1)S(1)}, u32[]{:S(2)}, u32[]{:S(2)}) async-start(bf16[4,128,1024]{2,1,0:T(8,128)(2,1)} %shard_map.181), calls=%async_computation.1 | async-start | bytes 2097152 | tf_op jit(solution)/shard_map/all_to_all | solution.py:846
  32.5 7.5 %copy-start.13 = (f32[8,512]{1,0:T(8,128)S(1)}, f32[8,512]{1,0:T(8,128)}, u32[]{:S(2)}) copy-start(f32[8,512]{1,0:T(8,128)} %select_maximum_fusion.chan_ref.refs_10_.refs_15_) | copy-start | bytes 49156
  35.9 11.9 %collective-permute-start.3 = (bf16[272,512]{1,0:T(8,128)(2,1)}, bf16[272,512]{1,0:T(8,128)(2,1)}, u32[]{:S(2)}, u32[]{:S(2)}) collective-permute-start(bf16[272,512]{1,0:T(8,128)(2,1)} %get-tuple-element.72), channel_id=1, source_target_pairs={{0,8},{2,10},{4,12},{6,14},{8,0},{10,2},{12,4},{14,6},{16,24},{18,... | collective-permute-start | bytes 835592 | tf_op jit(solution)/shard_map/ppermute | solution.py:746
  37.4 21.4 %collective-permute-start.4 = (bf16[272,512]{1,0:T(8,128)(2,1)}, bf16[272,512]{1,0:T(8,128)(2,1)}, u32[]{:S(2)}, u32[]{:S(2)}) collective-permute-start(bf16[272,512]{1,0:T(8,128)(2,1)} %get-tuple-element.72), channel_id=1, source_target_pairs={{0,16},{2,18},{4,20},{6,22},{8,24},{10,26},{12,28},{14,30},{16,0},... | collective-permute-start | bytes 835592 | tf_op jit(solution)/shard_map/ppermute | solution.py:746
  39.4 24.4 %collective-permute-start.5 = (bf16[272,512]{1,0:T(8,128)(2,1)}, bf16[272,512]{1,0:T(8,128)(2,1)}, u32[]{:S(2)}, u32[]{:S(2)}) collective-permute-start(bf16[272,512]{1,0:T(8,128)(2,1)} %get-tuple-element.72), channel_id=1, source_target_pairs={{0,24},{2,26},{4,28},{6,30},{8,16},{10,18},{12,20},{14,22},{16,8},... | collective-permute-start | bytes 835592 | tf_op jit(solution)/shard_map/ppermute | solution.py:746
  40.0 3.2 %copy-start.6 = (bf16[128,1024]{1,0:T(8,128)(2,1)S(1)}, bf16[128,1024]{1,0:T(8,128)(2,1)}, u32[]{:S(2)}) copy-start(bf16[128,1024]{1,0:T(8,128)(2,1)} %get-tuple-element.67) | copy-start | bytes 786436
  40.0 3.2 %copy-start.8 = (bf16[128,1024]{1,0:T(8,128)(2,1)S(1)}, bf16[128,1024]{1,0:T(8,128)(2,1)}, u32[]{:S(2)}) copy-start(bf16[128,1024]{1,0:T(8,128)(2,1)} %copy-done.7) | copy-start | bytes 786436
  40.0 3.2 %copy-start.10 = (bf16[128,1024]{1,0:T(8,128)(2,1)S(1)}, bf16[128,1024]{1,0:T(8,128)(2,1)}, u32[]{:S(2)}) copy-start(bf16[128,1024]{1,0:T(8,128)(2,1)} %copy-done.9) | copy-start | bytes 786436
  44.2 19.7 %copy-start.1 = (f32[512,512]{1,0:T(8,128)S(1)}, f32[512,512]{1,0:T(8,128)}, u32[]{:S(2)}) copy-start(f32[512,512]{1,0:T(8,128)} %copy-done) | copy-start | bytes 3145732
  44.2 19.7 %copy-start.14 = (f32[8,512]{1,0:T(8,128)S(1)}, f32[8,512]{1,0:T(8,128)}, u32[]{:S(2)}) copy-start(f32[8,512]{1,0:T(8,128)} %select_maximum_fusion.chan_ref.refs_10_.refs_15_) | copy-start | bytes 49156
  44.2 19.7 %copy-start.19 = (f32[8,8]{1,0:T(8,128)S(1)}, f32[8,8]{1,0:T(8,128)}, u32[]{:S(2)}) copy-start(f32[8,8]{1,0:T(8,128)} %get-tuple-element.80.refs_12_) | copy-start | bytes 772
  44.2 19.7 %copy-start.20 = (f32[8,8]{1,0:T(8,128)S(1)}, f32[8,8]{1,0:T(8,128)}, u32[]{:S(2)}) copy-start(f32[8,8]{1,0:T(8,128)} %get-tuple-element.79.refs_11_) | copy-start | bytes 772
  44.2 19.7 %copy-start.21 = (f32[8,8]{1,0:T(8,128)S(1)}, f32[8,8]{1,0:T(8,128)}, u32[]{:S(2)}) copy-start(f32[8,8]{1,0:T(8,128)} %concatenate.13.refs_13_) | copy-start | bytes 772
  44.3 19.6 %copy-start.18 = (f32[8,8]{1,0:T(8,128)S(1)}, f32[8,8]{1,0:T(8,128)}, u32[]{:S(2)}) copy-start(f32[8,8]{1,0:T(8,128)} %pad_convert_fusion.refs_14_) | copy-start | bytes 772
  44.3 35.1 %collective-permute-start.13 = (bf16[4,128,1024]{2,1,0:T(8,128)(2,1)S(1)}, bf16[4,128,1024]{2,1,0:T(8,128)(2,1)S(1)}, u32[]{:S(2)}, u32[]{:S(2)}) collective-permute-start(bf16[4,128,1024]{2,1,0:T(8,128)(2,1)S(1)} %shard_map.187.refs_2_), channel_id=1, source_target_pairs={{0,2},{2,0},{4,6},{6,4},{8,10},{10,8},{12,14},{14,12},{16,18},{18,... | collective-permute-start | bytes 3145736 | tf_op jit(solution)/shard_map/ppermute | solution.py:737
  46.3 33.0 %collective-permute-start.14 = (bf16[4,128,1024]{2,1,0:T(8,128)(2,1)S(1)}, bf16[4,128,1024]{2,1,0:T(8,128)(2,1)S(1)}, u32[]{:S(2)}, u32[]{:S(2)}) collective-permute-start(bf16[4,128,1024]{2,1,0:T(8,128)(2,1)S(1)} %shard_map.187.refs_2_), channel_id=1, source_target_pairs={{0,4},{2,6},{4,0},{6,2},{8,12},{10,14},{12,8},{14,10},{16,20},{18,... | collective-permute-start | bytes 3145736 | tf_op jit(solution)/shard_map/ppermute | solution.py:737
  67.9 1.2 collective-permute-start.6
  69.1 3.7 %collective-permute-start.7 = (f32[8,512]{1,0:T(8,128)S(1)}, f32[8,512]{1,0:T(8,128)S(1)}, u32[]{:S(2)}, u32[]{:S(2)}) collective-permute-start(f32[8,512]{1,0:T(8,128)S(1)} %add.334.refs_2_), channel_id=1, source_target_pairs={{0,2},{2,0},{4,6},{6,4},{8,10},{10,8},{12,14},{14,12},{16,18},{18,... | collective-permute-start | bytes 49160 | tf_op jit(solution)/shard_map/ppermute | solution.py:737
  70.8 3.7 %collective-permute-start.8 = (f32[8,512]{1,0:T(8,128)S(1)}, f32[8,512]{1,0:T(8,128)S(1)}, u32[]{:S(2)}, u32[]{:S(2)}) collective-permute-start(f32[8,512]{1,0:T(8,128)S(1)} %add.334.refs_2_), channel_id=1, source_target_pairs={{0,4},{2,6},{4,0},{6,2},{8,12},{10,14},{12,8},{14,10},{16,20},{18,... | collective-permute-start | bytes 49160 | tf_op jit(solution)/shard_map/ppermute | solution.py:737
  72.3 4.6 %collective-permute-start.9 = (f32[8,512]{1,0:T(8,128)S(1)}, f32[8,512]{1,0:T(8,128)S(1)}, u32[]{:S(2)}, u32[]{:S(2)}) collective-permute-start(f32[8,512]{1,0:T(8,128)S(1)} %add.334.refs_2_), channel_id=1, source_target_pairs={{0,6},{2,4},{4,2},{6,0},{8,14},{10,12},{12,10},{14,8},{16,22},{18,... | collective-permute-start | bytes 49160 | tf_op jit(solution)/shard_map/ppermute | solution.py:737
  79.4 12.3 %collective-permute-start.15 = (bf16[2,128,1024]{2,1,0:T(8,128)(2,1)S(1)}, bf16[2,128,1024]{2,1,0:T(8,128)(2,1)S(1)}, u32[]{:S(2)}, u32[]{:S(2)}) collective-permute-start(bf16[2,128,1024]{2,1,0:T(8,128)(2,1)S(1)} %slice.10), channel_id=1, source_target_pairs={{0,4},{2,6},{4,0},{6,2},{8,12},{10,14},{12,8},{14,10},{16,20},{18,... | collective-permute-start | bytes 1572872 | tf_op jit(solution)/shard_map/ppermute | solution.py:737
  80.1 12.2 %collective-permute-start.16 = (bf16[2,128,1024]{2,1,0:T(8,128)(2,1)S(1)}, bf16[2,128,1024]{2,1,0:T(8,128)(2,1)S(1)}, u32[]{:S(2)}, u32[]{:S(2)}) collective-permute-start(bf16[2,128,1024]{2,1,0:T(8,128)(2,1)S(1)} %slice.11), channel_id=1, source_target_pairs={{0,2},{2,0},{4,6},{6,4},{8,10},{10,8},{12,14},{14,12},{16,18},{18,... | collective-permute-start | bytes 1572872 | tf_op jit(solution)/shard_map/ppermute | solution.py:737
  80.4 26.6 %collective-permute-start.10 = (bf16[256,512]{1,0:T(8,128)(2,1)S(1)}, bf16[256,512]{1,0:T(8,128)(2,1)S(1)}, u32[]{:S(2)}, u32[]{:S(2)}) collective-permute-start(bf16[256,512]{1,0:T(8,128)(2,1)S(1)} %get-tuple-element.86), channel_id=1, source_target_pairs={{0,8},{2,10},{4,12},{6,14},{8,0},{10,2},{12,4},{14,6},{16,24},{18,... | collective-permute-start | bytes 786440 | tf_op jit(solution)/shard_map/ppermute | solution.py:746
  80.4 26.6 %collective-permute-start.11 = (bf16[256,512]{1,0:T(8,128)(2,1)S(1)}, bf16[256,512]{1,0:T(8,128)(2,1)S(1)}, u32[]{:S(2)}, u32[]{:S(2)}) collective-permute-start(bf16[256,512]{1,0:T(8,128)(2,1)S(1)} %get-tuple-element.86), channel_id=1, source_target_pairs={{0,16},{2,18},{4,20},{6,22},{8,24},{10,26},{12,28},{14,30},{16,0},... | collective-permute-start | bytes 786440 | tf_op jit(solution)/shard_map/ppermute | solution.py:746
  83.3 23.7 %collective-permute-start.12 = (bf16[256,512]{1,0:T(8,128)(2,1)S(1)}, bf16[256,512]{1,0:T(8,128)(2,1)S(1)}, u32[]{:S(2)}, u32[]{:S(2)}) collective-permute-start(bf16[256,512]{1,0:T(8,128)(2,1)S(1)} %get-tuple-element.86), channel_id=1, source_target_pairs={{0,24},{2,26},{4,28},{6,30},{8,16},{10,18},{12,20},{14,22},{16,8},... | collective-permute-start | bytes 786440 | tf_op jit(solution)/shard_map/ppermute | solution.py:746
  83.9 8.3 %copy-start.2 = (bf16[128,2048]{1,0:T(8,128)(2,1)S(1)}, bf16[128,2048]{1,0:T(8,128)(2,1)}, u32[]{:S(2)}) copy-start(bf16[128,2048]{1,0:T(8,128)(2,1)} %refs_7_.1) | copy-start | bytes 1572868
  83.9 8.3 %copy-start.3 = (bf16[128,2048]{1,0:T(8,128)(2,1)S(1)}, bf16[128,2048]{1,0:T(8,128)(2,1)}, u32[]{:S(2)}) copy-start(bf16[128,2048]{1,0:T(8,128)(2,1)} %refs_8_.1) | copy-start | bytes 1572868
  83.9 8.3 %copy-start.17 = (s32[2,16]{1,0:T(2,128)S(1)}, s32[2,16]{1,0:T(2,128)}, u32[]{:S(2)}) copy-start(s32[2,16]{1,0:T(2,128)} %pad_add_fusion.2.refs_0_) | copy-start | bytes 388
  83.9 8.3 %copy-start.25 = (s32[2]{0:T(128)S(1)}, s32[2]{0:T(128)}, u32[]{:S(2)}) copy-start(s32[2]{0:T(128)} %pad_add_fusion.5.refs_1_) | copy-start | bytes 28
  87.8 19.3 %copy-start.16 = (f32[512,128]{1,0:T(8,128)S(1)}, f32[512,128]{1,0:T(8,128)}, u32[]{:S(2)}) copy-start(f32[512,128]{1,0:T(8,128)} %copy-done.15) | copy-start | bytes 786436
  110.5 10.5 %collective-permute-start.17 = (bf16[128,1280]{1,0:T(8,128)(2,1)S(1)}, bf16[128,1280]{1,0:T(8,128)(2,1)S(1)}, u32[]{:S(2)}, u32[]{:S(2)}) collective-permute-start(bf16[128,1280]{1,0:T(8,128)(2,1)S(1)} %get-tuple-element.115), channel_id=1, source_target_pairs={{0,2},{2,0},{4,6},{6,4},{8,10},{10,8},{12,14},{14,12},{16,18},{18,... | collective-permute-start | bytes 983048 | tf_op jit(solution)/shard_map/ppermute | solution.py:737
  110.9 10.5 %collective-permute-start.18 = (bf16[128,1280]{1,0:T(8,128)(2,1)S(1)}, bf16[128,1280]{1,0:T(8,128)(2,1)S(1)}, u32[]{:S(2)}, u32[]{:S(2)}) collective-permute-start(bf16[128,1280]{1,0:T(8,128)(2,1)S(1)} %get-tuple-element.116), channel_id=1, source_target_pairs={{0,4},{2,6},{4,0},{6,2},{8,12},{10,14},{12,8},{14,10},{16,20},{18,... | collective-permute-start | bytes 983048 | tf_op jit(solution)/shard_map/ppermute | solution.py:737
  112.5 12.8 %collective-permute-start.19 = (bf16[128,1280]{1,0:T(8,128)(2,1)S(1)}, bf16[128,1280]{1,0:T(8,128)(2,1)S(1)}, u32[]{:S(2)}, u32[]{:S(2)}) collective-permute-start(bf16[128,1280]{1,0:T(8,128)(2,1)S(1)} %get-tuple-element.117), channel_id=1, source_target_pairs={{0,6},{2,4},{4,2},{6,0},{8,14},{10,12},{12,10},{14,8},{16,22},{18,... | collective-permute-start | bytes 983048 | tf_op jit(solution)/shard_map/ppermute | solution.py:737
  (18 other events, 15.8 us)

commit v4 on v3

--- a/solution.py
+++ b/solution.py
@@ -12,7 +12,7 @@
 EXTRA = 16
 NORM_EPS = 1e-05
 NEG_FILL = -1e30
-KEY_CHUNK = 512
+KEY_CHUNK = 1024
 LOG2_E = 1.4426950408889634
 F32 = jnp.float32
 BF16 = jnp.bfloat16
@@ -602,18 +602,26 @@
         blocks_ref, own_ref = refs[:2]
         piece_refs = refs[2 : 2 + n_pieces]
         q_ref, g_ref, out_ref, dq_ref, kv, scores, q_all, g_all = refs[2 + n_pieces :]
+        every = range(kv_heads)
+        k_at = [slice(g * AHD, (g + 1) * AHD) for g in every]
+        v_at = [slice(half_width + 2 * g * AHD, half_width + (2 * g + 1) * AHD) for g in every]
+        w_at = [slice(half_width + 2 * g * AHD, half_width + (2 * g + 2) * AHD) for g in every]
+        for g in every:
+            kv[:, half_width + (2 * g + 1) * AHD : half_width + (2 * g + 2) * AHD] = jnp.ones(
+                (tokens, AHD), BF16
+            )
         index = 0
         for ref in piece_refs:
             for u in range(ref.shape[0]):
                 for half in range(2):
                     at = pl.ds(pl.multiple_of(blocks_ref[half, index] * STRETCH, 64), STRETCH)
-                    kv[at, :] = ref[u, half * STRETCH : (half + 1) * STRETCH, :]
+                    rows_at = slice(half * STRETCH, (half + 1) * STRETCH)
+                    kv[at, 0:half_width] = ref[u, rows_at, 0:half_width]
+                    for g in range(kv_heads):
+                        kv[at, v_at[g]] = ref[u, rows_at, half_width + g * AHD : half_width + (g + 1) * AHD]
                 index += 1
         offset = lax.broadcasted_iota(jnp.int32, (tall, chunk), 0) % STRETCH
         column = lax.broadcasted_iota(jnp.int32, (tall, chunk), 1)
-        every = range(kv_heads)
-        k_at = [slice(g * AHD, (g + 1) * AHD) for g in every]
-        v_at = [slice(half_width + g * AHD, half_width + (g + 1) * AHD) for g in every]
 
         def stacked(ref, src, g):
             parts = [ref[src, (g * per_kv + i) * AHD : (g * per_kv + i + 1) * AHD] for i in range(per_kv)]
@@ -638,29 +646,30 @@
                     value = mm_nt(q_all[g], kv[keys_of(c), k_at[g]]) * (scale * LOG2_E)
                     value = jnp.where(kept, value, NEG_FILL)
                     scores[g, c] = value
-                    new.append(jnp.maximum(peaks[g], jnp.max(value, axis=1, keepdims=True)))
+                    best = peaks[g]
+                    for i in range(chunk // 128):
+                        best = jnp.maximum(best, value[:, i * 128 : (i + 1) * 128])
+                    new.append(best)
                 return tuple(new)
 
             peaks = lax.fori_loop(
-                0, steps, first, tuple(jnp.full((tall, 1), NEG_FILL, F32) for _ in every)
+                0, steps, first, tuple(jnp.full((tall, 128), NEG_FILL, F32) for _ in every)
             )
+            peaks = [jnp.max(peak, axis=1, keepdims=True) for peak in peaks]
 
             def second(c, carry):
                 new = []
                 for g in every:
-                    total, out = carry[g]
                     value = jnp.exp2(scores[g, c] - peaks[g])
                     scores[g, c] = value
-                    out = out + mm(value.astype(BF16), kv[keys_of(c), v_at[g]])
-                    new.append((total + jnp.sum(value, axis=1, keepdims=True), out))
+                    new.append(carry[g] + mm(value.astype(BF16), kv[keys_of(c), w_at[g]]))
                 return tuple(new)
 
-            empty = (jnp.zeros((tall, 1), F32), jnp.zeros((tall, AHD), F32))
+            empty = jnp.zeros((tall, 2 * AHD), F32)
             done = lax.fori_loop(0, steps, second, tuple(empty for _ in every))
             deltas = []
             for g in every:
-                total, out = done[g]
-                out = (out / total).astype(BF16)
+                out = (done[g][:, :AHD] / done[g][:, AHD:]).astype(BF16)
                 deltas.append(
                     jnp.sum(g_all[g].astype(F32) * out.astype(F32), axis=1, keepdims=True)
                 )
@@ -680,7 +689,7 @@
                 0, steps, third, tuple(jnp.zeros((tall, AHD), F32) for _ in every)
             )
             for g in every:
-                change = (changes[g] * (scale / done[g][0])).astype(BF16)
+                change = (changes[g] * (scale / done[g][:, AHD:])).astype(BF16)
                 for i in range(per_kv):
                     at = slice((g * per_kv + i) * AHD, (g * per_kv + i + 1) * AHD)
                     dq_ref[src, at] = change[i * STRETCH : (i + 1) * STRETCH]
@@ -691,12 +700,12 @@
         (blocks, own_blocks, *pieces, queries, grads),
         smem=(0, 1),
         scratch=[
-            pltpu.VMEM((tokens, 2 * half_width), BF16),
+            pltpu.VMEM((tokens, 3 * half_width), BF16),
             pltpu.VMEM((kv_heads, tokens // chunk, tall, chunk), F32),
             pltpu.VMEM((kv_heads, tall, AHD), BF16),
             pltpu.VMEM((kv_heads, tall, AHD), BF16),
         ],
-        mib=24,
+        mib=36,
         flops=10 * queries.size * tokens,
         nbytes=4 * tokens * half_width,
     )

time: 127 us -> 126 us (level)
  Pallas kernels: 37.5 us -> 35.9 us
    pallas_call x10, Pallas kernels: 34.4 us -> 32.8 us  [call(): pl.pallas_call(fn, out_shape=tuple((jax.ShapeDtypeStruct(s, d) for s, d i...]
  transfers between devices with their start and end apart: 22 -> 22, of which waited for: 12 -> 12; matrix products, arithmetic and copies ran while one was open for 6% -> 6% of each run, Pallas kernels for 24% -> 23%
where the time goes in v4:
time: 126 us; the launch traced here: 125 us
  waiting for transfers between devices  41.4 us (33%)
  Pallas kernels  35.9 us (28%)
  starting transfers between devices  30.1 us (24%)
  local copies, waits for them, and re-layouts  10.8 us (9%)
  other arithmetic  5.16 us (4%)
  between operations  1.53 us (1%)
    pallas_call x10, Pallas kernels, call(): pl.pallas_call(fn, out_shape=tuple((jax.ShapeDtypeStruct(s, d) for s, d i...  32.8 us
    ppermute x10, waiting for transfers between devices, to_place(): return lax.ppermute(value, 'ctx', pairs)  20 us
    ppermute x9, waiting for transfers between devices, across(): moved.append(lax.ppermute(value, 'ctx', pairs))  16.1 us
    ppermute x10, starting transfers between devices, to_place(): return lax.ppermute(value, 'ctx', pairs)  11.6 us
    ppermute x9, starting transfers between devices, across(): moved.append(lax.ppermute(value, 'ctx', pairs))  11.1 us
    unnamed x121, local copies, waits for them, and re-layouts  8.88 us
    all_to_all x1, waiting for transfers between devices, body(): lax.all_to_all(packed, 'ctx', 0, 0, axis_index_groups=planes, tiled=True)  4.18 us
    all_to_all x1, starting transfers between devices, body(): lax.all_to_all(packed, 'ctx', 0, 0, axis_index_groups=planes, tiled=True)  3.85 us
  transfers between devices with their start and end apart: 22, of which 12 were waited for; matrix products, arithmetic and copies ran while one was open for 6% of the time, Pallas kernels for 23%

profile of v4, /device:TPU:8, one launch (start us, length us, event | category | flops | bytes accessed | tf_op | source)
XLA Modules:
  0.0 124.9 jit_solution(16381485745274499126)
XLA Ops:
  0.6 1.4 %copy.21.step_ref = f32[128,32]{1,0:T(8,128)} copy(f32[128,32]{0,1:T(8,128)} %param.23) | data formatting | bytes 32768 | tf_op args[9]
  2.1 3.1 %shard_map.182 = (bf16[128,1024]{1,0:T(8,128)(2,1)}, bf16[4,128,896]{2,1,0:T(8,128)(2,1)}) custom-call(f32[128,32]{1,0:T(8,128)} %copy.21.step_ref, bf16[128,2048]{1,0:T(8,128)(2,1)} %refs_0_.1, bf16[128,512]{1,0:T(8,128)(2,1)} %refs_1_.1, bf16[128,512]{1,0:T(8,128)(2,1)} %refs_2_.1, bf16[128,512]{1,0:T(8,128)(2,1)} %refs_3_.1, bf16[128,512]{1,0:T(8,128)(2,1)} %refs_4_.1), custom_call_target="tpu_custom_call" | custom-call | bytes 1024 | tf_op jit(solution)/shard_map/pallas_call | solution.py:150
  5.3 3.0 %collective-permute-start.1 = (bf16[128,1024]{1,0:T(8,128)(2,1)}, bf16[128,1024]{1,0:T(8,128)(2,1)S(1)}, u32[]{:S(2)}, u32[]{:S(2)}) collective-permute-start(bf16[128,1024]{1,0:T(8,128)(2,1)} %get-tuple-element.67), channel_id=1, source_target_pairs={{0,16},{2,18},{4,20},{6,22},{8,24},{10,26},{12,28},{14,30},{16,0},... | collective-permute-start | bytes 786440 | tf_op jit(solution)/shard_map/ppermute | solution.py:755
  8.3 0.5 collective-permute-start.2
  8.8 3.8 %all-to-all-start = ((bf16[4,128,896]{2,1,0:T(8,128)(2,1)}), bf16[4,128,896]{2,1,0:T(8,128)(2,1)S(1)}, u32[]{:S(2)}, u32[]{:S(2)}) async-start(bf16[4,128,896]{2,1,0:T(8,128)(2,1)} %get-tuple-element.65), calls=%async_computation | async-start | bytes 1835008 | tf_op jit(solution)/shard_map/all_to_all | solution.py:773
  13.1 0.1 le.28
  13.5 0.7 compare_convert_fusion.2
  14.3 0.7 fusion.refs_2_.info_ref.refs_9_.refs_14_
  15.0 0.1 add_add_fusion
  15.3 0.7 copy-done.58
  16.1 0.6 pad_convert_fusion.refs_14_
  16.7 0.8 dynamic_slice.11
  17.5 1.0 shard_map.181
  18.6 0.6 pad_add_fusion.2.refs_0_
  19.2 0.6 select_maximum_fusion.chan_ref.refs_10_.refs_15_
  19.9 4.2 %all-to-all-done.refs_1_ = bf16[4,128,896]{2,1,0:T(8,128)(2,1)S(1)} async-done(((bf16[4,128,896]{2,1,0:T(8,128)(2,1)}), bf16[4,128,896]{2,1,0:T(8,128)(2,1)S(1)}, u32[]{:S(2)}, u32[]{:S(2)}) %all-to-all-start) | async-done | bytes 917536 | tf_op jit(solution)/shard_map/all_to_all | solution.py:773
  24.1 3.5 %all-to-all-start.1 = ((bf16[4,128,1024]{2,1,0:T(8,128)(2,1)}), bf16[4,128,1024]{2,1,0:T(8,128)(2,1)S(1)}, u32[]{:S(2)}, u32[]{:S(2)}) async-start(bf16[4,128,1024]{2,1,0:T(8,128)(2,1)} %shard_map.181), calls=%async_computation.1 | async-start | bytes 2097152 | tf_op jit(solution)/shard_map/all_to_all | solution.py:855
  27.7 0.7 compare_convert_fusion
  28.3 0.6 pad_add_fusion.5.refs_1_
  28.9 0.6 concatenate.13.refs_13_
  29.7 0.5 copy-done.27
  30.2 0.1 fusion.7.refs_3_.info_t_ref.refs_9_
  30.4 0.7 copy-done.7
  31.1 0.7 copy-done.9
  31.8 0.7 copy-done.11
  32.5 2.7 %shard_map.183 = (bf16[272,512]{1,0:T(8,128)(2,1)}, bf16[512,512]{1,0:T(8,128)(2,1)S(1)}, bf16[512,128]{1,0:T(8,128)(2,1)S(1)}, bf16[512,128]{1,0:T(8,128)(2,1)S...) custom-call(s32[1]{0:T(128)} %bitcast.refs_0_.me_ref, ...), custom_call_target="tpu_custom_call" | custom-call | flops 134217 | bytes 1572 | tf_op jit(solution)/shard_map/pallas_call | solution.py:59
  35.2 0.7 copy-done.15
  35.9 1.4 %collective-permute-start.3 = (bf16[272,512]{1,0:T(8,128)(2,1)}, bf16[272,512]{1,0:T(8,128)(2,1)}, u32[]{:S(2)}, u32[]{:S(2)}) collective-permute-start(bf16[272,512]{1,0:T(8,128)(2,1)} %get-tuple-element.72), channel_id=1, source_target_pairs={{0,8},{2,10},{4,12},{6,14},{8,0},{10,2},{12,4},{14,6},{16,24},{18,... | collective-permute-start | bytes 835592 | tf_op jit(solution)/shard_map/ppermute | solution.py:755
  37.4 2.1 %collective-permute-start.4 = (bf16[272,512]{1,0:T(8,128)(2,1)}, bf16[272,512]{1,0:T(8,128)(2,1)}, u32[]{:S(2)}, u32[]{:S(2)}) collective-permute-start(bf16[272,512]{1,0:T(8,128)(2,1)} %get-tuple-element.72), channel_id=1, source_target_pairs={{0,16},{2,18},{4,20},{6,22},{8,24},{10,26},{12,28},{14,30},{16,0},... | collective-permute-start | bytes 835592 | tf_op jit(solution)/shard_map/ppermute | solution.py:755
  39.4 0.6 collective-permute-start.5
  40.0 2.2 %shard_map.184.refs_6_ = f32[512,512]{1,0:T(8,128)S(1)} custom-call(bf16[512,512]{1,0:T(8,128)(2,1)S(1)} %get-tuple-element.73.x_ref.refs_4_, bf16[512,128]{1,0:T(8,128)(2,1)S(1)} %get-tuple-element.74.w_ref.refs_5_, bf16[512,128]{1,0:T(8,128)(2,1)S(1)} %get-tuple-element.75.r_ref.refs_7_, f32[512,128]{1,0:T(8,128)S(1)} %get-tuple-element.76.cum_ref.refs_8_, ...), custom_call_target="tpu_custom_call" | custom-call | flops 536870 | bytes 2097 | tf_op jit(solution)/shard_map/pallas_call | solution.py:59
  42.2 1.0 copy-done
  43.2 0.9 copy-done.12
  44.3 2.1 %collective-permute-start.13 = (bf16[4,128,1024]{2,1,0:T(8,128)(2,1)S(1)}, bf16[4,128,1024]{2,1,0:T(8,128)(2,1)S(1)}, u32[]{:S(2)}, u32[]{:S(2)}) collective-permute-start(bf16[4,128,1024]{2,1,0:T(8,128)(2,1)S(1)} %shard_map.187.refs_2_), channel_id=1, source_target_pairs={{0,2},{2,0},{4,6},{6,4},{8,10},{10,8},{12,14},{14,12},{16,18},{18,... | collective-permute-start | bytes 3145736 | tf_op jit(solution)/shard_map/ppermute | solution.py:746
  46.3 1.5 %collective-permute-start.14 = (bf16[4,128,1024]{2,1,0:T(8,128)(2,1)S(1)}, bf16[4,128,1024]{2,1,0:T(8,128)(2,1)S(1)}, u32[]{:S(2)}, u32[]{:S(2)}) collective-permute-start(bf16[4,128,1024]{2,1,0:T(8,128)(2,1)S(1)} %shard_map.187.refs_2_), channel_id=1, source_target_pairs={{0,4},{2,6},{4,0},{6,2},{8,12},{10,14},{12,8},{14,10},{16,20},{18,... | collective-permute-start | bytes 3145736 | tf_op jit(solution)/shard_map/ppermute | solution.py:746
  47.8 11.0 %collective-permute-done.4 = bf16[272,512]{1,0:T(8,128)(2,1)} collective-permute-done((bf16[272,512]{1,0:T(8,128)(2,1)}, bf16[272,512]{1,0:T(8,128)(2,1)}, u32[]{:S(2)}, u32[]{:S(2)}) %collective-permute-start.4) | collective-permute-done | bytes 278560 | tf_op jit(solution)/shard_map/ppermute | solution.py:755
  58.8 5.1 %collective-permute-done.5 = bf16[272,512]{1,0:T(8,128)(2,1)} collective-permute-done((bf16[272,512]{1,0:T(8,128)(2,1)}, bf16[272,512]{1,0:T(8,128)(2,1)}, u32[]{:S(2)}, u32[]{:S(2)}) %collective-permute-start.5) | collective-permute-done | bytes 278560 | tf_op jit(solution)/shard_map/ppermute | solution.py:755
  63.9 0.6 copy-done.23
  64.5 3.4 %shard_map.185 = (f32[512,512]{1,0:T(8,128)S(1)}, f32[8,512]{1,0:T(8,128)S(1)}, bf16[256,512]{1,0:T(8,128)(2,1)S(1)}, f32[8,512]{1,0:T(8,128)S(1)}, f32[8,512]{1,0:T(8,128)S(1)}) custom-call(s32[1]{0:T(128)} %bitcast.refs_0_.me_ref, bf16[1,272,512]{2,1,0:T(8,128)(2,1)} %bitcast.14.refs_1_, bf16[1,272,512]{2,1,0:T(8,128)(2,1)} %bitcast.15.refs_2_, ...), custom_call_target="tpu_custom_call" | custom-call | flops 35000000512 | bytes 4194 | tf_op jit(solution)/shard_map/pallas_call | solution.py:59
  68.0 1.2 collective-permute-done.6
  69.1 1.7 %collective-permute-start.7 = (f32[8,512]{1,0:T(8,128)S(1)}, f32[8,512]{1,0:T(8,128)S(1)}, u32[]{:S(2)}, u32[]{:S(2)}) collective-permute-start(f32[8,512]{1,0:T(8,128)S(1)} %add.334.refs_2_), channel_id=1, source_target_pairs={{0,2},{2,0},{4,6},{6,4},{8,10},{10,8},{12,14},{14,12},{16,18},{18,... | collective-permute-start | bytes 49160 | tf_op jit(solution)/shard_map/ppermute | solution.py:746
  70.8 1.5 %collective-permute-start.8 = (f32[8,512]{1,0:T(8,128)S(1)}, f32[8,512]{1,0:T(8,128)S(1)}, u32[]{:S(2)}, u32[]{:S(2)}) collective-permute-start(f32[8,512]{1,0:T(8,128)S(1)} %add.334.refs_2_), channel_id=1, source_target_pairs={{0,4},{2,6},{4,0},{6,2},{8,12},{10,14},{12,8},{14,10},{16,20},{18,... | collective-permute-start | bytes 49160 | tf_op jit(solution)/shard_map/ppermute | solution.py:746
  72.3 0.3 collective-permute-start.9
  72.6 0.2 collective-permute-done.7.refs_3_
  72.9 1.7 %collective-permute-done.8.refs_4_ = f32[8,512]{1,0:T(8,128)S(1)} collective-permute-done((f32[8,512]{1,0:T(8,128)S(1)}, f32[8,512]{1,0:T(8,128)S(1)}, u32[]{:S(2)}, u32[]{:S(2)}) %collective-permute-start.8) | collective-permute-done | bytes 16416 | tf_op jit(solution)/shard_map/ppermute | solution.py:746
  74.6 2.4 %collective-permute-done.9.refs_5_ = f32[8,512]{1,0:T(8,128)S(1)} collective-permute-done((f32[8,512]{1,0:T(8,128)S(1)}, f32[8,512]{1,0:T(8,128)S(1)}, u32[]{:S(2)}, u32[]{:S(2)}) %collective-permute-start.9) | collective-permute-done | bytes 16416 | tf_op jit(solution)/shard_map/ppermute | solution.py:746
  76.9 2.4 %shard_map.186 = (bf16[256,512]{1,0:T(8,128)(2,1)S(1)}, f32[512,512]{1,0:T(8,128)S(1)}, bf16[512,512]{1,0:T(8,128)(2,1)S(1)}, f32[512,128]{1,0:T(8,128)S(1)}) custom-call(s32[1]{0:T(128)} %bitcast.refs_0_.me_ref, bf16[4,128,1024]{2,1,0:T(8,128)(2,1)S(1)} %all-to-all-done.1.refs_5_.refs_1_, f32[8,512]{1,0:T(8,128)S(1)} %add.334.refs_2_, ...), custom_call_target="tpu_custom_call" | custom-call | flops 134217 | bytes 4194 | tf_op jit(solution)/shard_map/pallas_call | solution.py:59
  79.4 0.6 collective-permute-start.15
  80.1 0.4 collective-permute-start.16
  80.4 2.9 %collective-permute-start.11 = (bf16[256,512]{1,0:T(8,128)(2,1)S(1)}, bf16[256,512]{1,0:T(8,128)(2,1)S(1)}, u32[]{:S(2)}, u32[]{:S(2)}) collective-permute-start(bf16[256,512]{1,0:T(8,128)(2,1)S(1)} %get-tuple-element.86), channel_id=1, source_target_pairs={{0,16},{2,18},{4,20},{6,22},{8,24},{10,26},{12,28},{14,30},{16,0},... | collective-permute-start | bytes 786440 | tf_op jit(solution)/shard_map/ppermute | solution.py:755
  83.3 0.6 collective-permute-start.12
  83.9 3.8 %shard_map.189 = (f32[512,512]{1,0:T(8,128)S(1)}, f32[512,128]{1,0:T(8,128)S(1)}, f32[512,128]{1,0:T(8,128)S(1)}) custom-call(bf16[512,512]{1,0:T(8,128)(2,1)S(1)} %get-tuple-element.73.x_ref.refs_4_, bf16[512,128]{1,0:T(8,128)(2,1)S(1)} %get-tuple-element.74.w_ref.refs_5_, bf16[512,128]{1,0:T(8,128)(2,1)S(1)} %get-tuple-element.75.r_ref.refs_7_, ...), custom_call_target="tpu_custom_call" | custom-call | flops 1073741 | bytes 4194 | tf_op jit(solution)/shard_map/pallas_call | solution.py:59
  87.8 4.0 %collective-permute-done.15.refs_5_ = bf16[2,128,1024]{2,1,0:T(8,128)(2,1)S(1)} collective-permute-done((bf16[2,128,1024]{2,1,0:T(8,128)(2,1)S(1)}, bf16[2,128,1024]{2,1,0:T(8,128)(2,1)S(1)}, u32[]{:S(2)}, u32[]{:S(2)}) %collective-permute-start.15) | collective-permute-done | bytes 524320 | tf_op jit(solution)/shard_map/ppermute | solution.py:746
  91.7 0.5 collective-permute-done.16.refs_6_
  92.2 13.2 %shard_map.188 = (bf16[128,2048]{1,0:T(8,128)(2,1)}, bf16[128,2048]{1,0:T(8,128)(2,1)}) custom-call(s32[2,16]{1,0:T(2,128)S(1)} %copy-done.17, s32[2]{0:T(128)S(1)} %copy-done.25, bf16[4,128,1024]{2,1,0:T(8,128)(2,1)S(1)} %shard_map.187.refs_2_, bf16[4,128,1024]{2,1,0:T(8,128)(2,1)S(1)} %collective-permute-done.13.refs_3_, ...), custom_call_target="tpu_custom_call" | custom-call | flops 5368709 | bytes 4194 | tf_op jit(solution)/shard_map/pallas_call | solution.py:59
  105.5 0.6 copy-done.24
  106.1 2.8 %shard_map.190 = (bf16[128,1280]{1,0:T(8,128)(2,1)S(1)}, bf16[128,1280]{1,0:T(8,128)(2,1)S(1)}, bf16[128,1280]{1,0:T(8,128)(2,1)S(1)}, bf16[128,1280]{1,0:T(8,128)(2,1)S(1)}) custom-call(bf16[1,256,512]{2,1,0:T(8,128)(2,1)S(1)} %bitcast.28, bf16[1,256,512]{2,1,0:T(8,128)(2,1)S(1)} %bitcast.29, bf16[1,256,512]{2,1,0:T(8,128)(2,1)S(1)} %bitcast.30, ...), custom_call_target="tpu_custom_call" | custom-call | flops 268435 | bytes 4194 | tf_op jit(solution)/shard_map/pallas_call | solution.py:59
  108.9 1.0 collective-permute-start.17
  110.0 1.4 %collective-permute-start.18 = (bf16[128,1280]{1,0:T(8,128)(2,1)S(1)}, bf16[128,1280]{1,0:T(8,128)(2,1)S(1)}, u32[]{:S(2)}, u32[]{:S(2)}) collective-permute-start(bf16[128,1280]{1,0:T(8,128)(2,1)S(1)} %get-tuple-element.116), channel_id=1, source_target_pairs={{0,4},{2,6},{4,0},{6,2},{8,12},{10,14},{12,8},{14,10},{16,20},{18,... | collective-permute-start | bytes 983048 | tf_op jit(solution)/shard_map/ppermute | solution.py:746
  111.4 1.1 collective-permute-start.19
  112.5 7.0 %collective-permute-done.17.refs_1_ = bf16[128,1280]{1,0:T(8,128)(2,1)S(1)} collective-permute-done((bf16[128,1280]{1,0:T(8,128)(2,1)S(1)}, bf16[128,1280]{1,0:T(8,128)(2,1)S(1)}, u32[]{:S(2)}, u32[]{:S(2)}) %collective-permute-start.17) | collective-permute-done | bytes 327712 | tf_op jit(solution)/shard_map/ppermute | solution.py:746
  119.4 3.2 %collective-permute-done.18.refs_2_ = bf16[128,1280]{1,0:T(8,128)(2,1)S(1)} collective-permute-done((bf16[128,1280]{1,0:T(8,128)(2,1)S(1)}, bf16[128,1280]{1,0:T(8,128)(2,1)S(1)}, u32[]{:S(2)}, u32[]{:S(2)}) %collective-permute-start.18) | collective-permute-done | bytes 327712 | tf_op jit(solution)/shard_map/ppermute | solution.py:746
  122.6 1.1 collective-permute-done.19.refs_3_
  123.7 1.2 shard_map.191
  (149 shorter events, 1.4 us)
Async XLA Ops:
  5.2 25.1 %collective-permute-start = (bf16[128,1024]{1,0:T(8,128)(2,1)}, bf16[128,1024]{1,0:T(8,128)(2,1)S(1)}, u32[]{:S(2)}, u32[]{:S(2)}) collective-permute-start(bf16[128,1024]{1,0:T(8,128)(2,1)} %get-tuple-element.67), channel_id=1, source_target_pairs={{0,8},{2,10},{4,12},{6,14},{8,0},{10,2},{12,4},{14,6},{16,24},{18,... | collective-permute-start | bytes 786440 | tf_op jit(solution)/shard_map/ppermute | solution.py:755
  5.3 25.8 %collective-permute-start.1 = (bf16[128,1024]{1,0:T(8,128)(2,1)}, bf16[128,1024]{1,0:T(8,128)(2,1)S(1)}, u32[]{:S(2)}, u32[]{:S(2)}) collective-permute-start(bf16[128,1024]{1,0:T(8,128)(2,1)} %get-tuple-element.67), channel_id=1, source_target_pairs={{0,16},{2,18},{4,20},{6,22},{8,24},{10,26},{12,28},{14,30},{16,0},... | collective-permute-start | bytes 786440 | tf_op jit(solution)/shard_map/ppermute | solution.py:755
  8.3 23.5 %collective-permute-start.2 = (bf16[128,1024]{1,0:T(8,128)(2,1)}, bf16[128,1024]{1,0:T(8,128)(2,1)S(1)}, u32[]{:S(2)}, u32[]{:S(2)}) collective-permute-start(bf16[128,1024]{1,0:T(8,128)(2,1)} %get-tuple-element.67), channel_id=1, source_target_pairs={{0,24},{2,26},{4,28},{6,30},{8,16},{10,18},{12,20},{14,22},{16,8},... | collective-permute-start | bytes 786440 | tf_op jit(solution)/shard_map/ppermute | solution.py:755
  8.8 3.9 %copy-start.38 = (s32[16]{0:T(128)S(1)}, s32[16]{0:T(128)}, u32[]{:S(2)}) copy-start(s32[16]{0:T(128)} %param.14) | copy-start | bytes 196
  8.8 8.7 %copy-start.5 = (bf16[128,2048]{1,0:T(8,128)(2,1)S(1)}, bf16[128,2048]{1,0:T(8,128)(2,1)}, u32[]{:S(2)}) copy-start(bf16[128,2048]{1,0:T(8,128)(2,1)} %grad_ref.1) | copy-start | bytes 1572868
  8.8 15.3 %all-to-all-start = ((bf16[4,128,896]{2,1,0:T(8,128)(2,1)}), bf16[4,128,896]{2,1,0:T(8,128)(2,1)S(1)}, u32[]{:S(2)}, u32[]{:S(2)}) async-start(bf16[4,128,896]{2,1,0:T(8,128)(2,1)} %get-tuple-element.65), calls=%async_computation | async-start | bytes 1835008 | tf_op jit(solution)/shard_map/all_to_all | solution.py:773
  12.6 4.9 %copy-start.4 = (bf16[128,2048]{1,0:T(8,128)(2,1)S(1)}, bf16[128,2048]{1,0:T(8,128)(2,1)}, u32[]{:S(2)}) copy-start(bf16[128,2048]{1,0:T(8,128)(2,1)} %gate_ref) | copy-start | bytes 1572868
  12.7 1.4 %copy-start.26 = (s32[512]{0:T(512)}, s32[512]{0:T(512)S(1)}, u32[]{:S(2)}) copy-start(s32[512]{0:T(512)S(1)} %get-tuple-element.133) | copy-start | bytes 6148
  12.7 1.4 %copy-start.28 = (s32[512]{0:T(512)}, s32[512]{0:T(512)S(1)}, u32[]{:S(2)}) copy-start(s32[512]{0:T(512)S(1)} %get-tuple-element.134) | copy-start | bytes 6148
  12.7 1.4 %copy-start.30 = (s32[512]{0:T(512)}, s32[512]{0:T(512)S(1)}, u32[]{:S(2)}) copy-start(s32[512]{0:T(512)S(1)} %get-tuple-element.135) | copy-start | bytes 6148
  12.8 1.4 %copy-start.32 = (s32[512]{0:T(512)}, s32[512]{0:T(512)S(1)}, u32[]{:S(2)}) copy-start(s32[512]{0:T(512)S(1)} %get-tuple-element.136) | copy-start | bytes 6148
  12.8 1.4 %copy-start.34 = (s32[512]{0:T(512)}, s32[512]{0:T(512)S(1)}, u32[]{:S(2)}) copy-start(s32[512]{0:T(512)S(1)} %get-tuple-element.139) | copy-start | bytes 6148
  12.8 1.4 %copy-start.36 = (s32[512]{0:T(512)}, s32[512]{0:T(512)S(1)}, u32[]{:S(2)}) copy-start(s32[512]{0:T(512)S(1)} %get-tuple-element.140) | copy-start | bytes 6148
  12.8 1.4 %copy-start.40 = (pred[512]{0:T(512)(128)(4,1)}, pred[512]{0:T(512)(128)(4,1)S(1)}, u32[]{:S(2)}) copy-start(pred[512]{0:T(512)(128)(4,1)S(1)} %get-tuple-element.137) | copy-start | bytes 1540
  12.8 1.4 %copy-start.42 = (pred[512]{0:T(512)(128)(4,1)}, pred[512]{0:T(512)(128)(4,1)S(1)}, u32[]{:S(2)}) copy-start(pred[512]{0:T(512)(128)(4,1)S(1)} %get-tuple-element.138) | copy-start | bytes 1540
  12.8 1.3 %copy-start.44 = (pred[8]{0:T(512)(128)(4,1)}, pred[8]{0:T(512)(128)(4,1)S(1)}, u32[]{:S(2)}) copy-start(pred[8]{0:T(512)(128)(4,1)S(1)} %get-tuple-element.141) | copy-start | bytes 28
  12.9 1.3 %copy-start.46 = (pred[8]{0:T(512)(128)(4,1)}, pred[8]{0:T(512)(128)(4,1)S(1)}, u32[]{:S(2)}) copy-start(pred[8]{0:T(512)(128)(4,1)S(1)} %get-tuple-element.142) | copy-start | bytes 28
  12.9 1.3 %copy-start.48 = (pred[8]{0:T(512)(128)(4,1)}, pred[8]{0:T(512)(128)(4,1)S(1)}, u32[]{:S(2)}) copy-start(pred[8]{0:T(512)(128)(4,1)S(1)} %get-tuple-element.143) | copy-start | bytes 28
  14.1 14.8 %copy-start.22 = (f32[2,8]{1,0:T(2,128)}, f32[2,8]{1,0:T(2,128)S(1)}, u32[]{:S(2)}) copy-start(f32[2,8]{1,0:T(2,128)S(1)} %get-tuple-element.83.refs_15_) | copy-start | bytes 196
  24.0 5.5 %copy-start.31 = (s32[512]{0:T(512)S(1)}, s32[512]{0:T(512)}, u32[]{:S(2)}) copy-start(s32[512]{0:T(512)} %copy-done.30) | copy-start | bytes 6148
  24.0 5.5 %copy-start.33 = (s32[512]{0:T(512)S(1)}, s32[512]{0:T(512)}, u32[]{:S(2)}) copy-start(s32[512]{0:T(512)} %copy-done.32) | copy-start | bytes 6148
  24.0 5.5 %copy-start.35 = (s32[512]{0:T(512)S(1)}, s32[512]{0:T(512)}, u32[]{:S(2)}) copy-start(s32[512]{0:T(512)} %copy-done.34) | copy-start | bytes 6148
  24.0 5.5 %copy-start.37 = (s32[512]{0:T(512)S(1)}, s32[512]{0:T(512)}, u32[]{:S(2)}) copy-start(s32[512]{0:T(512)} %copy-done.36) | copy-start | bytes 6148
  24.1 5.6 %copy-start.43 = (pred[512]{0:T(512)(128)(4,1)S(1)}, pred[512]{0:T(512)(128)(4,1)}, u32[]{:S(2)}) copy-start(pred[512]{0:T(512)(128)(4,1)} %copy-done.42) | copy-start | bytes 1540
  24.1 5.6 %copy-start.45 = (pred[8]{0:T(512)(128)(4,1)S(1)}, pred[8]{0:T(512)(128)(4,1)}, u32[]{:S(2)}) copy-start(pred[8]{0:T(512)(128)(4,1)} %copy-done.44) | copy-start | bytes 28
  24.1 5.6 %copy-start.47 = (pred[8]{0:T(512)(128)(4,1)S(1)}, pred[8]{0:T(512)(128)(4,1)}, u32[]{:S(2)}) copy-start(pred[8]{0:T(512)(128)(4,1)} %copy-done.46) | copy-start | bytes 28
  24.1 5.6 %copy-start.49 = (pred[8]{0:T(512)(128)(4,1)S(1)}, pred[8]{0:T(512)(128)(4,1)}, u32[]{:S(2)}) copy-start(pred[8]{0:T(512)(128)(4,1)} %copy-done.48) | copy-start | bytes 28
  24.1 5.6 %copy-start.51 = (pred[8]{0:T(512)(128)(4,1)S(1)}, pred[8]{0:T(512)(128)(4,1)}, u32[]{:S(2)}) copy-start(pred[8]{0:T(512)(128)(4,1)} %copy-done.50) | copy-start | bytes 28
  24.1 5.6 %copy-start.53 = (pred[8]{0:T(512)(128)(4,1)S(1)}, pred[8]{0:T(512)(128)(4,1)}, u32[]{:S(2)}) copy-start(pred[8]{0:T(512)(128)(4,1)} %copy-done.52) | copy-start | bytes 28
  24.1 5.6 %copy-start.55 = (pred[8]{0:T(512)(128)(4,1)S(1)}, pred[8]{0:T(512)(128)(4,1)}, u32[]{:S(2)}) copy-start(pred[8]{0:T(512)(128)(4,1)} %copy-done.54) | copy-start | bytes 28
  24.1 5.6 %copy-start.57 = (pred[512]{0:T(512)(128)(4,1)S(1)}, pred[512]{0:T(512)(128)(4,1)}, u32[]{:S(2)}) copy-start(pred[512]{0:T(512)(128)(4,1)} %copy-done.56) | copy-start | bytes 1540
  24.1 19.1 %all-to-all-start.1 = ((bf16[4,128,1024]{2,1,0:T(8,128)(2,1)}), bf16[4,128,1024]{2,1,0:T(8,128)(2,1)S(1)}, u32[]{:S(2)}, u32[]{:S(2)}) async-start(bf16[4,128,1024]{2,1,0:T(8,128)(2,1)} %shard_map.181), calls=%async_computation.1 | async-start | bytes 2097152 | tf_op jit(solution)/shard_map/all_to_all | solution.py:855
  32.5 7.5 %copy-start.13 = (f32[8,512]{1,0:T(8,128)S(1)}, f32[8,512]{1,0:T(8,128)}, u32[]{:S(2)}) copy-start(f32[8,512]{1,0:T(8,128)} %select_maximum_fusion.chan_ref.refs_10_.refs_15_) | copy-start | bytes 49156
  35.9 11.9 %collective-permute-start.3 = (bf16[272,512]{1,0:T(8,128)(2,1)}, bf16[272,512]{1,0:T(8,128)(2,1)}, u32[]{:S(2)}, u32[]{:S(2)}) collective-permute-start(bf16[272,512]{1,0:T(8,128)(2,1)} %get-tuple-element.72), channel_id=1, source_target_pairs={{0,8},{2,10},{4,12},{6,14},{8,0},{10,2},{12,4},{14,6},{16,24},{18,... | collective-permute-start | bytes 835592 | tf_op jit(solution)/shard_map/ppermute | solution.py:755
  37.4 21.4 %collective-permute-start.4 = (bf16[272,512]{1,0:T(8,128)(2,1)}, bf16[272,512]{1,0:T(8,128)(2,1)}, u32[]{:S(2)}, u32[]{:S(2)}) collective-permute-start(bf16[272,512]{1,0:T(8,128)(2,1)} %get-tuple-element.72), channel_id=1, source_target_pairs={{0,16},{2,18},{4,20},{6,22},{8,24},{10,26},{12,28},{14,30},{16,0},... | collective-permute-start | bytes 835592 | tf_op jit(solution)/shard_map/ppermute | solution.py:755
  39.4 24.4 %collective-permute-start.5 = (bf16[272,512]{1,0:T(8,128)(2,1)}, bf16[272,512]{1,0:T(8,128)(2,1)}, u32[]{:S(2)}, u32[]{:S(2)}) collective-permute-start(bf16[272,512]{1,0:T(8,128)(2,1)} %get-tuple-element.72), channel_id=1, source_target_pairs={{0,24},{2,26},{4,28},{6,30},{8,16},{10,18},{12,20},{14,22},{16,8},... | collective-permute-start | bytes 835592 | tf_op jit(solution)/shard_map/ppermute | solution.py:755
  40.0 3.2 %copy-start.6 = (bf16[128,1024]{1,0:T(8,128)(2,1)S(1)}, bf16[128,1024]{1,0:T(8,128)(2,1)}, u32[]{:S(2)}) copy-start(bf16[128,1024]{1,0:T(8,128)(2,1)} %get-tuple-element.67) | copy-start | bytes 786436
  40.0 3.2 %copy-start.8 = (bf16[128,1024]{1,0:T(8,128)(2,1)S(1)}, bf16[128,1024]{1,0:T(8,128)(2,1)}, u32[]{:S(2)}) copy-start(bf16[128,1024]{1,0:T(8,128)(2,1)} %copy-done.7) | copy-start | bytes 786436
  40.0 3.2 %copy-start.10 = (bf16[128,1024]{1,0:T(8,128)(2,1)S(1)}, bf16[128,1024]{1,0:T(8,128)(2,1)}, u32[]{:S(2)}) copy-start(bf16[128,1024]{1,0:T(8,128)(2,1)} %copy-done.9) | copy-start | bytes 786436
  44.2 19.7 %copy-start.1 = (f32[512,512]{1,0:T(8,128)S(1)}, f32[512,512]{1,0:T(8,128)}, u32[]{:S(2)}) copy-start(f32[512,512]{1,0:T(8,128)} %copy-done) | copy-start | bytes 3145732
  44.2 19.7 %copy-start.14 = (f32[8,512]{1,0:T(8,128)S(1)}, f32[8,512]{1,0:T(8,128)}, u32[]{:S(2)}) copy-start(f32[8,512]{1,0:T(8,128)} %select_maximum_fusion.chan_ref.refs_10_.refs_15_) | copy-start | bytes 49156
  44.2 19.7 %copy-start.19 = (f32[8,8]{1,0:T(8,128)S(1)}, f32[8,8]{1,0:T(8,128)}, u32[]{:S(2)}) copy-start(f32[8,8]{1,0:T(8,128)} %get-tuple-element.80.refs_12_) | copy-start | bytes 772
  44.2 19.7 %copy-start.20 = (f32[8,8]{1,0:T(8,128)S(1)}, f32[8,8]{1,0:T(8,128)}, u32[]{:S(2)}) copy-start(f32[8,8]{1,0:T(8,128)} %get-tuple-element.79.refs_11_) | copy-start | bytes 772
  44.2 19.7 %copy-start.21 = (f32[8,8]{1,0:T(8,128)S(1)}, f32[8,8]{1,0:T(8,128)}, u32[]{:S(2)}) copy-start(f32[8,8]{1,0:T(8,128)} %concatenate.13.refs_13_) | copy-start | bytes 772
  44.3 19.6 %copy-start.18 = (f32[8,8]{1,0:T(8,128)S(1)}, f32[8,8]{1,0:T(8,128)}, u32[]{:S(2)}) copy-start(f32[8,8]{1,0:T(8,128)} %pad_convert_fusion.refs_14_) | copy-start | bytes 772
  44.3 35.1 %collective-permute-start.13 = (bf16[4,128,1024]{2,1,0:T(8,128)(2,1)S(1)}, bf16[4,128,1024]{2,1,0:T(8,128)(2,1)S(1)}, u32[]{:S(2)}, u32[]{:S(2)}) collective-permute-start(bf16[4,128,1024]{2,1,0:T(8,128)(2,1)S(1)} %shard_map.187.refs_2_), channel_id=1, source_target_pairs={{0,2},{2,0},{4,6},{6,4},{8,10},{10,8},{12,14},{14,12},{16,18},{18,... | collective-permute-start | bytes 3145736 | tf_op jit(solution)/shard_map/ppermute | solution.py:746
  46.3 33.0 %collective-permute-start.14 = (bf16[4,128,1024]{2,1,0:T(8,128)(2,1)S(1)}, bf16[4,128,1024]{2,1,0:T(8,128)(2,1)S(1)}, u32[]{:S(2)}, u32[]{:S(2)}) collective-permute-start(bf16[4,128,1024]{2,1,0:T(8,128)(2,1)S(1)} %shard_map.187.refs_2_), channel_id=1, source_target_pairs={{0,4},{2,6},{4,0},{6,2},{8,12},{10,14},{12,8},{14,10},{16,20},{18,... | collective-permute-start | bytes 3145736 | tf_op jit(solution)/shard_map/ppermute | solution.py:746
  67.9 1.2 collective-permute-start.6
  69.1 3.7 %collective-permute-start.7 = (f32[8,512]{1,0:T(8,128)S(1)}, f32[8,512]{1,0:T(8,128)S(1)}, u32[]{:S(2)}, u32[]{:S(2)}) collective-permute-start(f32[8,512]{1,0:T(8,128)S(1)} %add.334.refs_2_), channel_id=1, source_target_pairs={{0,2},{2,0},{4,6},{6,4},{8,10},{10,8},{12,14},{14,12},{16,18},{18,... | collective-permute-start | bytes 49160 | tf_op jit(solution)/shard_map/ppermute | solution.py:746
  70.8 3.7 %collective-permute-start.8 = (f32[8,512]{1,0:T(8,128)S(1)}, f32[8,512]{1,0:T(8,128)S(1)}, u32[]{:S(2)}, u32[]{:S(2)}) collective-permute-start(f32[8,512]{1,0:T(8,128)S(1)} %add.334.refs_2_), channel_id=1, source_target_pairs={{0,4},{2,6},{4,0},{6,2},{8,12},{10,14},{12,8},{14,10},{16,20},{18,... | collective-permute-start | bytes 49160 | tf_op jit(solution)/shard_map/ppermute | solution.py:746
  72.3 4.6 %collective-permute-start.9 = (f32[8,512]{1,0:T(8,128)S(1)}, f32[8,512]{1,0:T(8,128)S(1)}, u32[]{:S(2)}, u32[]{:S(2)}) collective-permute-start(f32[8,512]{1,0:T(8,128)S(1)} %add.334.refs_2_), channel_id=1, source_target_pairs={{0,6},{2,4},{4,2},{6,0},{8,14},{10,12},{12,10},{14,8},{16,22},{18,... | collective-permute-start | bytes 49160 | tf_op jit(solution)/shard_map/ppermute | solution.py:746
  79.4 12.3 %collective-permute-start.15 = (bf16[2,128,1024]{2,1,0:T(8,128)(2,1)S(1)}, bf16[2,128,1024]{2,1,0:T(8,128)(2,1)S(1)}, u32[]{:S(2)}, u32[]{:S(2)}) collective-permute-start(bf16[2,128,1024]{2,1,0:T(8,128)(2,1)S(1)} %slice.10), channel_id=1, source_target_pairs={{0,4},{2,6},{4,0},{6,2},{8,12},{10,14},{12,8},{14,10},{16,20},{18,... | collective-permute-start | bytes 1572872 | tf_op jit(solution)/shard_map/ppermute | solution.py:746
  80.1 12.2 %collective-permute-start.16 = (bf16[2,128,1024]{2,1,0:T(8,128)(2,1)S(1)}, bf16[2,128,1024]{2,1,0:T(8,128)(2,1)S(1)}, u32[]{:S(2)}, u32[]{:S(2)}) collective-permute-start(bf16[2,128,1024]{2,1,0:T(8,128)(2,1)S(1)} %slice.11), channel_id=1, source_target_pairs={{0,2},{2,0},{4,6},{6,4},{8,10},{10,8},{12,14},{14,12},{16,18},{18,... | collective-permute-start | bytes 1572872 | tf_op jit(solution)/shard_map/ppermute | solution.py:746
  80.4 25.0 %collective-permute-start.10 = (bf16[256,512]{1,0:T(8,128)(2,1)S(1)}, bf16[256,512]{1,0:T(8,128)(2,1)S(1)}, u32[]{:S(2)}, u32[]{:S(2)}) collective-permute-start(bf16[256,512]{1,0:T(8,128)(2,1)S(1)} %get-tuple-element.86), channel_id=1, source_target_pairs={{0,8},{2,10},{4,12},{6,14},{8,0},{10,2},{12,4},{14,6},{16,24},{18,... | collective-permute-start | bytes 786440 | tf_op jit(solution)/shard_map/ppermute | solution.py:755
  80.4 25.0 %collective-permute-start.11 = (bf16[256,512]{1,0:T(8,128)(2,1)S(1)}, bf16[256,512]{1,0:T(8,128)(2,1)S(1)}, u32[]{:S(2)}, u32[]{:S(2)}) collective-permute-start(bf16[256,512]{1,0:T(8,128)(2,1)S(1)} %get-tuple-element.86), channel_id=1, source_target_pairs={{0,16},{2,18},{4,20},{6,22},{8,24},{10,26},{12,28},{14,30},{16,0},... | collective-permute-start | bytes 786440 | tf_op jit(solution)/shard_map/ppermute | solution.py:755
  83.3 22.1 %collective-permute-start.12 = (bf16[256,512]{1,0:T(8,128)(2,1)S(1)}, bf16[256,512]{1,0:T(8,128)(2,1)S(1)}, u32[]{:S(2)}, u32[]{:S(2)}) collective-permute-start(bf16[256,512]{1,0:T(8,128)(2,1)S(1)} %get-tuple-element.86), channel_id=1, source_target_pairs={{0,24},{2,26},{4,28},{6,30},{8,16},{10,18},{12,20},{14,22},{16,8},... | collective-permute-start | bytes 786440 | tf_op jit(solution)/shard_map/ppermute | solution.py:755
  83.9 8.3 %copy-start.2 = (bf16[128,2048]{1,0:T(8,128)(2,1)S(1)}, bf16[128,2048]{1,0:T(8,128)(2,1)}, u32[]{:S(2)}) copy-start(bf16[128,2048]{1,0:T(8,128)(2,1)} %refs_7_.1) | copy-start | bytes 1572868
  83.9 8.3 %copy-start.3 = (bf16[128,2048]{1,0:T(8,128)(2,1)S(1)}, bf16[128,2048]{1,0:T(8,128)(2,1)}, u32[]{:S(2)}) copy-start(bf16[128,2048]{1,0:T(8,128)(2,1)} %refs_8_.1) | copy-start | bytes 1572868
  83.9 8.3 %copy-start.17 = (s32[2,16]{1,0:T(2,128)S(1)}, s32[2,16]{1,0:T(2,128)}, u32[]{:S(2)}) copy-start(s32[2,16]{1,0:T(2,128)} %pad_add_fusion.2.refs_0_) | copy-start | bytes 388
  83.9 8.3 %copy-start.25 = (s32[2]{0:T(128)S(1)}, s32[2]{0:T(128)}, u32[]{:S(2)}) copy-start(s32[2]{0:T(128)} %pad_add_fusion.5.refs_1_) | copy-start | bytes 28
  87.8 17.7 %copy-start.16 = (f32[512,128]{1,0:T(8,128)S(1)}, f32[512,128]{1,0:T(8,128)}, u32[]{:S(2)}) copy-start(f32[512,128]{1,0:T(8,128)} %copy-done.15) | copy-start | bytes 786436
  108.9 10.5 %collective-permute-start.17 = (bf16[128,1280]{1,0:T(8,128)(2,1)S(1)}, bf16[128,1280]{1,0:T(8,128)(2,1)S(1)}, u32[]{:S(2)}, u32[]{:S(2)}) collective-permute-start(bf16[128,1280]{1,0:T(8,128)(2,1)S(1)} %get-tuple-element.115), channel_id=1, source_target_pairs={{0,2},{2,0},{4,6},{6,4},{8,10},{10,8},{12,14},{14,12},{16,18},{18,... | collective-permute-start | bytes 983048 | tf_op jit(solution)/shard_map/ppermute | solution.py:746
  110.0 12.6 %collective-permute-start.18 = (bf16[128,1280]{1,0:T(8,128)(2,1)S(1)}, bf16[128,1280]{1,0:T(8,128)(2,1)S(1)}, u32[]{:S(2)}, u32[]{:S(2)}) collective-permute-start(bf16[128,1280]{1,0:T(8,128)(2,1)S(1)} %get-tuple-element.116), channel_id=1, source_target_pairs={{0,4},{2,6},{4,0},{6,2},{8,12},{10,14},{12,8},{14,10},{16,20},{18,... | collective-permute-start | bytes 983048 | tf_op jit(solution)/shard_map/ppermute | solution.py:746
  111.4 12.4 %collective-permute-start.19 = (bf16[128,1280]{1,0:T(8,128)(2,1)S(1)}, bf16[128,1280]{1,0:T(8,128)(2,1)S(1)}, u32[]{:S(2)}, u32[]{:S(2)}) collective-permute-start(bf16[128,1280]{1,0:T(8,128)(2,1)S(1)} %get-tuple-element.117), channel_id=1, source_target_pairs={{0,6},{2,4},{4,2},{6,0},{8,14},{10,12},{12,10},{14,8},{16,22},{18,... | collective-permute-start | bytes 983048 | tf_op jit(solution)/shard_map/ppermute | solution.py:746
  (18 other events, 15.8 us)
